TPU v7x, 32 devices: a whole 2x2x4 slice. The times are simulated.
32 devices in a mesh: narrow: 4 (over y, core), wide: 8 (over z, x).
Axes of the slice: x: 2, y: 2, z: 4, core: 2. Of those that a mesh axis runs over, the one named last changes fastest.
Arguments:
- tokens: bfloat16 [4, 2048, 2048], P('narrow', 'wide'), may hold values from -12 to 12
- cotangent: bfloat16 [4, 2048, 2048], P('narrow', 'wide'), may hold values from -6 to 6
- qkv_weight: bfloat16 [2048, 6144], P('wide'), may hold values from -0.25 to 0.25
- out_weight: bfloat16 [2048, 2048], P('wide'), may hold values from -0.5 to 0.5
- gain_attn: bfloat16 [2048], P('wide'), may hold values from 0.5 to 1.5
- gate_up_weight: bfloat16 [2048, 16384], P('wide'), may hold values from -0.125 to 0.125
- down_weight: bfloat16 [2048, 8192], P('wide'), may hold values from -0.125 to 0.125
- gain_mlp: bfloat16 [2048], P('wide'), may hold values from 0.5 to 1.5
- gate_logit: float32 [16], replicated, may hold values from -2 to 2
- memory_in: float32 [4, 16, 128, 128], P('narrow'), may hold values from -24 to 24
- normalizer_in: float32 [4, 16, 128], P('narrow'), may hold values from 0.25 to 2
Outputs:
- output: bfloat16 [4, 2048, 2048], P('narrow', 'wide')
- grad_tokens: bfloat16 [4, 2048, 2048], P('narrow', 'wide')
- grad_memory_in: float32 [4, 16, 128, 128], P('narrow')
- grad_normalizer_in: float32 [4, 16, 128], P('narrow')
- grad_qkv_weight: float32 [2048, 6144], P('wide')
- grad_out_weight: float32 [2048, 2048], P('wide')
- grad_gain_attn: float32 [2048], P('wide')
- grad_gate_up_weight: float32 [2048, 16384], P('wide')
- grad_down_weight: float32 [2048, 8192], P('wide')
- grad_gain_mlp: float32 [2048], P('wide')
- grad_gate_logit: float32 [16], replicated
All inputs are finite; a program needn't handle non-finite values.
Results may differ from a plain program's by a relative error of at most 0.02.
Values may be sent and summed in bfloat16 or wider, within the bound.
No kernel may reach another device: no remote copies, remote signals or barrier semaphores. Data moves between devices by JAX's collectives and lax.ppermute only.
A program may use at most 512 MiB of HBM per device.

v0:
```python
import jax
import jax.numpy as jnp
from jax import lax
from jax.sharding import PartitionSpec as P

D = 2048
H = 16
DK = 128
FF = 8192
SEG = 1024


EPSILON = 1e-06
HIGHEST = lax.Precision.HIGHEST


def as_sent(x):

    def short(part):
        return part.astype(jnp.bfloat16) if part.dtype == jnp.float32 else part

    return jax.tree.map(short, x)


def shifted(block, axis, distance):
    devices = range(lax.axis_size(axis))
    route = [(i - distance, i) for i in devices if i - distance in devices]
    return lax.ppermute(block, axis, route)


def entering(x, axis, combine, identity):
    count, index = (lax.axis_size(axis), lax.axis_index(axis))
    everything = jax.tree.map(lambda part: lax.all_gather(part, axis), x)
    start = jax.tree.map(
        lambda part, zero: jnp.broadcast_to(jnp.asarray(zero, part.dtype), part.shape), x, identity
    )

    def hop(k, before):
        reached = k < index
        new = combine(before, jax.tree.map(lambda part: part[k], everything))
        return jax.tree.map(lambda a, b: jnp.where(reached, a, b), new, before)

    return lax.fori_loop(0, count, hop, start)


def entering_2(x, axis, join, neutral):
    count = lax.axis_size(axis)
    place = lax.axis_index(axis)
    ahead = count - 1 - place
    gathered = jax.tree.map(
        lambda a, kind: lax.all_gather(a.astype(kind), axis),
        x,
        jax.tree.map(lambda a: jnp.bfloat16 if a.dtype == jnp.float32 else a.dtype, x),
    )
    state = jax.tree.map(lambda a, e: jnp.zeros_like(a) + jnp.asarray(e, a.dtype), x, neutral)

    def one(hop, state):
        source = count - 1 - hop
        return join(
            state,
            jax.tree.map(
                lambda a, own: lax.dynamic_index_in_dim(a, source, 0, False).astype(own.dtype),
                gathered,
                x,
            ),
        )

    return lax.fori_loop(0, ahead, one, state)


def join_forward(earlier, later):
    early_closed_m, early_open_m, early_closed_n, early_open_n, early_flag = earlier
    late_closed_m, late_open_m, late_closed_n, late_open_n, late_flag = later
    border = late_flag > 0.5
    return (
        jnp.where(border, early_closed_m + early_open_m + late_closed_m, early_closed_m),
        jnp.where(border, late_open_m, early_open_m + late_open_m),
        jnp.where(border, early_closed_n + early_open_n + late_closed_n, early_closed_n),
        jnp.where(border, late_open_n, early_open_n + late_open_n),
        jnp.maximum(early_flag, late_flag),
    )


def join_backward(earlier, later):
    high_head_m, high_tail_m, high_head_n, high_tail_n, high_flag = earlier
    lower_head_m, lower_tail_m, lower_head_n, lower_tail_n, lower_flag = later
    border = lower_flag > 0.5
    return (
        jnp.where(border, lower_head_m, lower_head_m + high_head_m),
        jnp.where(border, lower_tail_m + high_head_m + high_tail_m, high_tail_m),
        jnp.where(border, lower_head_n, lower_head_n + high_head_n),
        jnp.where(border, lower_tail_n + high_head_n + high_tail_n, high_tail_n),
        jnp.maximum(high_flag, lower_flag),
    )


def contract_last(left, right):
    return lax.dot_general(
        left, right, (((1,), (1,)), ((), ())), preferred_element_type=jnp.float32
    )


def contract_first(left, right):
    return lax.dot_general(
        left, right, (((0,), (0,)), ((), ())), preferred_element_type=jnp.float32
    )


def norm_back(grad_unit, unit_rows, scale_rows):
    return scale_rows * (
        grad_unit - unit_rows * jnp.mean(grad_unit * unit_rows, axis=-1, keepdims=True)
    )


def elu_slope(inputs):
    return jnp.where(inputs > 0, 1.0, jnp.exp(jnp.minimum(inputs, 0.0)))


def weight_rows(term_fn, shard_rows):
    return lax.psum_scatter(
        term_fn(jnp.int32(0), shard_rows * lax.axis_size("wide")).astype(jnp.bfloat16),
        "wide",
        scatter_dimension=0,
        tiled=True,
    ).astype(jnp.float32)


def replica_total(members):
    return jax.tree.map(lambda part: part.astype(jnp.float32), lax.psum(as_sent(members), "narrow"))


def body(
    tokens,
    cotangent,
    qkv_weight,
    out_weight,
    gain_attn,
    gate_up_weight,
    down_weight,
    gain_mlp,
    gate_logit,
    memory_in,
    normalizer_in,
):
    float_type = jnp.float32
    brain_type = jnp.bfloat16
    shard_rows = qkv_weight.shape[0]
    rows_here = tokens.shape[1]
    span = SEG // rows_here
    place = lax.axis_index("wide") % span
    is_first = place == 0
    scale = DK ** (-0.5)

    def reduce_rows(term_fn):
        (summed,) = replica_total((weight_rows(term_fn, shard_rows),))
        return summed

    inputs = tokens[0].astype(float_type)
    scale_one = lax.rsqrt(jnp.mean(inputs * inputs, axis=-1, keepdims=True) + EPSILON)
    unit_one = inputs * scale_one
    qkv_full, out_full, gain_full = (
        lax.all_gather(qkv_weight, "wide", axis=0, tiled=True),
        lax.all_gather(out_weight, "wide", axis=0, tiled=True),
        lax.all_gather(gain_attn, "wide", axis=0, tiled=True),
    )
    gain_one = gain_full.astype(float_type)
    normed_one = (unit_one * gain_one).astype(brain_type)
    projected = jnp.dot(normed_one, qkv_full, preferred_element_type=float_type).astype(brain_type)
    queries = projected[:, :D].reshape(rows_here, H, DK)
    key_value = projected[:, D:]
    blocks = [key_value]
    for offset in range(1, span):
        blocks.append(shifted(key_value, "wide", offset))
    gathered = jnp.concatenate(blocks, axis=0)
    keys = gathered[:, :D].reshape(span * rows_here, H, DK)
    values = gathered[:, D:].reshape(span * rows_here, H, DK)
    query_pos = lax.broadcasted_iota(jnp.int32, (rows_here, span * rows_here), 0)
    key_index = lax.broadcasted_iota(jnp.int32, (rows_here, span * rows_here), 1)
    key_block = key_index // rows_here
    allowed = (key_block <= place) & (
        (key_block > 0) | (key_index - key_block * rows_here <= query_pos)
    )

    def score_table():
        raw_scores = (
            jnp.einsum("thd,shd->hts", queries, keys, preferred_element_type=float_type) * scale
        )
        return jnp.where(allowed[None], raw_scores, -1e30)

    scores = score_table()
    highest_score = jnp.max(scores, axis=-1, keepdims=True)
    raised = jnp.exp(scores - highest_score)
    totals = jnp.sum(raised, axis=-1, keepdims=True)
    attn_probs = raised / totals
    log_total = highest_score + jnp.log(totals)
    direct = jnp.einsum(
        "hts,shd->thd", attn_probs.astype(brain_type), values, preferred_element_type=float_type
    )
    query_f = queries.astype(float_type)
    key_f = key_value[:, :D].reshape(rows_here, H, DK).astype(float_type)
    value_f = key_value[:, D:].reshape(rows_here, H, DK).astype(float_type)
    lift_q = jax.nn.elu(query_f) + 1.0
    lift_k = jax.nn.elu(key_f) + 1.0
    part_mem = jnp.einsum("thd,the->hde", lift_k, value_f, precision=HIGHEST) / SEG
    part_norm = jnp.sum(lift_k, axis=0) / SEG
    start_flag = jnp.where(is_first, 1.0, 0.0).astype(float_type)
    empty_mem = jnp.zeros_like(part_mem)
    empty_norm = jnp.zeros_like(part_norm)
    zero_flag = jnp.zeros((), float_type)
    closed_m, open_m, closed_n, open_n, seen_flag = entering(
        (empty_mem, part_mem, empty_norm, part_norm, start_flag),
        "wide",
        join_forward,
        (empty_mem, empty_mem, empty_norm, empty_norm, zero_flag),
    )
    read_mem = memory_in[0] + jnp.where(is_first, closed_m + open_m, closed_m)
    read_norm = normalizer_in[0] + jnp.where(is_first, closed_n + open_n, closed_n)
    numerator = jnp.einsum("thd,hde->the", lift_q, read_mem, precision=HIGHEST)
    denominator = jnp.einsum("thd,hd->th", lift_q, read_norm, precision=HIGHEST)
    recalled = numerator / denominator[..., None]
    mixing = jax.nn.sigmoid(gate_logit)
    mix_full = mixing[None, :, None]
    attended = (
        (mix_full * recalled + (1.0 - mix_full) * direct).reshape(rows_here, D).astype(brain_type)
    )
    middle = inputs + jnp.dot(attended, out_full, preferred_element_type=float_type)
    scale_two = lax.rsqrt(jnp.mean(middle * middle, axis=-1, keepdims=True) + EPSILON)
    unit_two = middle * scale_two
    weight_piece = lax.all_gather(gate_up_weight, "wide", axis=0, tiled=True)
    gain_piece = lax.all_gather(gain_mlp, "wide", axis=0, tiled=True)
    gain_rows = gain_piece.astype(float_type)
    columns = (unit_two * gain_rows).astype(brain_type)
    product = jnp.dot(columns, weight_piece, preferred_element_type=float_type)
    normed = columns
    gate_part = product[:, :FF]
    up_part = product[:, FF:]
    gate_sig = jax.nn.sigmoid(gate_part)
    activation = (gate_part * gate_sig * up_part).astype(brain_type)
    mlp_out = contract_last(activation, lax.all_gather(down_weight, "wide", axis=0, tiled=True))
    output = (middle + mlp_out).astype(brain_type)[None]
    grad_top = cotangent[0]
    columns = grad_top
    grad_activ = jnp.dot(
        columns,
        lax.all_gather(down_weight, "wide", axis=0, tiled=True),
        preferred_element_type=float_type,
    )
    grad_gate = grad_activ * up_part * gate_sig * (1.0 + gate_part * (1.0 - gate_sig))
    grad_upper = grad_activ * gate_part * gate_sig
    grad_pair = jnp.concatenate([grad_gate, grad_upper], axis=1).astype(brain_type)
    grad_normed_two = contract_last(
        grad_pair, lax.all_gather(gate_up_weight, "wide", axis=0, tiled=True)
    )
    grad_gain_two = jnp.sum(grad_normed_two * unit_two, axis=0)
    grad_middle = grad_top.astype(float_type) + norm_back(
        grad_normed_two * gain_rows, unit_two, scale_two
    )

    def gate_up_terms(first_row, row_count):
        return contract_first(normed, grad_pair)

    def down_terms(first_row, row_count):
        return contract_first(grad_top, activation)

    grad_gate_up_rows = reduce_rows(gate_up_terms)
    grad_down_rows = reduce_rows(down_terms)
    grad_branch = grad_middle.astype(brain_type)
    qkv_back, out_back = (
        lax.all_gather(qkv_weight, "wide", axis=0, tiled=True),
        lax.all_gather(out_weight, "wide", axis=0, tiled=True),
    )
    grad_att = contract_last(grad_branch, out_back).reshape(rows_here, H, DK)
    grad_logit = jnp.sum(grad_att * (recalled - direct), axis=(0, 2)) * mixing * (1.0 - mixing)
    grad_direct = ((1.0 - mix_full) * grad_att).astype(brain_type)
    grad_recall = lax.optimization_barrier((mix_full * grad_att).astype(brain_type)).astype(
        float_type
    )
    again_scores = score_table()
    again_probs = jnp.exp(again_scores - log_total)
    grad_probs = jnp.einsum("thd,shd->hts", grad_direct, values, preferred_element_type=float_type)
    inner_sum = jnp.sum(again_probs * grad_probs, axis=-1, keepdims=True)
    grad_scores = (again_probs * (grad_probs - inner_sum)).astype(brain_type)
    grad_q_dot = (
        jnp.einsum("hts,shd->thd", grad_scores, keys, preferred_element_type=float_type) * scale
    )
    grad_k_dot = (
        jnp.einsum("hts,thd->shd", grad_scores, queries, preferred_element_type=float_type) * scale
    )
    grad_v_dot = jnp.einsum(
        "hts,thd->shd",
        again_probs.astype(brain_type),
        grad_direct,
        preferred_element_type=float_type,
    )
    grad_kv = jnp.concatenate(
        [grad_k_dot.reshape(span * rows_here, D), grad_v_dot.reshape(span * rows_here, D)], axis=1
    )
    own_grad = grad_kv[:rows_here]
    for offset in range(1, span):
        own_grad = own_grad + shifted(
            grad_kv[offset * rows_here : (offset + 1) * rows_here].astype(jnp.bfloat16),
            "wide",
            -offset,
        ).astype(jnp.float32)
    grad_numer = grad_recall / denominator[..., None]
    grad_denom = -jnp.sum(grad_recall * recalled, axis=-1) / denominator
    grad_lift_q = (
        jnp.einsum("the,hde->thd", grad_numer, read_mem, precision=HIGHEST)
        + grad_denom[..., None] * read_norm[None]
    )
    grad_read_mem = jnp.einsum("thd,the->hde", lift_q, grad_numer, precision=HIGHEST)
    grad_read_norm = jnp.einsum("th,thd->hd", grad_denom, lift_q, precision=HIGHEST)
    single_term = (
        jnp.where(is_first, empty_mem, grad_read_mem),
        jnp.where(is_first, grad_read_mem, empty_mem),
        jnp.where(is_first, empty_norm, grad_read_norm),
        jnp.where(is_first, grad_read_norm, empty_norm),
        start_flag,
    )
    ahead_head_m, later_mem, ahead_head_n, later_norm, ahead_flag = entering_2(
        single_term,
        "wide",
        join_backward,
        (empty_mem, empty_mem, empty_norm, empty_norm, zero_flag),
    )
    grad_lift_k = (
        jnp.einsum("the,hde->thd", value_f, later_mem, precision=HIGHEST) + later_norm[None]
    ) / SEG
    grad_v_mem = jnp.einsum("thd,hde->the", lift_k, later_mem, precision=HIGHEST) / SEG
    grad_query = grad_q_dot + grad_lift_q * elu_slope(query_f)
    grad_key = own_grad[:, :D].reshape(rows_here, H, DK) + grad_lift_k * elu_slope(key_f)
    grad_value = own_grad[:, D:].reshape(rows_here, H, DK) + grad_v_mem
    grad_projected = jnp.concatenate(
        [
            grad_query.reshape(rows_here, D),
            grad_key.reshape(rows_here, D),
            grad_value.reshape(rows_here, D),
        ],
        axis=1,
    ).astype(brain_type)
    grad_normed_one = contract_last(grad_projected, qkv_back)
    grad_gain_one = jnp.sum(grad_normed_one * unit_one, axis=0)
    grad_input = (grad_middle + norm_back(grad_normed_one * gain_one, unit_one, scale_one)).astype(
        brain_type
    )[None]

    def qkv_terms(first_row, row_count):
        return contract_first(normed_one, grad_projected)

    def out_terms(first_row, row_count):
        return contract_first(attended, grad_branch)

    totals_mem, totals_norm, totals_logit, totals_gain_one, totals_gain_two = (
        lax.psum(grad_read_mem.astype(jnp.bfloat16), "wide").astype(jnp.float32),
        lax.psum(grad_read_norm.astype(jnp.bfloat16), "wide").astype(jnp.float32),
        lax.psum(grad_logit.astype(jnp.bfloat16), "wide").astype(jnp.float32),
        lax.psum(grad_gain_one.astype(jnp.bfloat16), "wide").astype(jnp.float32),
        lax.psum(grad_gain_two.astype(jnp.bfloat16), "wide").astype(jnp.float32),
    )
    offset_row = lax.axis_index("wide") * shard_rows
    gain_one_rows = lax.dynamic_slice_in_dim(totals_gain_one, offset_row, shard_rows, 0)
    gain_two_rows = lax.dynamic_slice_in_dim(totals_gain_two, offset_row, shard_rows, 0)
    grad_qkv_rows = reduce_rows(qkv_terms)
    grad_out_rows = reduce_rows(out_terms)
    gain_one_sum, gain_two_sum, logit_sum = replica_total(
        (gain_one_rows, gain_two_rows, totals_logit)
    )
    return (
        output,
        grad_input,
        totals_mem[None],
        totals_norm[None],
        grad_qkv_rows,
        grad_out_rows,
        gain_one_sum,
        grad_gate_up_rows,
        grad_down_rows,
        gain_two_sum,
        logit_sum,
    )


def solution(mesh):
    return jax.shard_map(
        body,
        mesh=mesh,
        in_specs=(
            P("narrow", "wide", None),
            P("narrow", "wide", None),
            P("wide", None),
            P("wide", None),
            P("wide"),
            P("wide", None),
            P("wide", None),
            P("wide"),
            P(),
            P("narrow", None, None, None),
            P("narrow", None, None),
        ),
        out_specs=(
            P("narrow", "wide", None),
            P("narrow", "wide", None),
            P("narrow", None, None, None),
            P("narrow", None, None),
            P("wide", None),
            P("wide", None),
            P("wide"),
            P("wide", None),
            P("wide", None),
            P("wide"),
            P(),
        ),
        check_vma=False,
    )
```

profile of v0, /device:TPU:0, one launch (start us, length us, event | category | flops | bytes accessed | tf_op | source)
XLA Modules:
  0.0 5785.8 jit_solution(7445721822713864511)
XLA Ops:
  8.0 50.7 all-gather.5
  59.0 433.8 %all-gather.15.cloned.1.call-done = bf16[2048,6144]{1,0:T(8,128)(2,1)} async-done(((bf16[256,6144]{1,0:T(8,128)(2,1)}), bf16[2048,6144]{1,0:T(8,128)(2,1)}) %all-gather.15.cloned.1.call-update) | async-done | bytes 25165840 | tf_op jit(solution)/shard_map/all_gather | solution.py:162
  492.8 11.7 convolution_convert_fusion.2
  509.4 4.9 convolution_multiply_fusion
  516.3 3.1 slice.64
  519.5 4.7 collective-permute-start.2
  524.2 4.7 collective-permute-start.1
  528.9 4.3 collective-permute-start
  534.4 236.3 %all-reduce = f32[8]{0:T(128)S(1)} all-reduce(f32[8]{0:T(128)S(1)} %dynamic-update-slice), channel_id=1, replica_groups=mesh['narrow'=4,'wide'=8] {'wide'}, use_global_device_ids=true, to_apply=%add | all-reduce | flops 8 | bytes 64
  770.7 124.9 %all-gather.6 = bf16[8,1,256]{2,1,0:T(2,128)(2,1)S(1)} all-gather(bf16[1,1,256]{2,1,0:T(2,128)(2,1)S(1)} %reshape.231), channel_id=1, replica_groups=mesh['narrow'=4,'wide'=8] {'wide'}, dimensions={0}, use_global_device_ids=true | all-gather | bytes 4608 | tf_op jit(solution)/shard_map/all_gather | solution.py:230
  895.9 2.3 copy.79
  900.4 116.5 %all_gather.76 = f32[8,16,128]{2,1,0:T(8,128)S(1)} all-gather(f32[1,16,128]{2,1,0:T(8,128)S(1)} %multiply_bitcast_fusion), channel_id=1, replica_groups=mesh['narrow'=4,'wide'=8] {'wide'}, dimensions={0}, use_global_device_ids=true | all-gather | bytes 73728 | tf_op jit(solution)/shard_map/all_gather | solution.py:33
  1016.9 4.3 pad_maximum_fusion.1
  1021.2 3.9 slice_bitcast_fusion
  1025.1 6.4 copy.80
  1031.5 5.8 fusion.123
  1037.2 6.2 copy-done
  1043.4 3.6 fusion.3
  1047.0 24.4 while.41
  1071.5 3.3 fusion.58
  1075.1 4.2 bitcast_divide_fusion
  1079.4 10.2 fusion.51
  1089.6 6.2 multiply_reduce_fusion.3
  1095.8 1082.3 %all-gather.19.cloned.1.call-done = bf16[2048,16384]{1,0:T(8,128)(2,1)} async-done(((bf16[256,16384]{1,0:T(8,128)(2,1)}), bf16[2048,16384]{1,0:T(8,128)(2,1)}) %all-gather.19.cloned.1.call-update) | async-done | bytes 67108880 | tf_op jit(solution)/shard_map/all_gather | solution.py:229
  2178.0 33.3 fusion.120
  2211.3 605.8 %all-gather.21.cloned.1.call-done = bf16[2048,8192]{1,0:T(8,128)(2,1)} async-done(((bf16[256,8192]{1,0:T(8,128)(2,1)}), bf16[2048,8192]{1,0:T(8,128)(2,1)}) %all-gather.21.cloned.1.call-update) | async-done | bytes 33554448 | tf_op jit(solution)/shard_map/all_gather | solution.py:239
  2817.1 28.5 multiply_convert_fusion.2
  2845.7 29.8 multiply_reduce_fusion.1
  2875.5 2.8 multiply_add_fusion
  2878.4 7.9 multiply_convert_fusion.4
  2886.2 4.3 select_convert_fusion
  2892.0 21.1 all-reduce.1
  2913.1 6.8 convolution_convert_fusion.3
  2921.5 13.7 multiply_reduce_fusion
  2935.2 11.8 multiply_convert_fusion
  2947.0 3.3 copy-done.1
  2951.9 9.4 fusion.5
  2961.3 4.7 fusion.2
  2966.1 3.4 fusion.121
  2974.4 2.5 fusion.54
  2977.0 306.2 %all-gather.3 = bf16[128,128]{1,0:T(8,128)(2,1)S(1)} all-gather(bf16[16,128]{1,0:T(8,128)(2,1)S(1)} %get-tuple-element.500), channel_id=5, replica_groups=mesh['narrow'=4,'wide'=8] {'wide'}, dimensions={0}, use_global_device_ids=true | all-gather | bytes 36864 | tf_op jit(solution)/shard_map/all_gather | solution.py:51
  3283.2 31.3 all-gather.4
  3314.5 3.3 fusion.61
  3317.9 8.3 fusion.42
  3326.1 4.4 fusion.13
  3330.6 2.3 fusion.122
  3333.1 23.4 while.40
  3358.1 2.7 fusion.62
  3364.4 14.8 convolution_convert_fusion.1
  3380.5 16.1 convert_bitcast_fusion
  3398.2 28.9 convolution_convert_fusion
  3427.8 352.6 %reduce-scatter.5.cloned.1.call-done = bf16[256,6144]{1,0:T(8,128)(2,1)} async-done(((bf16[2048,6144]{1,0:T(8,128)(2,1)}), bf16[256,6144]{1,0:T(8,128)(2,1)}) %reduce-scatter.5.cloned.1.call-update) | async-done | bytes 3145744 | tf_op jit(solution)/shard_map/reduce_scatter | solution.py:120
  3780.4 546.4 %reduce-scatter.11.cloned.1.call-done = bf16[256,8192]{0,1:T(8,128)(2,1)} async-done(((bf16[2048,8192]{0,1:T(8,128)(2,1)}), bf16[256,8192]{0,1:T(8,128)(2,1)}) %reduce-scatter.11.cloned.1.call-update) | async-done | bytes 4194320 | tf_op jit(solution)/shard_map/reduce_scatter | solution.py:120
  4326.8 1059.1 %reduce-scatter.9.cloned.1.call-done = bf16[256,16384]{1,0:T(8,128)(2,1)} async-done(((bf16[2048,16384]{1,0:T(8,128)(2,1)}), bf16[256,16384]{1,0:T(8,128)(2,1)}) %reduce-scatter.9.cloned.1.call-update) | async-done | bytes 8388624 | tf_op jit(solution)/shard_map/reduce_scatter | solution.py:120
  5386.5 16.8 fusion.25
  5403.3 57.8 all-reduce.8.cloned.1.call-done
  5463.3 14.9 fusion.33
  5478.2 34.9 all-reduce.2
  5513.9 6.2 all-reduce.3
  5521.7 3.2 fusion.69
  5524.8 228.4 %all-reduce.10.cloned.1.call-done = (bf16[256,8192]{0,1:T(8,128)(2,1)}, bf16[256,6144]{1,0:T(8,128)(2,1)}, bf16[256,2048]{1,0:T(8,128)(2,1)}, bf16[256,16384]{1,0:T(8,128)(2,1)}) async-done(((bf16[256,8192]{0,1:T(8,128)(2,1)}, bf16[256,6144]{1,0:T(8,128)(2,1)}, bf16[256,2048]{1,0:T(8,128)(2,1)}, bf16[256,16384]{1,0:T(8,128)(2,1)}), (bf16[256,8192]{0,1:T(8,128)(2,1)}, bf16[256,6144]{1,0:T(8,128)(2,1)}, ...) | async-done | bytes 16777232 | tf_op jit(solution)/shard_map/psum | solution.py:129
  5753.3 5.4 convert_element_type.260
  5760.2 11.5 convert_element_type.268
  5771.8 7.0 copy.65
  (230 shorter events, 74.3 us)
Async XLA Ops:
  7.2 51.5 copy-start.9
  7.2 485.6 %all-gather.15.cloned.1.call-start = ((), (), s32[]{:S(2)}) async-start(), calls=%async_computation.4 | async-start | bytes 28311552 | tf_op jit(solution)/shard_map/all_gather | solution.py:162
  7.9 1039.1 %all-gather.23.cloned.1.call-start = ((), (), s32[]{:S(2)}) async-start(), calls=%async_computation.13 | async-start | bytes 9437184 | tf_op jit(solution)/shard_map/all_gather | solution.py:33
  58.7 445.8 %copy-start.32 = (f32[8,1,256]{2,1,0:T(1,128)}, f32[8,1,256]{2,1,0:T(1,128)S(1)}, u32[]{:S(2)}) copy-start(f32[8,1,256]{2,1,0:T(1,128)S(1)} %convert_element_type.284) | copy-start | bytes 24580
  59.0 445.6 %copy-start.34 = (f32[256]{0:T(256)}, f32[256]{0:T(256)S(1)}, u32[]{:S(2)}) copy-start(f32[256]{0:T(256)S(1)} %add_rsqrt_fusion.1) | copy-start | bytes 3076
  504.5 3.0 copy-start.15
  509.4 4.9 copy-start.7
  514.3 575.2 %all-gather.17.cloned.1.call-start = ((), (), s32[]{:S(2)}) async-start(), calls=%async_computation.5 | async-start | bytes 9437184 | tf_op jit(solution)/shard_map/all_gather | solution.py:163
  515.1 1663.0 %all-gather.19.cloned.1.call-start = ((), (), s32[]{:S(2)}) async-start(), calls=%async_computation.6 | async-start | bytes 75497472 | tf_op jit(solution)/shard_map/all_gather | solution.py:229
  515.7 2301.5 %all-gather.21.cloned.1.call-start = ((), (), s32[]{:S(2)}) async-start(), calls=%async_computation.7 | async-start | bytes 37748736 | tf_op jit(solution)/shard_map/all_gather | solution.py:239
  516.2 16.9 copy-start.47
  516.3 254.4 %copy-start.45 = (bf16[256]{0:T(256)(128)(2,1)S(1)}, bf16[256]{0:T(256)(128)(2,1)}, u32[]{:S(2)}) copy-start(bf16[256]{0:T(256)(128)(2,1)} %param.22) | copy-start | bytes 1540
  516.3 379.4 %copy-start.46 = (f32[16]{0:T(128)S(1)}, f32[16]{0:T(128)}, u32[]{:S(2)}) copy-start(f32[16]{0:T(128)} %param.23) | copy-start | bytes 196
  516.3 2816.6 %all-gather.25.cloned.1.call-start = ((), (), s32[]{:S(2)}) async-start(), calls=%async_computation.14 | async-start | bytes 4718592 | tf_op jit(solution)/shard_map/all_gather | solution.py:51
  519.5 497.5 %collective-permute-start.2 = (bf16[256,4096]{1,0:T(8,128)(2,1)}, bf16[256,4096]{1,0:T(8,128)(2,1)}, u32[]{:S(2)}, u32[]{:S(2)}) collective-permute-start(bf16[256,4096]{1,0:T(8,128)(2,1)} %slice.64), channel_id=1, source_target_pairs={{0,3},{1,4},{2,5},{3,6},{4,7},{8,11},{9,12},{10,13},{11,14},{12,15... | collective-permute-start | bytes 6291464 | tf_op jit(solution)/shard_map/ppermute | solution.py:28
  524.2 492.8 %collective-permute-start.1 = (bf16[256,4096]{1,0:T(8,128)(2,1)}, bf16[256,4096]{1,0:T(8,128)(2,1)}, u32[]{:S(2)}, u32[]{:S(2)}) collective-permute-start(bf16[256,4096]{1,0:T(8,128)(2,1)} %slice.64), channel_id=1, source_target_pairs={{0,2},{1,3},{2,4},{3,5},{4,6},{5,7},{8,10},{9,11},{10,12},{11,13},... | collective-permute-start | bytes 6291464 | tf_op jit(solution)/shard_map/ppermute | solution.py:28
  528.9 488.0 %collective-permute-start = (bf16[256,4096]{1,0:T(8,128)(2,1)}, bf16[256,4096]{1,0:T(8,128)(2,1)}, u32[]{:S(2)}, u32[]{:S(2)}) collective-permute-start(bf16[256,4096]{1,0:T(8,128)(2,1)} %slice.64), channel_id=1, source_target_pairs={{0,1},{1,2},{2,3},{3,4},{4,5},{5,6},{6,7},{8,9},{9,10},{10,11},{11... | collective-permute-start | bytes 6291464 | tf_op jit(solution)/shard_map/ppermute | solution.py:28
  895.7 1982.6 %copy-start.42 = (f32[16]{0:T(128)}, f32[16]{0:T(128)S(1)}, u32[]{:S(2)}) copy-start(f32[16]{0:T(128)S(1)} %get-tuple-element.475) | copy-start | bytes 196
  1037.2 6.2 copy-start
  1047.0 24.5 copy-start.38
  1071.5 3.4 copy-start.27
  1071.5 3.6 copy-start.39
  1071.5 3.6 copy-start.13
  1074.8 4.5 copy-start.36
  1075.1 4.3 copy-start.29
  1075.1 4.3 copy-start.11
  1095.8 1749.9 %copy-start.5 = (f32[256,2048]{1,0:T(8,128)}, f32[256,2048]{1,0:T(8,128)S(1)}, u32[]{:S(2)}) copy-start(f32[256,2048]{1,0:T(8,128)S(1)} %get-tuple-element.506) | copy-start | bytes 6291460
  2178.0 639.1 %copy-start.18 = (bf16[1,256,2048]{2,1,0:T(8,128)(2,1)S(1)}, bf16[1,256,2048]{2,1,0:T(8,128)(2,1)}, u32[]{:S(2)}) copy-start(bf16[1,256,2048]{2,1,0:T(8,128)(2,1)} %param.16) | copy-start | bytes 3145732
  2878.3 34.7 copy-start.2
  2878.3 7.9 copy-start.14
  2886.2 4.3 copy-start.23
  2890.5 442.3 %all-gather.27.cloned.1.call-start = ((), (), s32[]{:S(2)}) async-start(), calls=%async_computation.15 | async-start | bytes 4718592 | tf_op jit(solution)/shard_map/all_gather | solution.py:51
  2891.3 536.5 %reduce-scatter.7.cloned.1.call-start = ((), (), s32[]{:S(2)}) async-start(), calls=%async_computation.10 | async-start | bytes 9437184 | tf_op jit(solution)/shard_map/reduce_scatter | solution.py:120
  2919.9 1.6 copy-start.4
  2919.9 860.5 %reduce-scatter.5.cloned.1.call-start = ((), (), s32[]{:S(2)}) async-start(), calls=%async_computation.9 | async-start | bytes 28311552 | tf_op jit(solution)/shard_map/reduce_scatter | solution.py:120
  2947.0 3.3 copy-start.1
  2966.0 7.6 copy-start.24
  2966.0 7.6 copy-start.25
  2966.1 7.6 copy-start.26
  2969.5 356.7 %collective-permute-start.5 = (bf16[256,4096]{0,1:T(8,128)(2,1)}, bf16[256,4096]{0,1:T(8,128)(2,1)}, u32[]{:S(2)}, u32[]{:S(2)}) collective-permute-start(bf16[256,4096]{0,1:T(8,128)(2,1)} %get-tuple-element.488), channel_id=1, source_target_pairs={{3,0},{4,1},{5,2},{6,3},{7,4},{11,8},{12,9},{13,10},{14,11},{15,12... | collective-permute-start | bytes 6291464 | tf_op jit(solution)/shard_map/ppermute | solution.py:28
  2970.9 355.2 %collective-permute-start.4 = (bf16[256,4096]{0,1:T(8,128)(2,1)}, bf16[256,4096]{0,1:T(8,128)(2,1)}, u32[]{:S(2)}, u32[]{:S(2)}) collective-permute-start(bf16[256,4096]{0,1:T(8,128)(2,1)} %get-tuple-element.489), channel_id=1, source_target_pairs={{2,0},{3,1},{4,2},{5,3},{6,4},{7,5},{10,8},{11,9},{12,10},{13,11},... | collective-permute-start | bytes 6291464 | tf_op jit(solution)/shard_map/ppermute | solution.py:28
  2972.2 353.9 %collective-permute-start.3 = (bf16[256,4096]{0,1:T(8,128)(2,1)}, bf16[256,4096]{0,1:T(8,128)(2,1)}, u32[]{:S(2)}, u32[]{:S(2)}) collective-permute-start(bf16[256,4096]{0,1:T(8,128)(2,1)} %get-tuple-element.487), channel_id=1, source_target_pairs={{1,0},{2,1},{3,2},{4,3},{5,4},{6,5},{7,6},{9,8},{10,9},{11,10},{12... | collective-permute-start | bytes 6291464 | tf_op jit(solution)/shard_map/ppermute | solution.py:28
  2974.4 340.2 %copy-start.30 = (f32[16,128,128]{2,1,0:T(8,128)S(1)}, f32[16,128,128]{2,1,0:T(8,128)}, u32[]{:S(2)}) copy-start(f32[16,128,128]{2,1,0:T(8,128)} %copy-done.29) | copy-start | bytes 3145732
  3314.5 3.3 copy-start.12
  3314.5 3.3 copy-start.40
  3333.1 23.4 copy-start.21
  3356.5 1.6 copy-start.8
  3358.1 2.8 copy-start.16
  3360.8 1.9 copy-start.17
  3361.3 2.2 copy-start.20
  3362.8 1.7 copy-start.10
  3362.8 1.7 copy-start.28
  3362.8 1.7 copy-start.33
  3362.8 1.7 copy-start.35
  3363.5 1.0 copy-start.22
  3379.3 1.2 copy-start.19
  3379.3 947.6 %reduce-scatter.11.cloned.1.call-start = ((), (), s32[]{:S(2)}) async-start(), calls=%async_computation.12 | async-start | bytes 37748736 | tf_op jit(solution)/shard_map/reduce_scatter | solution.py:120
  3396.6 1.6 copy-start.6
  3396.6 1989.3 %reduce-scatter.9.cloned.1.call-start = ((), (), s32[]{:S(2)}) async-start(), calls=%async_computation.11 | async-start | bytes 75497472 | tf_op jit(solution)/shard_map/reduce_scatter | solution.py:120
  3427.1 2034.0 %all-reduce.8.cloned.1.call-start = ((), (), s32[]{:S(2)}) async-start(), calls=%async_computation.8 | async-start | bytes 1048576 | tf_op jit(solution)/shard_map/psum | solution.py:354
  3427.7 2325.5 %all-reduce.10.cloned.1.call-start = ((), (), s32[]{:S(2)}) async-start(), calls=%async_computation.16 | async-start | bytes 33554432 | tf_op jit(solution)/shard_map/psum | solution.py:129
  5463.3 14.9 copy-start.41
  5463.3 58.4 %copy-start.3 = (f32[256,2048]{1,0:T(8,128)S(1)}, f32[256,2048]{1,0:T(8,128)}, u32[]{:S(2)}) copy-start(f32[256,2048]{1,0:T(8,128)} %copy-done.2) | copy-start | bytes 6291460
  5753.2 5.4 copy-start.31
  (3 other events, 2.1 us)
Sparse Core Ops, SparseCore 0:
  9.6 483.1 all-gather.14
  514.5 200.2 all-gather.22
  716.9 192.0 all-gather.16
  910.3 1267.6 all-gather.18
  2179.4 637.6 all-gather.20
  2890.6 73.5 all-gather.24
  2966.4 159.4 all-gather.26
  3129.5 202.8 reduce-scatter.6
  3379.4 400.9 reduce-scatter.4
  3784.5 542.3 reduce-scatter.10
  4331.1 1054.7 reduce-scatter.8
  5389.6 71.5 all-reduce.7
  5463.9 289.2 all-reduce.9
where the time goes:
time: 5790 us
  waiting for transfers between devices  4370 us (75%)
  blocking collectives  928 us (16%)
  matrix products  291 us (5%)
  other arithmetic  93.2 us (2%)
  local copies, waits for them, and re-layouts  59.2 us (1%)
    reduce_scatter x4, waiting for transfers between devices, weight_rows(): lax.psum_scatter(term_fn(jnp.int32(0), shard_rows * lax.axis_size('wide')...  1960 us
    all_gather x1, waiting for transfers between devices, body(): weight_piece = lax.all_gather(gate_up_weight, 'wide', axis=0, tiled=True)  1080 us
    all_gather x1, waiting for transfers between devices, body(): lax.all_gather(down_weight, 'wide', axis=0, tiled=True)  606 us
    all_gather x1, waiting for transfers between devices, body(): lax.all_gather(qkv_weight, 'wide', axis=0, tiled=True)  434 us
    all_gather x2, blocking collectives, entering_2(): lax.all_gather(a.astype(kind), axis)  338 us
    unnamed x2, blocking collectives  257 us
    psum x1, waiting for transfers between devices, replica_total(): lax.psum(as_sent(members), 'narrow')  228 us
    all_gather x1, blocking collectives, body(): gain_piece = lax.all_gather(gain_mlp, 'wide', axis=0, tiled=True)  125 us
  transfers between devices with their start and end apart: 19, of which 8 were waited for; matrix products, arithmetic and copies ran while one was open for 5% of the time, Pallas kernels for 0%

commit v1 on v0

v1 whole, which is shorter than its diff:
```python
import functools

import jax
import jax.numpy as jnp
from jax import lax
from jax.experimental import pallas as pl
from jax.experimental.pallas import tpu as pltpu
from jax.sharding import PartitionSpec as P

D = 2048
H = 16
DK = 128
FF = 8192
SEG = 1024
EPSILON = 1e-06
F32 = jnp.float32
BF16 = jnp.bfloat16
GROUP = 8


def swap_x(v):
    n = lax.axis_size("wide")
    return lax.ppermute(v, "wide", [(i, i ^ 1) for i in range(n)])


def swap_y(v):
    return lax.ppermute(v, "narrow", [(i, i ^ 2) for i in range(4)])


def swap_core(v):
    return lax.ppermute(v, "narrow", [(i, i ^ 1) for i in range(4)])


def swap_z(v, d):
    n = lax.axis_size("wide")
    return lax.ppermute(v, "wide", [(i, i ^ (2 * d)) for i in range(n)])


def ring_z(v):
    n = lax.axis_size("wide")
    return lax.ppermute(v, "wide", [(i, (i - 2) % n) for i in range(n)])


def offset_bits(r):
    return (r >> 1) & 1, (r >> 2) & 1, r & 1


def absolute(r):
    y, core, x = offset_bits(r)
    return y * 4 + core * 2 + x


def send_offset(v, r):
    y, core, x = offset_bits(r)
    n = lax.axis_size("wide")
    flip = y * 2 + core
    route = [(a * n + b, (a ^ flip) * n + (b ^ x)) for a in range(4) for b in range(n)]
    return lax.ppermute(v, ("narrow", "wide"), route)


def gather_group(v):
    half = v.shape[0] // 2
    a, b = v[:half], v[half:]
    a1 = swap_x(a)
    b2 = swap_y(b)
    a2 = swap_y(jnp.stack([a, a1]))
    b1 = swap_x(jnp.stack([b, b2]))
    own = jnp.concatenate([a, b, a1, b1[0], a2[0], b2, a2[1], b1[1]], axis=0)
    return own, swap_core(own)


def add(a, b):
    return (a.astype(F32) + b.astype(F32)).astype(BF16)


def scatter_group(own, other):
    rows = own.shape[0] // 4
    half = rows // 2
    q = own.astype(F32) + swap_core(other).astype(F32)
    q = q.reshape(4, 2, half, -1)
    qs = q.astype(BF16)
    ay = swap_y(qs[2:4, 0])
    bx = swap_x(jnp.stack([qs[1, 1], qs[3, 1]]))
    a0, a1 = q[0, 0] + ay[0].astype(F32), q[1, 0] + ay[1].astype(F32)
    b0, b2 = q[0, 1] + bx[0].astype(F32), q[2, 1] + bx[1].astype(F32)
    a = a0 + swap_x(a1.astype(BF16)).astype(F32)
    b = b0 + swap_y(b2.astype(BF16)).astype(F32)
    return jnp.concatenate([a, b], axis=0)


def exchange_group(blocks):
    return [blocks[0]] + [send_offset(blocks[r], r) for r in range(1, GROUP)]


def by_bit(pair, bit):
    a, b = pair
    return jnp.where(bit == 0, jnp.stack([a, b]), jnp.stack([b, a]))


def by_index(parts, index):
    if len(parts) == 2:
        return by_bit(parts, index)
    out = jnp.zeros((len(parts),) + parts[0].shape, parts[0].dtype)
    for d, part in enumerate(parts):
        out = lax.dynamic_update_slice_in_dim(out, part[None], index ^ d, 0)
    return out


def gather_rows(weight, starts, width, z, x, n):
    c = n * 2 + x
    mine = jnp.concatenate(
        [lax.dynamic_slice_in_dim(weight, s + c * width, width, 1) for s in starts], axis=1
    )
    theirs = jnp.concatenate(
        [lax.dynamic_slice_in_dim(weight, s + (c ^ 1) * width, width, 1) for s in starts], axis=1
    )
    pair = by_bit([mine, swap_x(theirs)], x)
    rows = pair.shape[0] * pair.shape[1]
    block = pair.reshape(rows, -1)
    count = lax.axis_size("wide") // 2
    out = jnp.zeros((count * rows, block.shape[1]), block.dtype)
    out = lax.dynamic_update_slice_in_dim(out, block, z * rows, 0)
    for k in range(1, count):
        block = ring_z(block)
        out = lax.dynamic_update_slice_in_dim(out, block, lax.rem(z + k, count) * rows, 0)
    return out


def reduce_rows(partial, z):
    count = lax.axis_size("wide") // 2
    rows = partial.shape[0] // count

    def block(k):
        return lax.dynamic_slice_in_dim(partial, lax.rem(z + k, count) * rows, rows, 0)

    running = block(1)
    for k in range(2, count + 1):
        running = ring_z(running).astype(F32) + block(k).astype(F32)
        if k < count:
            running = running.astype(BF16)
    return running


def spread_columns(summed, x):
    rows = summed.shape[0] // 2
    short = summed.astype(BF16)
    keep = lax.dynamic_slice_in_dim(short, x * rows, rows, 0)
    give = lax.dynamic_slice_in_dim(short, (1 - x) * rows, rows, 0)
    pair = jnp.stack([keep, swap_x(give)])
    four = jnp.concatenate([pair, swap_y(pair)], axis=0)
    return four, swap_core(four)


def assemble_kernel(parts, low, high, order, a_ref, b_ref, o_ref):
    del parts, low, high
    which = order[pl.program_id(0)]

    @pl.when(which < 4)
    def _():
        o_ref[...] = a_ref[0].astype(o_ref.dtype)

    @pl.when(which >= 4)
    def _():
        o_ref[...] = b_ref[0].astype(o_ref.dtype)


def assemble(own, other, c, parts, dtype):
    rows = own.shape[1]
    width = own.shape[2] // parts
    flips = c ^ jnp.arange(GROUP, dtype=jnp.int32)
    order = ((flips >> 1) & 1) * 4 + ((flips >> 2) & 1) * 2 + (flips & 1)
    step = min(rows, 256)
    return pl.pallas_call(
        functools.partial(assemble_kernel, parts, 0, 0),
        grid_spec=pltpu.PrefetchScalarGridSpec(
            num_scalar_prefetch=1,
            grid=(GROUP, parts, rows // step),
            in_specs=[
                pl.BlockSpec((1, step, width), lambda j, p, i, o: (jnp.minimum(o[j], 3), i, p)),
                pl.BlockSpec((1, step, width), lambda j, p, i, o: (jnp.maximum(o[j] - 4, 0), i, p)),
            ],
            out_specs=pl.BlockSpec((step, width), lambda j, p, i, o: (i, p * GROUP + j)),
        ),
        out_shape=jax.ShapeDtypeStruct((rows, parts * GROUP * width), dtype),
        compiler_params=pltpu.CompilerParams(vmem_limit_bytes=24 * 2**20),
    )(order, own, other)


def dot(a, b):
    return jnp.dot(a, b, preferred_element_type=F32)


def dot_t(a, b):
    return lax.dot_general(a, b, (((1,), (1,)), ((), ())), preferred_element_type=F32)


def t_dot(a, b):
    return lax.dot_general(a, b, (((0,), (0,)), ((), ())), preferred_element_type=F32)


def norm_back(grad_unit, unit_rows, scale_rows):
    return scale_rows * (
        grad_unit - unit_rows * jnp.mean(grad_unit * unit_rows, axis=-1, keepdims=True)
    )


def elu_slope(inputs):
    return jnp.where(inputs > 0, 1.0, jnp.exp(jnp.minimum(inputs, 0.0)))


def body(
    tokens,
    cotangent,
    qkv_weight,
    out_weight,
    gain_attn,
    gate_up_weight,
    down_weight,
    gain_mlp,
    gate_logit,
    memory_in,
    normalizer_in,
):
    wide = lax.axis_size("wide")
    n = lax.axis_index("narrow")
    w = lax.axis_index("wide")
    z, x = w // 2, w % 2
    c = n * 2 + x
    rows_here = tokens.shape[1]
    shard = qkv_weight.shape[0]
    span = SEG // rows_here
    zspan = span // 2
    zi = z % zspan
    segments = wide // span
    units = GROUP // zspan
    head_cols = D // GROUP
    ff_cols = FF // GROUP
    scale = DK ** (-0.5)

    inputs = tokens[0].astype(F32)
    scale_one = lax.rsqrt(jnp.mean(inputs * inputs, axis=-1, keepdims=True) + EPSILON)
    unit_one = inputs * scale_one
    gains = lax.all_gather(jnp.stack([gain_attn, gain_mlp]), "wide", axis=1, tiled=True)
    gains = gains.astype(F32)
    gain_one, gain_two = gains[0], gains[1]
    normed_one = (unit_one * gain_one).astype(BF16)
    one_own, one_other = gather_group(normed_one)

    qkv_c = gather_rows(qkv_weight, (0, D, 2 * D), head_cols, z, x, n)
    out_quarter = lax.dynamic_slice_in_dim(out_weight, n * (D // 4), D // 4, 1)
    out_all = lax.all_gather(out_quarter, ("narrow", "wide"), axis=0)
    out_full = (
        out_all.reshape(4, wide, shard, D // 4).transpose(1, 2, 0, 3).reshape(D, D)
    )
    gate_c = gather_rows(gate_up_weight, (0,), ff_cols, z, x, n)
    up_c = gather_rows(gate_up_weight, (FF,), ff_cols, z, x, n)
    down_c = gather_rows(down_weight, (0,), ff_cols, z, x, n)

    cot = cotangent[0]
    cot_own, cot_other = gather_group(cot)

    def to_units(flat, parts):
        v = flat.reshape(2, 2, 2, rows_here, parts, 2, DK).transpose(2, 5, 0, 1, 4, 3, 6)
        v = by_bit([v[0], v[1]], x)
        v = v.transpose(1, 2, 3, 4, 0, 5, 6).reshape(GROUP, parts, 2 * rows_here, DK)
        blocks = []
        for d in range(zspan):
            block = lax.dynamic_slice_in_dim(v, (zi ^ d) * units, units, 0)
            blocks.append(block if d == 0 else swap_z(block, d))
        v = by_index(blocks, zi)
        return v.transpose(1, 2, 0, 3, 4).reshape(units, parts, SEG, DK)

    def from_units(v, parts):
        v = v.reshape(units, parts, zspan, 2 * rows_here, DK)
        blocks = []
        for d in range(zspan):
            block = lax.dynamic_slice_in_dim(v, zi ^ d, 1, 2)[:, :, 0]
            blocks.append(block if d == 0 else swap_z(block, d))
        v = by_index(blocks, zi).reshape(2, 2, 2, parts, 2, rows_here, DK)
        v = by_bit([v[:, :, :, :, 0], v[:, :, :, :, 1]], x)
        v = v.transpose(2, 3, 0, 5, 4, 1, 6)
        return v.reshape(GROUP * rows_here, parts * head_cols)

    one_all = jnp.concatenate([one_own, one_other], axis=0)
    projected = dot(one_all, qkv_c).astype(BF16)
    qkv_units = to_units(projected, 3)
    queries, keys, values = qkv_units[:, 0], qkv_units[:, 1], qkv_units[:, 2]

    positions = jnp.arange(SEG)
    allowed = positions[None, :] <= positions[:, None]
    raw = jnp.einsum("utd,usd->uts", queries, keys, preferred_element_type=F32) * scale
    scores = jnp.where(allowed[None], raw, -1e30)
    highest = jnp.max(scores, axis=-1, keepdims=True)
    raised = jnp.exp(scores - highest)
    attn_probs = raised / jnp.sum(raised, axis=-1, keepdims=True)
    short_probs = attn_probs.astype(BF16)
    direct = jnp.einsum("uts,usd->utd", short_probs, values, preferred_element_type=F32)

    head_count = max(1, units // 4)
    seq_count = units // head_count
    first_head = (zi * units) // 4
    first_seq = (zi * units) % 4
    held = jnp.concatenate([memory_in[0], normalizer_in[0][:, None]], axis=1)
    fetched = []
    for offset in range(4):
        core, y = offset >> 1, offset & 1
        flip = y * 2 + core
        block = lax.dynamic_slice_in_dim(
            held, ((n ^ flip) * 2 + x) * 2 + first_head, head_count, 0
        )
        if flip:
            block = lax.ppermute(block, "narrow", [(i, i ^ flip) for i in range(4)])
        fetched.append(block)
    mem_in = jnp.stack(fetched, axis=1)
    mem_in = lax.dynamic_slice_in_dim(mem_in, first_seq, seq_count, 1)
    mem_in = mem_in.reshape(units, DK + 1, DK)

    query_f, key_f, value_f = (a.astype(F32) for a in (queries, keys, values))
    lift_q = jax.nn.elu(query_f) + 1.0
    lift_k = jax.nn.elu(key_f) + 1.0
    part_mem = jnp.einsum("utd,ute->ude", lift_k, value_f, preferred_element_type=F32)
    part_norm = jnp.sum(lift_k, axis=1)
    part = jnp.concatenate([part_mem, part_norm[:, None]], axis=1) / SEG
    read = mem_in
    for k in range(1, segments):
        read = read + lax.ppermute(
            part, "wide", [(i, i + k * span) for i in range(wide - k * span)]
        )
    read_mem, read_norm = read[:, :DK], read[:, DK]
    numerator = jnp.einsum("utd,ude->ute", lift_q, read_mem, preferred_element_type=F32)
    denominator = jnp.sum(lift_q * read_norm[:, None], axis=-1, keepdims=True)
    recalled = numerator / denominator

    unit_heads = c * 2 + (zi * units + jnp.arange(units)) // 4
    mixing = jax.nn.sigmoid(gate_logit[unit_heads])
    mix = mixing[:, None, None]
    attended_units = (mix * recalled + (1.0 - mix) * direct).astype(BF16)
    attended_c = from_units(attended_units[:, None], 1).reshape(GROUP, rows_here, head_cols)
    sent = exchange_group([attended_c[r] for r in range(GROUP)])
    attended = assemble(jnp.stack(sent[:4]), jnp.stack(sent[4:]), c, 1, BF16)

    middle = inputs + dot(attended, out_full)
    scale_two = lax.rsqrt(jnp.mean(middle * middle, axis=-1, keepdims=True) + EPSILON)
    unit_two = middle * scale_two
    normed_two = (unit_two * gain_two).astype(BF16)
    two_own, two_other = gather_group(normed_two)
    two_all = jnp.concatenate([two_own, two_other], axis=0)
    cot_all = jnp.concatenate([cot_own, cot_other], axis=0)

    gate_part = dot(two_all, gate_c)
    up_part = dot(two_all, up_c)
    gate_sig = jax.nn.sigmoid(gate_part)
    activation = (gate_part * gate_sig * up_part).astype(BF16)

    def group_sum(product):
        half = 4 * rows_here
        return scatter_group(product[:half], product[half:])

    output = (middle + group_sum(dot_t(activation, down_c).astype(BF16))).astype(BF16)[None]

    grad_down_c = reduce_rows(t_dot(cot_all, activation).astype(BF16), z)
    grad_activ = dot(cot_all, down_c)
    grad_gate = (grad_activ * up_part * gate_sig * (1.0 + gate_part * (1.0 - gate_sig))).astype(BF16)
    grad_upper = (grad_activ * gate_part * gate_sig).astype(BF16)
    grad_normed_two = group_sum(
        (dot_t(grad_gate, gate_c) + dot_t(grad_upper, up_c)).astype(BF16)
    )
    grad_gate_c = reduce_rows(t_dot(two_all, grad_gate).astype(BF16), z)
    grad_up_c = reduce_rows(t_dot(two_all, grad_upper).astype(BF16), z)
    grad_gain_two = jnp.sum(grad_normed_two * unit_two, axis=0)
    grad_middle = cot.astype(F32) + norm_back(grad_normed_two * gain_two, unit_two, scale_two)

    grad_branch = grad_middle.astype(BF16)
    grad_att_rows = dot_t(grad_branch, out_full).astype(BF16)
    sent = exchange_group(
        [
            lax.dynamic_slice_in_dim(grad_att_rows, (c ^ absolute(r)) * head_cols, head_cols, 1)
            for r in range(GROUP)
        ]
    )
    grad_att = to_units(jnp.concatenate(sent, axis=0), 1)[:, 0].astype(F32)

    unit_logit = jnp.sum(grad_att * (recalled - direct), axis=(1, 2)) * mixing * (1.0 - mixing)
    grad_logit = jnp.sum(
        jnp.where(unit_heads[:, None] == jnp.arange(H)[None], unit_logit[:, None], 0.0), axis=0
    )
    grad_direct = ((1.0 - mix) * grad_att).astype(BF16)
    grad_recall = (mix * grad_att).astype(BF16).astype(F32)
    grad_probs = jnp.einsum("utd,usd->uts", grad_direct, values, preferred_element_type=F32)
    inner = jnp.sum(attn_probs * grad_probs, axis=-1, keepdims=True)
    grad_scores = (attn_probs * (grad_probs - inner)).astype(BF16)
    grad_q_dot = jnp.einsum("uts,usd->utd", grad_scores, keys, preferred_element_type=F32) * scale
    grad_k_dot = jnp.einsum("uts,utd->usd", grad_scores, queries, preferred_element_type=F32) * scale
    grad_v_dot = jnp.einsum("uts,utd->usd", short_probs, grad_direct, preferred_element_type=F32)

    grad_numer = grad_recall / denominator
    grad_denom = -jnp.sum(grad_recall * recalled, axis=-1, keepdims=True) / denominator
    grad_lift_q = (
        jnp.einsum("ute,ude->utd", grad_numer, read_mem, preferred_element_type=F32)
        + grad_denom * read_norm[:, None]
    )
    grad_read_mem = jnp.einsum("utd,ute->ude", lift_q, grad_numer, preferred_element_type=F32)
    grad_read_norm = jnp.sum(grad_denom * lift_q, axis=1)
    grad_read = jnp.concatenate([grad_read_mem, grad_read_norm[:, None]], axis=1)
    later = jnp.zeros_like(grad_read)
    for k in range(1, segments):
        later = later + lax.ppermute(
            grad_read, "wide", [(i + k * span, i) for i in range(wide - k * span)]
        )
    later = later / SEG
    later_mem, later_norm = later[:, :DK], later[:, DK]
    grad_lift_k = (
        jnp.einsum("ute,ude->utd", value_f, later_mem, preferred_element_type=F32)
        + later_norm[:, None]
    )
    grad_v_mem = jnp.einsum("utd,ude->ute", lift_k, later_mem, preferred_element_type=F32)
    grad_units = jnp.stack(
        [
            grad_q_dot + grad_lift_q * elu_slope(query_f),
            grad_k_dot + grad_lift_k * elu_slope(key_f),
            grad_v_dot + grad_v_mem,
        ],
        axis=1,
    ).astype(BF16)
    grad_projected = from_units(grad_units, 3)

    grad_normed_one = group_sum(dot_t(grad_projected, qkv_c).astype(BF16))
    grad_gain_one = jnp.sum(grad_normed_one * unit_one, axis=0)
    grad_tokens = (
        grad_middle + norm_back(grad_normed_one * gain_one, unit_one, scale_one)
    ).astype(BF16)[None]
    grad_qkv_c = reduce_rows(t_dot(one_all, grad_projected).astype(BF16), z)

    att_own, att_other = gather_group(attended)
    att_all = jnp.concatenate([att_own, att_other], axis=0)
    sent = exchange_group(
        [
            lax.dynamic_slice_in_dim(grad_branch, (c ^ absolute(r)) * head_cols, head_cols, 1)
            for r in range(GROUP)
        ]
    )
    grad_out_c = reduce_rows(t_dot(att_all, jnp.concatenate(sent, axis=0)).astype(BF16), z)

    def whole_rows(summed, parts):
        own, other = spread_columns(summed, x)
        return assemble(own, other, c, parts, F32)

    grad_gate_up = whole_rows(jnp.concatenate([grad_gate_c, grad_up_c], axis=1), 2)
    grad_down = whole_rows(grad_down_c, 1)
    grad_qkv = whole_rows(grad_qkv_c, 3)
    grad_out = whole_rows(grad_out_c, 1)

    placed = jnp.zeros((GROUP, DK + 1, DK), BF16)
    placed = lax.dynamic_update_slice_in_dim(placed, grad_read.astype(BF16), zi * units, 0)
    placed = placed.reshape(2, 4, DK + 1, DK)
    got = []
    for flip in range(4):
        core, y = flip & 1, flip >> 1
        block = placed[:, core * 2 + y]
        if flip:
            block = lax.ppermute(block, "narrow", [(i, i ^ flip) for i in range(4)])
        got.append(block)
    by_narrow = by_index(got, n)[:, None]
    heads = jnp.zeros((4, 2, 2, DK + 1, DK), BF16)
    heads = lax.dynamic_update_slice_in_dim(heads, by_narrow, x, 1)
    heads = lax.psum(heads.reshape(H, DK + 1, DK), "wide").astype(F32)

    small = lax.psum(
        jnp.concatenate([grad_gain_one, grad_gain_two, grad_logit]), ("narrow", "wide")
    )
    gain_one_sum = lax.dynamic_slice_in_dim(small, w * shard, shard, 0)
    gain_two_sum = lax.dynamic_slice_in_dim(small, D + w * shard, shard, 0)
    return (
        output,
        grad_tokens,
        heads[None, :, :DK],
        heads[None, :, DK],
        grad_qkv,
        grad_out,
        gain_one_sum,
        grad_gate_up,
        grad_down,
        gain_two_sum,
        small[2 * D :],
    )


def solution(mesh):
    return jax.shard_map(
        body,
        mesh=mesh,
        in_specs=(
            P("narrow", "wide", None),
            P("narrow", "wide", None),
            P("wide", None),
            P("wide", None),
            P("wide"),
            P("wide", None),
            P("wide", None),
            P("wide"),
            P(),
            P("narrow", None, None, None),
            P("narrow", None, None),
        ),
        out_specs=(
            P("narrow", "wide", None),
            P("narrow", "wide", None),
            P("narrow", None, None, None),
            P("narrow", None, None),
            P("wide", None),
            P("wide", None),
            P("wide"),
            P("wide", None),
            P("wide", None),
            P("wide"),
            P(),
        ),
        check_vma=False,
    )
```

time: 5790 us -> 1430 us (0.25)
  waiting for transfers between devices: 4370 us -> 574 us
  blocking collectives: 928 us -> 62.3 us
  starting transfers between devices: 18.6 us -> 228 us
  local copies, waits for them, and re-layouts: 59.2 us -> 174 us
  matrix products: 291 us -> 225 us
    all_gather x7 -> x1, waiting for transfers between devices: 2120 us -> 0.02 us  [body(): out_all = lax.all_gather(out_quarter, ('narrow', 'wide'), axis=0)]
    reduce_scatter x4 -> x0, waiting for transfers between devices: 1960 us -> none  [weight_rows(): lax.psum_scatter(term_fn(jnp.int32(0), shard_rows * lax.axis_size('wide')...]
    all_gather x5 -> x1, blocking collectives: 630 us -> 22.2 us  [body(): lax.all_gather(jnp.stack([gain_attn, gain_mlp]), 'wide', axis=1, tiled=True)]
    ppermute x6 -> x111, waiting for transfers between devices: 0.02 us -> 512 us  [the longest x27 222 us: ring_z(): return lax.ppermute(v, 'wide', [(i, (i - 2) % n) for i in range(n)])]
    unnamed x2 -> x0, blocking collectives: 257 us -> none
    psum x2 -> x1, waiting for transfers between devices: 286 us -> 61.3 us  [body(): heads = lax.psum(heads.reshape(H, DK + 1, DK), 'wide').astype(F32)]
    ppermute x6 -> x111, starting transfers between devices: 17.9 us -> 228 us  [the longest x27 80.1 us: ring_z(): return lax.ppermute(v, 'wide', [(i, (i - 2) % n) for i in range(n)])]
    dot_general x26, matrix products: 291 us -> 213 us  [the longest x5 62.2 us: dot(): return jnp.dot(a, b, preferred_element_type=F32)]
  transfers between devices with their start and end apart: 19 -> 113, of which waited for: 8 -> 53; matrix products, arithmetic and copies ran while one was open for 5% -> 26% of each run, Pallas kernels for 0% -> 3%
where the time goes in v1:
time: 1430 us; the launch traced here: 1420 us
  waiting for transfers between devices  574 us (40%)
  starting transfers between devices  228 us (16%)
  matrix products  225 us (16%)
  local copies, waits for them, and re-layouts  174 us (12%)
  other arithmetic  97.2 us (7%)
  blocking collectives  62.3 us (4%)
  Pallas kernels  44.7 us (3%)
  between operations  16.9 us (1%)
    ppermute x27, waiting for transfers between devices, ring_z(): return lax.ppermute(v, 'wide', [(i, (i - 2) % n) for i in range(n)])  222 us
    ppermute x22, waiting for transfers between devices, swap_x(): return lax.ppermute(v, 'wide', [(i, i ^ 1) for i in range(n)])  130 us
    ppermute x18, waiting for transfers between devices, swap_y(): return lax.ppermute(v, 'narrow', [(i, i ^ 2) for i in range(4)])  90.1 us
    ppermute x27, starting transfers between devices, ring_z(): return lax.ppermute(v, 'wide', [(i, (i - 2) % n) for i in range(n)])  80.1 us
    ppermute x4, starting transfers between devices, swap_z(): return lax.ppermute(v, 'wide', [(i, i ^ 2 * d) for i in range(n)])  70.3 us
    unnamed x272, local copies, waits for them, and re-layouts  67.5 us
    dot_general x5, matrix products, dot(): return jnp.dot(a, b, preferred_element_type=F32)  62.2 us
    psum x1, waiting for transfers between devices, body(): heads = lax.psum(heads.reshape(H, DK + 1, DK), 'wide').astype(F32)  61.3 us
  transfers between devices with their start and end apart: 113, of which 53 were waited for; matrix products, arithmetic and copies ran while one was open for 26% of the time, Pallas kernels for 3%

profile of v1, /device:TPU:0, one launch (start us, length us, event | category | flops | bytes accessed | tf_op | source)
XLA Modules:
  0.0 1420.9 jit_solution(18135442027125598876)
XLA Ops:
  8.6 22.2 %all_gather.9 = bf16[2,2048]{1,0:T(2,128)(2,1)S(1)} all-gather(bf16[2,256]{1,0:T(2,128)(2,1)S(1)} %pad_maximum_fusion.29), channel_id=1, replica_groups=mesh['narrow'=4,'wide'=8] {'wide'}, dimensions={1}, use_global_device_ids=true | all-gather | bytes 9216 | tf_op jit(solution)/shard_map/all_gather | solution.py:243
  63.1 38.1 %collective-permute-done.2 = bf16[2,128,2048]{2,1,0:T(8,128)(2,1)S(1)} collective-permute-done((bf16[2,128,2048]{2,1,0:T(8,128)(2,1)S(1)}, bf16[2,128,2048]{2,1,0:T(8,128)(2,1)S(1)}, u32[]{:S(2)}, u32[]{:S(2)}) %collective-permute-start.2) | collective-permute-done | bytes 1048608 | tf_op jit(solution)/shard_map/ppermute | solution.py:23
  116.3 9.9 collective-permute-done.35
  130.3 10.8 collective-permute-done.31
  156.7 26.3 %collective-permute-done.7 = bf16[512,768]{1,0:T(8,128)(2,1)S(1)} collective-permute-done((bf16[512,768]{1,0:T(8,128)(2,1)S(1)}, bf16[512,768]{1,0:T(8,128)(2,1)S(1)}, u32[]{:S(2)}, u32[]{:S(2)}) %collective-permute-start.7) | collective-permute-done | bytes 786464 | tf_op jit(solution)/shard_map/ppermute | solution.py:41
  188.7 12.4 collective-permute-done.8
  212.8 8.0 convolution_convert_fusion.5
  220.8 6.9 reshape.497
  241.3 27.1 %collective-permute-done.9 = bf16[4,3,512,128]{3,2,1,0:T(8,128)(2,1)S(1)} collective-permute-done((bf16[4,3,512,128]{3,2,1,0:T(8,128)(2,1)S(1)}, bf16[4,3,512,128]{3,2,1,0:T(8,128)(2,1)S(1)}, u32[]{:S(2)}, u32[]{:S(2)}) %collective-permute-start.9) | collective-permute-done | bytes 1572896 | tf_op jit(solution)/shard_map/ppermute | solution.py:36
  275.8 11.4 fusion.158
  302.9 11.6 add_convert_fusion.11
  315.8 70.1 %collective-permute-start.14 = (bf16[4,1,512,128]{3,2,0,1:T(8,128)(2,1)S(1)}, bf16[4,1,512,128]{3,2,0,1:T(8,128)(2,1)S(1)}, u32[]{:S(2)}, u32[]{:S(2)}) collective-permute-start(bf16[4,1,512,128]{3,2,0,1:T(8,128)(2,1)S(1)} %get-tuple-element.143), channel_id=1, source_target_pairs={{0,2},{1,3},{2,0},{3,1},{4,6},{5,7},{6,4},{7,5},{8,10},{9,11},{10,... | collective-permute-start | bytes 1572872 | tf_op jit(solution)/shard_map/ppermute | solution.py:36
  406.7 13.8 collective-permute-done.38
  427.2 12.6 collective-permute-start.34
  443.4 14.5 %copy.148 = bf16[4,8,256,512]{2,1,3,0:T(8,128)(2,1)} copy(bf16[4,8,256,512]{3,2,1,0:T(8,128)(2,1)} %bitcast.586) | data formatting | bytes 16777216 | tf_op jit(solution)/shard_map/reshape | solution.py:253
  457.9 10.5 copy.194
  468.4 5.9 multiply_reduce_fusion.5
  477.4 7.0 collective-permute-done.30
  493.1 7.5 collective-permute-done.22
  504.3 18.8 %collective-permute-done.24 = bf16[2,128,2048]{2,1,0:T(8,128)(2,1)S(1)} collective-permute-done((bf16[2,128,2048]{2,1,0:T(8,128)(2,1)S(1)}, bf16[2,128,2048]{2,1,0:T(8,128)(2,1)S(1)}, u32[]{:S(2)}, u32[]{:S(2)}) %collective-permute-start.24) | collective-permute-done | bytes 1048608 | tf_op jit(solution)/shard_map/ppermute | solution.py:23
  527.2 5.2 collective-permute-done.79
  535.8 13.4 fusion.160
  558.7 13.2 fusion.159
  571.9 21.8 %multiply_convert_fusion.2 = (bf16[2048,1024]{1,0:T(8,128)(2,1)}, bf16[2048,1024]{1,0:T(8,128)(2,1)}, bf16[2048,1024]{1,0:T(8,128)(2,1)}) fusion(f32[2048,1024]{1,0:T(8,128)} %fusion.160, f32[2048,1024]{1,0:T(8,128)} %fusion.159, bf16[2048,2048]{1,0:T(8,128)(2,1)} %constant_dynamic-update-slice_fusion.10, ...), kind=kOutput, calls=%fused_computation.14 | convolution fusion | flops 8623489024 | bytes 41943040 | tf_op jit(solution)/shard_map/dot_general | solution.py:190
  593.7 15.4 %fusion.161 = f32[2048,2048]{1,0:T(8,128)} fusion(bf16[2048,1024]{1,0:T(8,128)(2,1)} %get-tuple-element.28, bf16[2048,1024]{1,0:T(8,128)(2,1)} %copy-done.37), kind=kOutput, calls=%fused_computation.497 | convolution fusion | flops 8589934592 | bytes 25165824 | tf_op jit(solution)/shard_map/dot_general | solution.py:194
  609.1 10.9 convolution_convert_fusion.3
  620.1 10.6 convolution_convert_fusion.4
  630.7 14.6 %add_convert_fusion = bf16[2048,2048]{1,0:T(8,128)(2,1)S(1)} fusion(f32[2048,2048]{1,0:T(8,128)} %fusion.161, bf16[2048,1024]{1,0:T(8,128)(2,1)} %get-tuple-element.26, bf16[2048,1024]{1,0:T(8,128)(2,1)} %copy-done.31), kind=kOutput, calls=%fused_computation.4 | convolution fusion | flops 8598323200 | bytes 33554432 | tf_op jit(solution)/shard_map/dot_general | solution.py:194
  657.6 11.5 convolution_convert_fusion.2
  670.5 9.0 collective-permute-done.96
  684.2 17.7 %collective-permute-done.99 = bf16[512,1024]{1,0:T(8,128)(2,1)S(1)} collective-permute-done((bf16[512,1024]{1,0:T(8,128)(2,1)S(1)}, bf16[512,1024]{1,0:T(8,128)(2,1)S(1)}, u32[]{:S(2)}, u32[]{:S(2)}) %collective-permute-start.99) | collective-permute-done | bytes 1048608 | tf_op jit(solution)/shard_map/ppermute | solution.py:41
  707.6 11.0 convolution_convert_fusion.1
  729.1 17.7 %collective-permute-done.97 = bf16[512,1024]{1,0:T(8,128)(2,1)} collective-permute-done((bf16[512,1024]{1,0:T(8,128)(2,1)S(1)}, bf16[512,1024]{1,0:T(8,128)(2,1)}, u32[]{:S(2)}, u32[]{:S(2)}) %collective-permute-start.97) | collective-permute-done | bytes 1048608 | tf_op jit(solution)/shard_map/ppermute | solution.py:41
  752.9 16.5 %collective-permute-done.100 = bf16[512,1024]{1,0:T(8,128)(2,1)} collective-permute-done((bf16[512,1024]{1,0:T(8,128)(2,1)}, bf16[512,1024]{1,0:T(8,128)(2,1)}, u32[]{:S(2)}, u32[]{:S(2)}) %collective-permute-start.100) | collective-permute-done | bytes 1048608 | tf_op jit(solution)/shard_map/ppermute | solution.py:41
  777.6 14.2 collective-permute-done.106
  797.8 16.4 %collective-permute-done.98 = bf16[512,1024]{1,0:T(8,128)(2,1)S(1)} collective-permute-done((bf16[512,1024]{1,0:T(8,128)(2,1)S(1)}, bf16[512,1024]{1,0:T(8,128)(2,1)S(1)}, u32[]{:S(2)}, u32[]{:S(2)}) %collective-permute-start.98) | collective-permute-done | bytes 1048608 | tf_op jit(solution)/shard_map/ppermute | solution.py:41
  814.7 22.1 %collective-permute-done.101 = bf16[512,1024]{1,0:T(8,128)(2,1)S(1)} collective-permute-done((bf16[512,1024]{1,0:T(8,128)(2,1)S(1)}, bf16[512,1024]{1,0:T(8,128)(2,1)S(1)}, u32[]{:S(2)}, u32[]{:S(2)}) %collective-permute-start.101) | collective-permute-done | bytes 1048608 | tf_op jit(solution)/shard_map/ppermute | solution.py:41
  848.8 5.4 convert_add_fusion.2
  854.7 17.5 %collective-permute-done.50 = bf16[2,128,2048]{2,1,0:T(8,128)(2,1)S(1)} collective-permute-done((bf16[2,128,2048]{2,1,0:T(8,128)(2,1)}, bf16[2,128,2048]{2,1,0:T(8,128)(2,1)S(1)}, u32[]{:S(2)}, u32[]{:S(2)}) %collective-permute-start.50) | collective-permute-done | bytes 1048608 | tf_op jit(solution)/shard_map/ppermute | solution.py:27
  873.2 19.5 %collective-permute-done.40 = bf16[2,128,2048]{2,1,0:T(8,128)(2,1)S(1)} collective-permute-done((bf16[2,128,2048]{2,1,0:T(8,128)(2,1)S(1)}, bf16[2,128,2048]{2,1,0:T(8,128)(2,1)S(1)}, u32[]{:S(2)}, u32[]{:S(2)}) %collective-permute-start.40) | collective-permute-done | bytes 1048608 | tf_op jit(solution)/shard_map/ppermute | solution.py:27
  901.8 20.2 %collective-permute-done.42 = bf16[2,128,2048]{2,1,0:T(8,128)(2,1)S(1)} collective-permute-done((bf16[2,128,2048]{2,1,0:T(8,128)(2,1)S(1)}, bf16[2,128,2048]{2,1,0:T(8,128)(2,1)S(1)}, u32[]{:S(2)}, u32[]{:S(2)}) %collective-permute-start.42) | collective-permute-done | bytes 1048608 | tf_op jit(solution)/shard_map/ppermute | solution.py:23
  922.0 9.5 collective-permute-done.41
  936.3 8.0 collective-permute-done.43
  960.7 11.7 collective-permute-done.56
  992.0 5.6 collective-permute-done.61
  998.0 10.5 multiply_reduce_fusion
  1008.5 11.7 multiply_convert_fusion
  1036.7 9.6 fusion.5
  1082.2 8.7 collective-permute-done.63
  1097.4 8.0 reshape.507
  1105.4 9.5 convolution_convert_fusion
  1116.8 9.4 convolution_convert_fusion.6
  1128.3 5.9 convolution_convert_fusion.7
  1134.9 11.9 collective-permute-done.72
  1156.4 7.5 shard_map.198
  1164.5 8.4 collective-permute-done.91
  1183.7 13.7 collective-permute-done.74
  1213.4 18.6 %collective-permute-done.65 = bf16[2,128,2048]{2,1,0:T(8,128)(2,1)S(1)} collective-permute-done((bf16[2,128,2048]{2,1,0:T(8,128)(2,1)S(1)}, bf16[2,128,2048]{2,1,0:T(8,128)(2,1)S(1)}, u32[]{:S(2)}, u32[]{:S(2)}) %collective-permute-start.65) | collective-permute-done | bytes 1048608 | tf_op jit(solution)/shard_map/ppermute | solution.py:27
  1234.0 16.2 %collective-permute-done.76 = bf16[2,256,768]{2,1,0:T(8,128)(2,1)S(1)} collective-permute-done((bf16[2,256,768]{2,1,0:T(8,128)(2,1)S(1)}, bf16[2,256,768]{2,1,0:T(8,128)(2,1)S(1)}, u32[]{:S(2)}, u32[]{:S(2)}) %collective-permute-start.76) | collective-permute-done | bytes 786464 | tf_op jit(solution)/shard_map/ppermute | solution.py:27
  1253.3 6.8 collective-permute-done.66
  1265.2 61.3 %all-reduce.2.cloned.1.call-done = bf16[16,129,128]{2,1,0:T(8,128)(2,1)} async-done(((bf16[16,129,128]{2,1,0:T(8,128)(2,1)}), bf16[16,129,128]{2,1,0:T(8,128)(2,1)}) %all-reduce.2.cloned.1.call-update) | async-done | bytes 528400 | tf_op jit(solution)/shard_map/psum | solution.py:466
  1333.6 17.8 %shard_map.197 = f32[256,16384]{1,0:T(8,128)} custom-call(s32[8]{0:T(128)S(1)} %copy-done.3, bf16[4,256,2048]{2,1,0:T(8,128)(2,1)} %pad_maximum_fusion.a_ref, bf16[4,256,2048]{2,1,0:T(8,128)(2,1)} %collective-permute-done.104.b_ref), custom_call_target="tpu_custom_call" | custom-call | tf_op jit(solution)/shard_map/pallas_call | solution.py:173
  1351.4 14.9 %shard_map.195 = f32[256,6144]{1,0:T(8,128)} custom-call(s32[8]{0:T(128)S(1)} %copy-done.3, bf16[4,256,768]{2,1,0:T(8,128)(2,1)S(1)} %pad_maximum_fusion.8.a_ref, bf16[4,256,768]{2,1,0:T(8,128)(2,1)} %collective-permute-done.77.b_ref), custom_call_target="tpu_custom_call" | custom-call | tf_op jit(solution)/shard_map/pallas_call | solution.py:173
  1369.2 40.1 %psum.15 = f32[4112]{0:T(1024)S(1)} all-reduce(f32[4112]{0:T(1024)S(1)} %pad_maximum_fusion.28), channel_id=1, replica_groups=mesh['narrow'=4,'wide'=8] {'narrow','wide'}, use_global_device_ids=true, to_apply=%region_16.17 | all-reduce | flops 4112 | bytes 32896 | tf_op jit(solution)/shard_map/psum | solution.py:468
  (677 shorter events, 429.5 us)
Async XLA Ops:
  7.2 436.2 %all-gather.3.cloned.1.call-start = ((), (), s32[]{:S(2)}) async-start(), calls=%async_computation.1 | async-start | bytes 8650752 | tf_op jit(solution)/shard_map/all_gather | solution.py:251
  40.8 73.9 %collective-permute-start.5 = (bf16[256,768]{1,0:T(8,128)(2,1)}, bf16[256,768]{1,0:T(8,128)(2,1)}, u32[]{:S(2)}, u32[]{:S(2)}) collective-permute-start(bf16[256,768]{1,0:T(8,128)(2,1)} %pad_maximum_fusion.25), channel_id=1, source_target_pairs={{0,1},{1,0},{2,3},{3,2},{4,5},{5,4},{6,7},{7,6},{8,9},{9,8},{10,11... | collective-permute-start | bytes 1179656 | tf_op jit(solution)/shard_map/ppermute | solution.py:23
  43.6 1282.9 %all-reduce.2.cloned.1.call-start = ((), (), s32[]{:S(2)}) async-start(), calls=%async_computation | async-start | bytes 1114112 | tf_op jit(solution)/shard_map/psum | solution.py:466
  45.1 106.4 %collective-permute-start.44 = (bf16[128,2048]{1,0:T(8,128)(2,1)}, bf16[128,2048]{1,0:T(8,128)(2,1)}, u32[]{:S(2)}, u32[]{:S(2)}) collective-permute-start(bf16[128,2048]{1,0:T(8,128)(2,1)} %get-tuple-element.117), channel_id=1, source_target_pairs={{0,1},{1,0},{2,3},{3,2},{4,5},{5,4},{6,7},{7,6},{8,9},{9,8},{10,11... | collective-permute-start | bytes 1572872 | tf_op jit(solution)/shard_map/ppermute | solution.py:23
  45.1 82.0 %collective-permute-start.45 = (bf16[128,2048]{1,0:T(8,128)(2,1)}, bf16[128,2048]{1,0:T(8,128)(2,1)}, u32[]{:S(2)}, u32[]{:S(2)}) collective-permute-start(bf16[128,2048]{1,0:T(8,128)(2,1)} %get-tuple-element.118), channel_id=1, source_target_pairs={{0,16},{8,24},{16,0},{24,8},{1,17},{9,25},{17,1},{25,9},{2,18},{10... | collective-permute-start | bytes 1572872 | tf_op jit(solution)/shard_map/ppermute | solution.py:27
  52.4 48.9 %collective-permute-start.2 = (bf16[2,128,2048]{2,1,0:T(8,128)(2,1)S(1)}, bf16[2,128,2048]{2,1,0:T(8,128)(2,1)S(1)}, u32[]{:S(2)}, u32[]{:S(2)}) collective-permute-start(bf16[2,128,2048]{2,1,0:T(8,128)(2,1)S(1)} %pad_maximum_fusion.9), channel_id=1, source_target_pairs={{0,1},{1,0},{2,3},{3,2},{4,5},{5,4},{6,7},{7,6},{8,9},{9,8},{10,11... | collective-permute-start | bytes 3145736 | tf_op jit(solution)/shard_map/ppermute | solution.py:23
  58.5 43.7 %collective-permute-start.3 = (bf16[2,128,2048]{2,1,0:T(8,128)(2,1)S(1)}, bf16[2,128,2048]{2,1,0:T(8,128)(2,1)S(1)}, u32[]{:S(2)}, u32[]{:S(2)}) collective-permute-start(bf16[2,128,2048]{2,1,0:T(8,128)(2,1)S(1)} %pad_maximum_fusion.10), channel_id=1, source_target_pairs={{0,16},{8,24},{16,0},{24,8},{1,17},{9,25},{17,1},{25,9},{2,18},{10... | collective-permute-start | bytes 3145736 | tf_op jit(solution)/shard_map/ppermute | solution.py:27
  106.9 98.8 %collective-permute-start.4 = (bf16[1024,2048]{1,0:T(8,128)(2,1)}, bf16[1024,2048]{1,0:T(8,128)(2,1)}, u32[]{:S(2)}, u32[]{:S(2)}) collective-permute-start(bf16[1024,2048]{1,0:T(8,128)(2,1)} %get-tuple-element.144), channel_id=1, source_target_pairs={{0,8},{8,0},{16,24},{24,16},{1,9},{9,1},{17,25},{25,17},{2,10},{10... | collective-permute-start | bytes 12582920 | tf_op jit(solution)/shard_map/ppermute | solution.py:31
  116.0 29.9 %collective-permute-start.6 = (bf16[512,768]{1,0:T(8,128)(2,1)S(1)}, bf16[512,768]{1,0:T(8,128)(2,1)S(1)}, u32[]{:S(2)}, u32[]{:S(2)}) collective-permute-start(bf16[512,768]{1,0:T(8,128)(2,1)S(1)} %bitcast.606), channel_id=1, source_target_pairs={{0,6},{1,7},{2,0},{3,1},{4,2},{5,3},{6,4},{7,5},{8,14},{9,15},{10,... | collective-permute-start | bytes 2359304 | tf_op jit(solution)/shard_map/ppermute | solution.py:41
  141.1 44.6 %collective-permute-start.36 = (bf16[512,1024]{1,0:T(8,128)(2,1)S(1)}, bf16[512,1024]{1,0:T(8,128)(2,1)S(1)}, u32[]{:S(2)}, u32[]{:S(2)}) collective-permute-start(bf16[512,1024]{1,0:T(8,128)(2,1)S(1)} %bitcast.602), channel_id=1, source_target_pairs={{0,6},{1,7},{2,0},{3,1},{4,2},{5,3},{6,4},{7,5},{8,14},{9,15},{10,... | collective-permute-start | bytes 3145736 | tf_op jit(solution)/shard_map/ppermute | solution.py:41
  145.9 37.1 %collective-permute-start.7 = (bf16[512,768]{1,0:T(8,128)(2,1)S(1)}, bf16[512,768]{1,0:T(8,128)(2,1)S(1)}, u32[]{:S(2)}, u32[]{:S(2)}) collective-permute-start(bf16[512,768]{1,0:T(8,128)(2,1)S(1)} %collective-permute-done.6), channel_id=1, source_target_pairs={{0,6},{1,7},{2,0},{3,1},{4,2},{5,3},{6,4},{7,5},{8,14},{9,15},{10,... | collective-permute-start | bytes 2359304 | tf_op jit(solution)/shard_map/ppermute | solution.py:41
  148.5 37.4 %collective-permute-start.46 = (bf16[2,128,2048]{2,1,0:T(8,128)(2,1)S(1)}, bf16[2,128,2048]{2,1,0:T(8,128)(2,1)S(1)}, u32[]{:S(2)}, u32[]{:S(2)}) collective-permute-start(bf16[2,128,2048]{2,1,0:T(8,128)(2,1)S(1)} %pad_maximum_fusion.14), channel_id=1, source_target_pairs={{0,1},{1,0},{2,3},{3,2},{4,5},{5,4},{6,7},{7,6},{8,9},{9,8},{10,11... | collective-permute-start | bytes 3145736 | tf_op jit(solution)/shard_map/ppermute | solution.py:23
  151.5 120.7 %collective-permute-start.12 = (f32[1,129,128]{2,0,1:T(1,128)S(1)}, f32[1,129,128]{2,0,1:T(1,128)S(1)}, u32[]{:S(2)}, u32[]{:S(2)}) collective-permute-start(f32[1,129,128]{2,0,1:T(1,128)S(1)} %copy-done.82), channel_id=1, source_target_pairs={{0,24},{8,16},{16,8},{24,0},{1,25},{9,17},{17,9},{25,1},{2,26},{10... | collective-permute-start | bytes 198152 | tf_op jit(solution)/shard_map/ppermute | solution.py:312
  185.7 101.5 %collective-permute-start.11 = (f32[1,129,128]{2,0,1:T(1,128)S(1)}, f32[1,129,128]{2,0,1:T(1,128)S(1)}, u32[]{:S(2)}, u32[]{:S(2)}) collective-permute-start(f32[1,129,128]{2,0,1:T(1,128)S(1)} %copy-done.81), channel_id=1, source_target_pairs={{0,8},{8,0},{16,24},{24,16},{1,9},{9,1},{17,25},{25,17},{2,10},{10... | collective-permute-start | bytes 198152 | tf_op jit(solution)/shard_map/ppermute | solution.py:312
  185.9 101.4 %collective-permute-start.10 = (f32[1,129,128]{2,0,1:T(1,128)S(1)}, f32[1,129,128]{2,0,1:T(1,128)S(1)}, u32[]{:S(2)}, u32[]{:S(2)}) collective-permute-start(f32[1,129,128]{2,0,1:T(1,128)S(1)} %copy-done.80), channel_id=1, source_target_pairs={{0,16},{8,24},{16,0},{24,8},{1,17},{9,25},{17,1},{25,9},{2,18},{10... | collective-permute-start | bytes 198152 | tf_op jit(solution)/shard_map/ppermute | solution.py:312
  201.2 86.2 %collective-permute-start.32 = (bf16[512,1024]{1,0:T(8,128)(2,1)S(1)}, bf16[512,1024]{1,0:T(8,128)(2,1)}, u32[]{:S(2)}, u32[]{:S(2)}) collective-permute-start(bf16[512,1024]{1,0:T(8,128)(2,1)S(1)} %bitcast.598), channel_id=1, source_target_pairs={{0,6},{1,7},{2,0},{3,1},{4,2},{5,3},{6,4},{7,5},{8,14},{9,15},{10,... | collective-permute-start | bytes 3145736 | tf_op jit(solution)/shard_map/ppermute | solution.py:41
  205.7 28.1 %collective-permute-start.47 = (bf16[2,128,2048]{2,1,0:T(8,128)(2,1)}, bf16[2,128,2048]{2,1,0:T(8,128)(2,1)}, u32[]{:S(2)}, u32[]{:S(2)}) collective-permute-start(bf16[2,128,2048]{2,1,0:T(8,128)(2,1)} %pad_maximum_fusion.15), channel_id=1, source_target_pairs={{0,16},{8,24},{16,0},{24,8},{1,17},{9,25},{17,1},{25,9},{2,18},{10... | collective-permute-start | bytes 3145736 | tf_op jit(solution)/shard_map/ppermute | solution.py:27
  233.8 34.6 %collective-permute-start.9 = (bf16[4,3,512,128]{3,2,1,0:T(8,128)(2,1)S(1)}, bf16[4,3,512,128]{3,2,1,0:T(8,128)(2,1)S(1)}, u32[]{:S(2)}, u32[]{:S(2)}) collective-permute-start(bf16[4,3,512,128]{3,2,1,0:T(8,128)(2,1)S(1)} %get-tuple-element.54), channel_id=1, source_target_pairs={{0,2},{1,3},{2,0},{3,1},{4,6},{5,7},{6,4},{7,5},{8,10},{9,11},{10,... | collective-permute-start | bytes 4718600 | tf_op jit(solution)/shard_map/ppermute | solution.py:36
  287.2 199.5 %collective-permute-start.48 = (bf16[1024,2048]{1,0:T(8,128)(2,1)}, bf16[1024,2048]{1,0:T(8,128)(2,1)}, u32[]{:S(2)}, u32[]{:S(2)}) collective-permute-start(bf16[1024,2048]{1,0:T(8,128)(2,1)} %get-tuple-element.106), channel_id=1, source_target_pairs={{0,8},{8,0},{16,24},{24,16},{1,9},{9,1},{17,25},{25,17},{2,10},{10... | collective-permute-start | bytes 12582920 | tf_op jit(solution)/shard_map/ppermute | solution.py:31
  287.3 103.1 %collective-permute-start.37 = (bf16[512,1024]{1,0:T(8,128)(2,1)}, bf16[512,1024]{1,0:T(8,128)(2,1)}, u32[]{:S(2)}, u32[]{:S(2)}) collective-permute-start(bf16[512,1024]{1,0:T(8,128)(2,1)} %copy-done.62), channel_id=1, source_target_pairs={{0,6},{1,7},{2,0},{3,1},{4,2},{5,3},{6,4},{7,5},{8,14},{9,15},{10,... | collective-permute-start | bytes 3145736 | tf_op jit(solution)/shard_map/ppermute | solution.py:41
  287.4 108.2 %collective-permute-start.33 = (bf16[512,1024]{1,0:T(8,128)(2,1)}, bf16[512,1024]{1,0:T(8,128)(2,1)}, u32[]{:S(2)}, u32[]{:S(2)}) collective-permute-start(bf16[512,1024]{1,0:T(8,128)(2,1)} %collective-permute-done.32), channel_id=1, source_target_pairs={{0,6},{1,7},{2,0},{3,1},{4,2},{5,3},{6,4},{7,5},{8,14},{9,15},{10,... | collective-permute-start | bytes 3145736 | tf_op jit(solution)/shard_map/ppermute | solution.py:41
  292.1 111.4 %collective-permute-start.29 = (bf16[512,1024]{1,0:T(8,128)(2,1)}, bf16[512,1024]{1,0:T(8,128)(2,1)}, u32[]{:S(2)}, u32[]{:S(2)}) collective-permute-start(bf16[512,1024]{1,0:T(8,128)(2,1)} %collective-permute-done.28), channel_id=1, source_target_pairs={{0,6},{1,7},{2,0},{3,1},{4,2},{5,3},{6,4},{7,5},{8,14},{9,15},{10,... | collective-permute-start | bytes 3145736 | tf_op jit(solution)/shard_map/ppermute | solution.py:41
  315.8 82.8 %collective-permute-start.14 = (bf16[4,1,512,128]{3,2,0,1:T(8,128)(2,1)S(1)}, bf16[4,1,512,128]{3,2,0,1:T(8,128)(2,1)S(1)}, u32[]{:S(2)}, u32[]{:S(2)}) collective-permute-start(bf16[4,1,512,128]{3,2,0,1:T(8,128)(2,1)S(1)} %get-tuple-element.143), channel_id=1, source_target_pairs={{0,2},{1,3},{2,0},{3,1},{4,6},{5,7},{6,4},{7,5},{8,10},{9,11},{10,... | collective-permute-start | bytes 1572872 | tf_op jit(solution)/shard_map/ppermute | solution.py:36
  390.4 30.1 %collective-permute-start.38 = (bf16[512,1024]{1,0:T(8,128)(2,1)}, bf16[512,1024]{1,0:T(8,128)(2,1)}, u32[]{:S(2)}, u32[]{:S(2)}) collective-permute-start(bf16[512,1024]{1,0:T(8,128)(2,1)} %collective-permute-done.37), channel_id=1, source_target_pairs={{0,6},{1,7},{2,0},{3,1},{4,2},{5,3},{6,4},{7,5},{8,14},{9,15},{10,... | collective-permute-start | bytes 3145736 | tf_op jit(solution)/shard_map/ppermute | solution.py:41
  427.2 48.3 %collective-permute-start.34 = (bf16[512,1024]{1,0:T(8,128)(2,1)}, bf16[512,1024]{1,0:T(8,128)(2,1)S(1)}, u32[]{:S(2)}, u32[]{:S(2)}) collective-permute-start(bf16[512,1024]{1,0:T(8,128)(2,1)} %collective-permute-done.33), channel_id=1, source_target_pairs={{0,6},{1,7},{2,0},{3,1},{4,2},{5,3},{6,4},{7,5},{8,14},{9,15},{10,... | collective-permute-start | bytes 3145736 | tf_op jit(solution)/shard_map/ppermute | solution.py:41
  439.8 44.5 %collective-permute-start.30 = (bf16[512,1024]{1,0:T(8,128)(2,1)}, bf16[512,1024]{1,0:T(8,128)(2,1)}, u32[]{:S(2)}, u32[]{:S(2)}) collective-permute-start(bf16[512,1024]{1,0:T(8,128)(2,1)} %collective-permute-done.29), channel_id=1, source_target_pairs={{0,6},{1,7},{2,0},{3,1},{4,2},{5,3},{6,4},{7,5},{8,14},{9,15},{10,... | collective-permute-start | bytes 3145736 | tf_op jit(solution)/shard_map/ppermute | solution.py:41
  492.0 31.0 %collective-permute-start.24 = (bf16[2,128,2048]{2,1,0:T(8,128)(2,1)S(1)}, bf16[2,128,2048]{2,1,0:T(8,128)(2,1)S(1)}, u32[]{:S(2)}, u32[]{:S(2)}) collective-permute-start(bf16[2,128,2048]{2,1,0:T(8,128)(2,1)S(1)} %pad_maximum_fusion.11), channel_id=1, source_target_pairs={{0,1},{1,0},{2,3},{3,2},{4,5},{5,4},{6,7},{7,6},{8,9},{9,8},{10,11... | collective-permute-start | bytes 3145736 | tf_op jit(solution)/shard_map/ppermute | solution.py:23
  502.1 31.7 %collective-permute-start.78 = (bf16[128,2048]{1,0:T(8,128)(2,1)S(1)}, bf16[128,2048]{1,0:T(8,128)(2,1)S(1)}, u32[]{:S(2)}, u32[]{:S(2)}) collective-permute-start(bf16[128,2048]{1,0:T(8,128)(2,1)S(1)} %get-tuple-element.93), channel_id=1, source_target_pairs={{0,1},{1,0},{2,3},{3,2},{4,5},{5,4},{6,7},{7,6},{8,9},{9,8},{10,11... | collective-permute-start | bytes 1572872 | tf_op jit(solution)/shard_map/ppermute | solution.py:23
  503.4 28.9 %collective-permute-start.79 = (bf16[128,2048]{1,0:T(8,128)(2,1)S(1)}, bf16[128,2048]{1,0:T(8,128)(2,1)S(1)}, u32[]{:S(2)}, u32[]{:S(2)}) collective-permute-start(bf16[128,2048]{1,0:T(8,128)(2,1)S(1)} %get-tuple-element.92), channel_id=1, source_target_pairs={{0,16},{8,24},{16,0},{24,8},{1,17},{9,25},{17,1},{25,9},{2,18},{10... | collective-permute-start | bytes 1572872 | tf_op jit(solution)/shard_map/ppermute | solution.py:27
  527.1 29.3 %collective-permute-start.26 = (bf16[1024,2048]{1,0:T(8,128)(2,1)S(1)}, bf16[1024,2048]{1,0:T(8,128)(2,1)S(1)}, u32[]{:S(2)}, u32[]{:S(2)}) collective-permute-start(bf16[1024,2048]{1,0:T(8,128)(2,1)S(1)} %get-tuple-element.120), channel_id=1, source_target_pairs={{0,8},{8,0},{16,24},{24,16},{1,9},{9,1},{17,25},{25,17},{2,10},{10... | collective-permute-start | bytes 12582920 | tf_op jit(solution)/shard_map/ppermute | solution.py:31
  651.5 189.3 %collective-permute-start.49 = (bf16[1024,2048]{1,0:T(8,128)(2,1)}, bf16[1024,2048]{1,0:T(8,128)(2,1)}, u32[]{:S(2)}, u32[]{:S(2)}) collective-permute-start(bf16[1024,2048]{1,0:T(8,128)(2,1)} %slice.447), channel_id=1, source_target_pairs={{0,8},{8,0},{16,24},{24,16},{1,9},{9,1},{17,25},{25,17},{2,10},{10... | collective-permute-start | bytes 12582920 | tf_op jit(solution)/shard_map/ppermute | solution.py:31
  651.6 27.8 %collective-permute-start.96 = (bf16[512,1024]{1,0:T(8,128)(2,1)S(1)}, bf16[512,1024]{1,0:T(8,128)(2,1)S(1)}, u32[]{:S(2)}, u32[]{:S(2)}) collective-permute-start(bf16[512,1024]{1,0:T(8,128)(2,1)S(1)} %constant_dynamic-slice_fusion.3), channel_id=1, source_target_pairs={{0,6},{1,7},{2,0},{3,1},{4,2},{5,3},{6,4},{7,5},{8,14},{9,15},{10,... | collective-permute-start | bytes 3145736 | tf_op jit(solution)/shard_map/ppermute | solution.py:41
  656.0 45.9 %collective-permute-start.99 = (bf16[512,1024]{1,0:T(8,128)(2,1)S(1)}, bf16[512,1024]{1,0:T(8,128)(2,1)S(1)}, u32[]{:S(2)}, u32[]{:S(2)}) collective-permute-start(bf16[512,1024]{1,0:T(8,128)(2,1)S(1)} %constant_dynamic-slice_fusion.2), channel_id=1, source_target_pairs={{0,6},{1,7},{2,0},{3,1},{4,2},{5,3},{6,4},{7,5},{8,14},{9,15},{10,... | collective-permute-start | bytes 3145736 | tf_op jit(solution)/shard_map/ppermute | solution.py:41
  669.2 55.2 %collective-permute-start.105 = (bf16[512,1024]{1,0:T(8,128)(2,1)S(1)}, bf16[512,1024]{1,0:T(8,128)(2,1)S(1)}, u32[]{:S(2)}, u32[]{:S(2)}) collective-permute-start(bf16[512,1024]{1,0:T(8,128)(2,1)S(1)} %constant_dynamic-slice_fusion.1), channel_id=1, source_target_pairs={{0,6},{1,7},{2,0},{3,1},{4,2},{5,3},{6,4},{7,5},{8,14},{9,15},{10,... | collective-permute-start | bytes 3145736 | tf_op jit(solution)/shard_map/ppermute | solution.py:41
  679.8 67.0 %collective-permute-start.97 = (bf16[512,1024]{1,0:T(8,128)(2,1)S(1)}, bf16[512,1024]{1,0:T(8,128)(2,1)}, u32[]{:S(2)}, u32[]{:S(2)}) collective-permute-start(bf16[512,1024]{1,0:T(8,128)(2,1)S(1)} %add_convert_fusion.9), channel_id=1, source_target_pairs={{0,6},{1,7},{2,0},{3,1},{4,2},{5,3},{6,4},{7,5},{8,14},{9,15},{10,... | collective-permute-start | bytes 3145736 | tf_op jit(solution)/shard_map/ppermute | solution.py:41
  703.3 66.1 %collective-permute-start.100 = (bf16[512,1024]{1,0:T(8,128)(2,1)}, bf16[512,1024]{1,0:T(8,128)(2,1)}, u32[]{:S(2)}, u32[]{:S(2)}) collective-permute-start(bf16[512,1024]{1,0:T(8,128)(2,1)} %add_convert_fusion.6), channel_id=1, source_target_pairs={{0,6},{1,7},{2,0},{3,1},{4,2},{5,3},{6,4},{7,5},{8,14},{9,15},{10,... | collective-permute-start | bytes 3145736 | tf_op jit(solution)/shard_map/ppermute | solution.py:41
  724.1 124.6 %collective-permute-start.39 = (bf16[1024,2048]{1,0:T(8,128)(2,1)}, bf16[1024,2048]{1,0:T(8,128)(2,1)}, u32[]{:S(2)}, u32[]{:S(2)}) collective-permute-start(bf16[1024,2048]{1,0:T(8,128)(2,1)} %slice.430), channel_id=1, source_target_pairs={{0,8},{8,0},{16,24},{24,16},{1,9},{9,1},{17,25},{25,17},{2,10},{10... | collective-permute-start | bytes 12582920 | tf_op jit(solution)/shard_map/ppermute | solution.py:31
  724.8 67.0 %collective-permute-start.106 = (bf16[512,1024]{1,0:T(8,128)(2,1)S(1)}, bf16[512,1024]{1,0:T(8,128)(2,1)S(1)}, u32[]{:S(2)}, u32[]{:S(2)}) collective-permute-start(bf16[512,1024]{1,0:T(8,128)(2,1)S(1)} %add_convert_fusion.3), channel_id=1, source_target_pairs={{0,6},{1,7},{2,0},{3,1},{4,2},{5,3},{6,4},{7,5},{8,14},{9,15},{10,... | collective-permute-start | bytes 3145736 | tf_op jit(solution)/shard_map/ppermute | solution.py:41
  748.5 65.8 %collective-permute-start.98 = (bf16[512,1024]{1,0:T(8,128)(2,1)S(1)}, bf16[512,1024]{1,0:T(8,128)(2,1)S(1)}, u32[]{:S(2)}, u32[]{:S(2)}) collective-permute-start(bf16[512,1024]{1,0:T(8,128)(2,1)S(1)} %add_convert_fusion.8), channel_id=1, source_target_pairs={{0,6},{1,7},{2,0},{3,1},{4,2},{5,3},{6,4},{7,5},{8,14},{9,15},{10,... | collective-permute-start | bytes 3145736 | tf_op jit(solution)/shard_map/ppermute | solution.py:41
  771.0 65.7 %collective-permute-start.101 = (bf16[512,1024]{1,0:T(8,128)(2,1)S(1)}, bf16[512,1024]{1,0:T(8,128)(2,1)S(1)}, u32[]{:S(2)}, u32[]{:S(2)}) collective-permute-start(bf16[512,1024]{1,0:T(8,128)(2,1)S(1)} %add_convert_fusion.5), channel_id=1, source_target_pairs={{0,6},{1,7},{2,0},{3,1},{4,2},{5,3},{6,4},{7,5},{8,14},{9,15},{10,... | collective-permute-start | bytes 3145736 | tf_op jit(solution)/shard_map/ppermute | solution.py:41
  793.2 158.9 %collective-permute-start.107 = (bf16[512,1024]{1,0:T(8,128)(2,1)}, bf16[512,1024]{1,0:T(8,128)(2,1)}, u32[]{:S(2)}, u32[]{:S(2)}) collective-permute-start(bf16[512,1024]{1,0:T(8,128)(2,1)} %add_convert_fusion.2), channel_id=1, source_target_pairs={{0,6},{1,7},{2,0},{3,1},{4,2},{5,3},{6,4},{7,5},{8,14},{9,15},{10,... | collective-permute-start | bytes 3145736 | tf_op jit(solution)/shard_map/ppermute | solution.py:41
  839.5 148.7 %collective-permute-start.102 = (bf16[256,2048]{1,0:T(8,128)(2,1)}, bf16[256,2048]{1,0:T(8,128)(2,1)}, u32[]{:S(2)}, u32[]{:S(2)}) collective-permute-start(bf16[256,2048]{1,0:T(8,128)(2,1)} %get-tuple-element.64), channel_id=1, source_target_pairs={{0,1},{1,0},{2,3},{3,2},{4,5},{5,4},{6,7},{7,6},{8,9},{9,8},{10,11... | collective-permute-start | bytes 3145736 | tf_op jit(solution)/shard_map/ppermute | solution.py:23
  847.9 45.7 %collective-permute-start.52 = (bf16[2,128,2048]{2,1,0:T(8,128)(2,1)S(1)}, bf16[2,128,2048]{2,1,0:T(8,128)(2,1)S(1)}, u32[]{:S(2)}, u32[]{:S(2)}) collective-permute-start(bf16[2,128,2048]{2,1,0:T(8,128)(2,1)S(1)} %pad_maximum_fusion.16), channel_id=1, source_target_pairs={{0,1},{1,0},{2,3},{3,2},{4,5},{5,4},{6,7},{7,6},{8,9},{9,8},{10,11... | collective-permute-start | bytes 3145736 | tf_op jit(solution)/shard_map/ppermute | solution.py:23
  854.3 38.5 %collective-permute-start.40 = (bf16[2,128,2048]{2,1,0:T(8,128)(2,1)S(1)}, bf16[2,128,2048]{2,1,0:T(8,128)(2,1)S(1)}, u32[]{:S(2)}, u32[]{:S(2)}) collective-permute-start(bf16[2,128,2048]{2,1,0:T(8,128)(2,1)S(1)} %slice_bitcast_fusion.16), channel_id=1, source_target_pairs={{0,16},{8,24},{16,0},{24,8},{1,17},{9,25},{17,1},{25,9},{2,18},{10... | collective-permute-start | bytes 3145736 | tf_op jit(solution)/shard_map/ppermute | solution.py:27
  872.4 27.2 %collective-permute-start.51 = (bf16[128,2048]{1,0:T(8,128)(2,1)S(1)}, bf16[128,2048]{1,0:T(8,128)(2,1)S(1)}, u32[]{:S(2)}, u32[]{:S(2)}) collective-permute-start(bf16[128,2048]{1,0:T(8,128)(2,1)S(1)} %fusion.68), channel_id=1, source_target_pairs={{0,1},{1,0},{2,3},{3,2},{4,5},{5,4},{6,7},{7,6},{8,9},{9,8},{10,11... | collective-permute-start | bytes 1572872 | tf_op jit(solution)/shard_map/ppermute | solution.py:23
  892.7 29.3 %collective-permute-start.42 = (bf16[2,128,2048]{2,1,0:T(8,128)(2,1)S(1)}, bf16[2,128,2048]{2,1,0:T(8,128)(2,1)S(1)}, u32[]{:S(2)}, u32[]{:S(2)}) collective-permute-start(bf16[2,128,2048]{2,1,0:T(8,128)(2,1)S(1)} %pad_maximum_fusion.13), channel_id=1, source_target_pairs={{0,1},{1,0},{2,3},{3,2},{4,5},{5,4},{6,7},{7,6},{8,9},{9,8},{10,11... | collective-permute-start | bytes 3145736 | tf_op jit(solution)/shard_map/ppermute | solution.py:23
  893.6 37.9 %collective-permute-start.41 = (bf16[128,2048]{1,0:T(8,128)(2,1)S(1)}, bf16[128,2048]{1,0:T(8,128)(2,1)S(1)}, u32[]{:S(2)}, u32[]{:S(2)}) collective-permute-start(bf16[128,2048]{1,0:T(8,128)(2,1)S(1)} %fusion.76), channel_id=1, source_target_pairs={{0,1},{1,0},{2,3},{3,2},{4,5},{5,4},{6,7},{7,6},{8,9},{9,8},{10,11... | collective-permute-start | bytes 1572872 | tf_op jit(solution)/shard_map/ppermute | solution.py:23
  900.0 33.9 %collective-permute-start.53 = (bf16[128,2048]{1,0:T(8,128)(2,1)S(1)}, bf16[128,2048]{1,0:T(8,128)(2,1)S(1)}, u32[]{:S(2)}, u32[]{:S(2)}) collective-permute-start(bf16[128,2048]{1,0:T(8,128)(2,1)S(1)} %get-tuple-element.32), channel_id=1, source_target_pairs={{0,16},{8,24},{16,0},{24,8},{1,17},{9,25},{17,1},{25,9},{2,18},{10... | collective-permute-start | bytes 1572872 | tf_op jit(solution)/shard_map/ppermute | solution.py:27
  956.7 29.3 %collective-permute-start.108 = (bf16[256,1024]{1,0:T(8,128)(2,1)}, bf16[256,1024]{1,0:T(8,128)(2,1)S(1)}, u32[]{:S(2)}, u32[]{:S(2)}) collective-permute-start(bf16[256,1024]{1,0:T(8,128)(2,1)} %get-tuple-element.71), channel_id=1, source_target_pairs={{0,1},{1,0},{2,3},{3,2},{4,5},{5,4},{6,7},{7,6},{8,9},{9,8},{10,11... | collective-permute-start | bytes 1572872 | tf_op jit(solution)/shard_map/ppermute | solution.py:23
  986.0 69.5 %collective-permute-start.82 = (bf16[1024,2048]{1,0:T(8,128)(2,1)}, bf16[1024,2048]{1,0:T(8,128)(2,1)}, u32[]{:S(2)}, u32[]{:S(2)}) collective-permute-start(bf16[1024,2048]{1,0:T(8,128)(2,1)} %get-tuple-element.80), channel_id=1, source_target_pairs={{0,8},{8,0},{16,24},{24,16},{1,9},{9,1},{17,25},{25,17},{2,10},{10... | collective-permute-start | bytes 12582920 | tf_op jit(solution)/shard_map/ppermute | solution.py:31
  987.1 73.8 %collective-permute-start.109 = (bf16[2,256,1024]{2,1,0:T(8,128)(2,1)}, bf16[2,256,1024]{2,1,0:T(8,128)(2,1)}, u32[]{:S(2)}, u32[]{:S(2)}) collective-permute-start(bf16[2,256,1024]{2,1,0:T(8,128)(2,1)} %pad_maximum_fusion.20), channel_id=1, source_target_pairs={{0,16},{8,24},{16,0},{24,8},{1,17},{9,25},{17,1},{25,9},{2,18},{10... | collective-permute-start | bytes 3145736 | tf_op jit(solution)/shard_map/ppermute | solution.py:27
  991.0 76.1 %collective-permute-start.103 = (bf16[2,256,2048]{2,1,0:T(8,128)(2,1)}, bf16[2,256,2048]{2,1,0:T(8,128)(2,1)}, u32[]{:S(2)}, u32[]{:S(2)}) collective-permute-start(bf16[2,256,2048]{2,1,0:T(8,128)(2,1)} %pad_maximum_fusion.6), channel_id=1, source_target_pairs={{0,16},{8,24},{16,0},{24,8},{1,17},{9,25},{17,1},{25,9},{2,18},{10... | collective-permute-start | bytes 6291464 | tf_op jit(solution)/shard_map/ppermute | solution.py:27
  1055.4 35.4 %collective-permute-start.63 = (bf16[4,3,512,128]{3,2,1,0:T(8,128)(2,1)S(1)}, bf16[4,3,512,128]{3,2,1,0:T(8,128)(2,1)S(1)}, u32[]{:S(2)}, u32[]{:S(2)}) collective-permute-start(bf16[4,3,512,128]{3,2,1,0:T(8,128)(2,1)S(1)} %bitcast.618), channel_id=1, source_target_pairs={{0,2},{1,3},{2,0},{3,1},{4,6},{5,7},{6,4},{7,5},{8,10},{9,11},{10,... | collective-permute-start | bytes 4718600 | tf_op jit(solution)/shard_map/ppermute | solution.py:36
  1063.3 93.0 %collective-permute-start.110 = (bf16[4,256,1024]{2,1,0:T(8,128)(2,1)S(1)}, bf16[4,256,1024]{2,1,0:T(8,128)(2,1)}, u32[]{:S(2)}, u32[]{:S(2)}) collective-permute-start(bf16[4,256,1024]{2,1,0:T(8,128)(2,1)S(1)} %pad_maximum_fusion.7.a_ref), channel_id=1, source_target_pairs={{0,8},{8,0},{16,24},{24,16},{1,9},{9,1},{17,25},{25,17},{2,10},{10... | collective-permute-start | bytes 6291464 | tf_op jit(solution)/shard_map/ppermute | solution.py:31
  1077.7 255.9 %collective-permute-start.104 = (bf16[4,256,2048]{2,1,0:T(8,128)(2,1)}, bf16[4,256,2048]{2,1,0:T(8,128)(2,1)}, u32[]{:S(2)}, u32[]{:S(2)}) collective-permute-start(bf16[4,256,2048]{2,1,0:T(8,128)(2,1)} %pad_maximum_fusion.a_ref), channel_id=1, source_target_pairs={{0,8},{8,0},{16,24},{24,16},{1,9},{9,1},{17,25},{25,17},{2,10},{10... | collective-permute-start | bytes 12582920 | tf_op jit(solution)/shard_map/ppermute | solution.py:31
  1115.3 82.5 %collective-permute-start.64 = (bf16[1024,2048]{1,0:T(8,128)(2,1)S(1)}, bf16[1024,2048]{1,0:T(8,128)(2,1)S(1)}, u32[]{:S(2)}, u32[]{:S(2)}) collective-permute-start(bf16[1024,2048]{1,0:T(8,128)(2,1)S(1)} %slice.466), channel_id=1, source_target_pairs={{0,8},{8,0},{16,24},{24,16},{1,9},{9,1},{17,25},{25,17},{2,10},{10... | collective-permute-start | bytes 12582920 | tf_op jit(solution)/shard_map/ppermute | solution.py:31
  1147.1 29.7 %collective-permute-start.73 = (bf16[512,768]{1,0:T(8,128)(2,1)S(1)}, bf16[512,768]{1,0:T(8,128)(2,1)S(1)}, u32[]{:S(2)}, u32[]{:S(2)}) collective-permute-start(bf16[512,768]{1,0:T(8,128)(2,1)S(1)} %add_convert_fusion.14), channel_id=1, source_target_pairs={{0,6},{1,7},{2,0},{3,1},{4,2},{5,3},{6,4},{7,5},{8,14},{9,15},{10,... | collective-permute-start | bytes 2359304 | tf_op jit(solution)/shard_map/ppermute | solution.py:41
  1177.5 28.4 %collective-permute-start.70 = (bf16[2,129,128]{2,1,0:T(8,128)(2,1)S(1)}, bf16[2,129,128]{2,1,0:T(8,128)(2,1)S(1)}, u32[]{:S(2)}, u32[]{:S(2)}) collective-permute-start(bf16[2,129,128]{2,1,0:T(8,128)(2,1)S(1)} %bitcast.651), channel_id=1, source_target_pairs={{0,16},{8,24},{16,0},{24,8},{1,17},{9,25},{17,1},{25,9},{2,18},{10... | collective-permute-start | bytes 198152 | tf_op jit(solution)/shard_map/ppermute | solution.py:461
  1183.6 68.0 %collective-permute-start.71 = (bf16[2,129,128]{2,1,0:T(8,128)(2,1)S(1)}, bf16[2,129,128]{2,1,0:T(8,128)(2,1)S(1)}, u32[]{:S(2)}, u32[]{:S(2)}) collective-permute-start(bf16[2,129,128]{2,1,0:T(8,128)(2,1)S(1)} %bitcast.650), channel_id=1, source_target_pairs={{0,24},{8,16},{16,8},{24,0},{1,25},{9,17},{17,9},{25,1},{2,26},{10... | collective-permute-start | bytes 198152 | tf_op jit(solution)/shard_map/ppermute | solution.py:461
  1207.5 45.2 %collective-permute-start.94 = (bf16[2,256,256]{2,1,0:T(8,128)(2,1)S(1)}, bf16[2,256,256]{2,1,0:T(8,128)(2,1)S(1)}, u32[]{:S(2)}, u32[]{:S(2)}) collective-permute-start(bf16[2,256,256]{2,1,0:T(8,128)(2,1)S(1)} %pad_maximum_fusion.27), channel_id=1, source_target_pairs={{0,16},{8,24},{16,0},{24,8},{1,17},{9,25},{17,1},{25,9},{2,18},{10... | collective-permute-start | bytes 786440 | tf_op jit(solution)/shard_map/ppermute | solution.py:27
  1209.4 40.7 %collective-permute-start.76 = (bf16[2,256,768]{2,1,0:T(8,128)(2,1)S(1)}, bf16[2,256,768]{2,1,0:T(8,128)(2,1)S(1)}, u32[]{:S(2)}, u32[]{:S(2)}) collective-permute-start(bf16[2,256,768]{2,1,0:T(8,128)(2,1)S(1)} %pad_maximum_fusion.21), channel_id=1, source_target_pairs={{0,16},{8,24},{16,0},{24,8},{1,17},{9,25},{17,1},{25,9},{2,18},{10... | collective-permute-start | bytes 2359304 | tf_op jit(solution)/shard_map/ppermute | solution.py:27
  1251.6 99.9 %collective-permute-start.77 = (bf16[4,256,768]{2,1,0:T(8,128)(2,1)S(1)}, bf16[4,256,768]{2,1,0:T(8,128)(2,1)}, u32[]{:S(2)}, u32[]{:S(2)}) collective-permute-start(bf16[4,256,768]{2,1,0:T(8,128)(2,1)S(1)} %pad_maximum_fusion.8.a_ref), channel_id=1, source_target_pairs={{0,8},{8,0},{16,24},{24,16},{1,9},{9,1},{17,25},{25,17},{2,10},{10... | collective-permute-start | bytes 4718600 | tf_op jit(solution)/shard_map/ppermute | solution.py:31
  1252.7 77.3 %collective-permute-start.95 = (bf16[4,256,256]{2,1,0:T(8,128)(2,1)S(1)}, bf16[4,256,256]{2,1,0:T(8,128)(2,1)S(1)}, u32[]{:S(2)}, u32[]{:S(2)}) collective-permute-start(bf16[4,256,256]{2,1,0:T(8,128)(2,1)S(1)} %pad_maximum_fusion.24.a_ref), channel_id=1, source_target_pairs={{0,8},{8,0},{16,24},{24,16},{1,9},{9,1},{17,25},{25,17},{2,10},{10... | collective-permute-start | bytes 1572872 | tf_op jit(solution)/shard_map/ppermute | solution.py:31
  1263.6 102.7 %collective-permute-start.68 = (bf16[128,2048]{1,0:T(8,128)(2,1)}, bf16[128,2048]{1,0:T(8,128)(2,1)}, u32[]{:S(2)}, u32[]{:S(2)}) collective-permute-start(bf16[128,2048]{1,0:T(8,128)(2,1)} %get-tuple-element.30), channel_id=1, source_target_pairs={{0,16},{8,24},{16,0},{24,8},{1,17},{9,25},{17,1},{25,9},{2,18},{10... | collective-permute-start | bytes 1572872 | tf_op jit(solution)/shard_map/ppermute | solution.py:27
  (164 other events, 3930.7 us)
Sparse Core Ops, SparseCore 0:
  43.7 99.0 all-gather.2
  1252.8 73.6 all-reduce.1

commit v2 on v1

v2 whole, which is shorter than its diff:
```python
import functools

import jax
import jax.numpy as jnp
from jax import lax
from jax.experimental import pallas as pl
from jax.experimental.pallas import tpu as pltpu
from jax.sharding import PartitionSpec as P

D = 2048
H = 16
DK = 128
FF = 8192
SEG = 1024
EPSILON = 1e-06
F32 = jnp.float32
BF16 = jnp.bfloat16
GROUP = 8


def swap_x(v):
    n = lax.axis_size("wide")
    return lax.ppermute(v, "wide", [(i, i ^ 1) for i in range(n)])


def swap_y(v):
    return lax.ppermute(v, "narrow", [(i, i ^ 2) for i in range(4)])


def swap_core(v):
    return lax.ppermute(v, "narrow", [(i, i ^ 1) for i in range(4)])


def swap_z(v, d):
    n = lax.axis_size("wide")
    return lax.ppermute(v, "wide", [(i, i ^ (2 * d)) for i in range(n)])


def offset_bits(r):
    return (r >> 1) & 1, (r >> 2) & 1, r & 1


def absolute(r):
    y, core, x = offset_bits(r)
    return y * 4 + core * 2 + x


def send_offset(v, r):
    y, core, x = offset_bits(r)
    n = lax.axis_size("wide")
    flip = y * 2 + core
    route = [(a * n + b, (a ^ flip) * n + (b ^ x)) for a in range(4) for b in range(n)]
    return lax.ppermute(v, ("narrow", "wide"), route)


def plane(v):
    return [v] + [send_offset(v, r) for r in range(1, 4)]


def both_cores(pieces):
    return pieces + [swap_core(p) for p in pieces]


def scatter_start(partial):
    rows = partial.shape[0] // GROUP
    parts = [partial[r * rows : (r + 1) * rows] for r in range(GROUP)]
    sums = [None] * 4
    for r in (3, 1, 2, 0):
        sums[r] = parts[r].astype(F32) + swap_core(parts[4 + r]).astype(F32)
    return [sums[0]] + [v.astype(BF16) for v in sums[1:]]


def scatter_sends(sums):
    return [sums[0]] + [send_offset(sums[r], r) for r in range(1, 4)]


def scatter_total(got):
    return got[0] + got[1].astype(F32) + got[2].astype(F32) + got[3].astype(F32)


def join_kernel(*refs):
    out = refs[-1]
    rows = refs[0].shape[0]
    for i, piece in enumerate(refs[:-1]):
        out[i * rows : (i + 1) * rows] = piece[...]


def join(pieces):
    rows, columns = pieces[0].shape
    step = min(columns, 512)
    return pl.pallas_call(
        join_kernel,
        grid=(columns // step,),
        in_specs=[pl.BlockSpec((rows, step), lambda j: (0, j))] * len(pieces),
        out_specs=pl.BlockSpec((len(pieces) * rows, step), lambda j: (0, j)),
        out_shape=jax.ShapeDtypeStruct((len(pieces) * rows, columns), pieces[0].dtype),
        compiler_params=pltpu.CompilerParams(vmem_limit_bytes=24 * 2**20),
    )(*pieces)


def exchange_group(blocks):
    return [blocks[0]] + [send_offset(blocks[r], r) for r in range(1, GROUP)]


def by_bit(pair, bit):
    a, b = pair
    return jnp.where(bit == 0, jnp.stack([a, b]), jnp.stack([b, a]))


def by_index(parts, index):
    if len(parts) == 2:
        return by_bit(parts, index)
    out = jnp.zeros((len(parts),) + parts[0].shape, parts[0].dtype)
    for d, part in enumerate(parts):
        out = lax.dynamic_update_slice_in_dim(out, part[None], index ^ d, 0)
    return out


def after(v, *others):
    return lax.optimization_barrier((v, others))[0]


def z_lines():
    n = lax.axis_size("wide")
    return [list(range(x, n, 2)) for x in range(2)]


def eighth_block(parts, x, n):
    c = n * 2 + x

    def columns(eighth):
        return jnp.concatenate(
            [lax.dynamic_slice_in_dim(a, s + eighth * m, m, 1) for a, s, m in parts], axis=1
        )

    give = columns(c ^ 1)
    pair = by_bit([columns(c), swap_x(give)], x)
    return pair.reshape(pair.shape[0] * pair.shape[1], -1), give


def gather_rows(block):
    return lax.all_gather(block, "wide", axis=0, tiled=True, axis_index_groups=z_lines())


def reduce_rows(partial):
    return lax.psum_scatter(
        partial, "wide", scatter_dimension=0, tiled=True, axis_index_groups=z_lines()
    )


def gather_gains(v, w):
    n = lax.axis_size("wide")
    blocks = [v]
    for d in range(1, n):
        blocks.append(lax.ppermute(v, "wide", [(i, i ^ d) for i in range(n)]))
    return by_index(blocks, w).transpose(1, 0, 2).reshape(2, -1)


def sum_z(v):
    d = 1
    while d < lax.axis_size("wide") // 2:
        v = (v.astype(F32) + swap_z(v, d).astype(F32)).astype(v.dtype)
        d *= 2
    return v


def sum_all(v):
    v = v + swap_core(v)
    v = v + swap_y(v)
    v = v + swap_x(v)
    return sum_z(v)


def spread_x(summed, x):
    rows = summed.shape[0] // 2
    keep = lax.dynamic_slice_in_dim(summed, x * rows, rows, 0)
    give = lax.dynamic_slice_in_dim(summed, (1 - x) * rows, rows, 0)
    return [keep, swap_x(give)]


def spread_y(pair):
    return pair + [swap_y(p) for p in pair]


def assemble_kernel(width, place, *refs):
    out = refs[GROUP]
    for r in range(GROUP):
        column = pl.multiple_of(place[r] * width, width)
        out[:, pl.ds(column, width)] = refs[r][...].astype(out.dtype)


def assemble(pieces, c, parts, dtype):
    rows = pieces[0].shape[0]
    width = pieces[0].shape[1] // parts
    r = jnp.arange(GROUP, dtype=jnp.int32)
    place = c ^ (((r >> 1) & 1) * 4 + ((r >> 2) & 1) * 2 + (r & 1))
    step = min(rows, (64 * 1024) // width)
    return pl.pallas_call(
        functools.partial(assemble_kernel, width),
        grid_spec=pltpu.PrefetchScalarGridSpec(
            num_scalar_prefetch=1,
            grid=(parts, rows // step),
            in_specs=[pl.BlockSpec((step, width), lambda p, i, o: (i, p))] * GROUP,
            out_specs=pl.BlockSpec((step, GROUP * width), lambda p, i, o: (i, p)),
        ),
        out_shape=jax.ShapeDtypeStruct((rows, parts * GROUP * width), dtype),
        compiler_params=pltpu.CompilerParams(vmem_limit_bytes=24 * 2**20),
    )(place, *pieces)


def assemble_stacked(stacked, c, dtype):
    rows, width = stacked.shape[0] // GROUP, stacked.shape[1]
    r = jnp.arange(GROUP, dtype=jnp.int32)
    place = c ^ (((r >> 1) & 1) * 4 + ((r >> 2) & 1) * 2 + (r & 1))
    return pl.pallas_call(
        functools.partial(assemble_kernel, width),
        grid_spec=pltpu.PrefetchScalarGridSpec(
            num_scalar_prefetch=1,
            grid=(1,),
            in_specs=[
                pl.BlockSpec((rows, width), lambda i, o, r=r: (r, 0)) for r in range(GROUP)
            ],
            out_specs=pl.BlockSpec((rows, GROUP * width), lambda i, o: (0, 0)),
        ),
        out_shape=jax.ShapeDtypeStruct((rows, GROUP * width), dtype),
        compiler_params=pltpu.CompilerParams(vmem_limit_bytes=24 * 2**20),
    )(place, *[stacked] * GROUP)


ROWS = 256


def masked_probs(queries, keys, first, scale):
    scores = lax.dot_general(
        queries, keys, (((1,), (1,)), ((), ())), preferred_element_type=F32
    ) * scale
    row = lax.broadcasted_iota(jnp.int32, scores.shape, 0) + first
    col = lax.broadcasted_iota(jnp.int32, scores.shape, 1)
    scores = jnp.where(col <= row, scores, -1e30)
    raised = jnp.exp(scores - jnp.max(scores, axis=-1, keepdims=True))
    return raised / jnp.sum(raised, axis=-1, keepdims=True)


def attention_kernel(scale, qkv_ref, out_ref):
    for first in range(0, SEG, ROWS):
        end = first + ROWS
        probs = masked_probs(qkv_ref[0, 0, first:end], qkv_ref[0, 1, :end], first, scale)
        out_ref[0, first:end] = jnp.dot(
            probs.astype(BF16), qkv_ref[0, 2, :end], preferred_element_type=F32
        )


def attention(qkv, scale):
    units = qkv.shape[0]
    return pl.pallas_call(
        functools.partial(attention_kernel, scale),
        grid=(units,),
        in_specs=[pl.BlockSpec((1, 3, SEG, DK), lambda u: (u, 0, 0, 0))],
        out_specs=pl.BlockSpec((1, SEG, DK), lambda u: (u, 0, 0)),
        out_shape=jax.ShapeDtypeStruct((units, SEG, DK), F32),
        compiler_params=pltpu.CompilerParams(vmem_limit_bytes=40 * 2**20),
        cost_estimate=pl.CostEstimate(
            flops=units * 4 * SEG * SEG * DK, bytes_accessed=units * SEG * DK * 10,
            transcendentals=units * SEG * SEG,
        ),
    )(qkv)


def attention_back_kernel(scale, qkv_ref, grad_ref, out_ref):
    out_ref[0, 1] = jnp.zeros((SEG, DK), F32)
    out_ref[0, 2] = jnp.zeros((SEG, DK), F32)
    for first in range(0, SEG, ROWS):
        end = first + ROWS
        queries, keys, values = qkv_ref[0, 0, first:end], qkv_ref[0, 1, :end], qkv_ref[0, 2, :end]
        grad = grad_ref[0, first:end]
        probs = masked_probs(queries, keys, first, scale)
        grad_probs = lax.dot_general(
            grad, values, (((1,), (1,)), ((), ())), preferred_element_type=F32
        )
        inner = jnp.sum(probs * grad_probs, axis=-1, keepdims=True)
        grad_scores = (probs * (grad_probs - inner)).astype(BF16)
        out_ref[0, 0, first:end] = jnp.dot(
            grad_scores, keys, preferred_element_type=F32
        ) * scale
        out_ref[0, 1, :end] += lax.dot_general(
            grad_scores, queries, (((0,), (0,)), ((), ())), preferred_element_type=F32
        )
        out_ref[0, 2, :end] += lax.dot_general(
            probs.astype(BF16), grad, (((0,), (0,)), ((), ())), preferred_element_type=F32
        )
    out_ref[0, 1] = out_ref[0, 1] * scale


def attention_back(qkv, grad, scale):
    units = qkv.shape[0]
    return pl.pallas_call(
        functools.partial(attention_back_kernel, scale),
        grid=(units,),
        in_specs=[
            pl.BlockSpec((1, 3, SEG, DK), lambda u: (u, 0, 0, 0)),
            pl.BlockSpec((1, SEG, DK), lambda u: (u, 0, 0)),
        ],
        out_specs=pl.BlockSpec((1, 3, SEG, DK), lambda u: (u, 0, 0, 0)),
        out_shape=jax.ShapeDtypeStruct((units, 3, SEG, DK), F32),
        compiler_params=pltpu.CompilerParams(vmem_limit_bytes=48 * 2**20),
        cost_estimate=pl.CostEstimate(
            flops=units * 10 * SEG * SEG * DK, bytes_accessed=units * SEG * DK * 20,
            transcendentals=units * SEG * SEG,
        ),
    )(qkv, grad)


def dot(a, b):
    return jnp.dot(a, b, preferred_element_type=F32)


def dot_t(a, b):
    return lax.dot_general(a, b, (((1,), (1,)), ((), ())), preferred_element_type=F32)


def t_dot(a, b):
    return lax.dot_general(a, b, (((0,), (0,)), ((), ())), preferred_element_type=F32)


def norm_back(grad_unit, unit_rows, scale_rows):
    return scale_rows * (
        grad_unit - unit_rows * jnp.mean(grad_unit * unit_rows, axis=-1, keepdims=True)
    )


def elu_slope(inputs):
    return jnp.where(inputs > 0, 1.0, jnp.exp(jnp.minimum(inputs, 0.0)))


def body(
    tokens,
    cotangent,
    qkv_weight,
    out_weight,
    gain_attn,
    gate_up_weight,
    down_weight,
    gain_mlp,
    gate_logit,
    memory_in,
    normalizer_in,
):
    wide = lax.axis_size("wide")
    n = lax.axis_index("narrow")
    w = lax.axis_index("wide")
    z, x = w // 2, w % 2
    c = n * 2 + x
    rows_here = tokens.shape[1]
    shard = qkv_weight.shape[0]
    span = SEG // rows_here
    zspan = span // 2
    zi = z % zspan
    segments = wide // span
    units = GROUP // zspan
    head_cols = D // GROUP
    ff_cols = FF // GROUP
    scale = DK ** (-0.5)

    first, _ = eighth_block(
        [(qkv_weight, 0, head_cols), (qkv_weight, D, head_cols), (qkv_weight, 2 * D, head_cols),
         (out_weight, 0, head_cols)], x, n
    )
    first_c = gather_rows(first)
    qkv_c = first_c[:, : 3 * head_cols]

    inputs = tokens[0].astype(F32)
    scale_one = lax.rsqrt(jnp.mean(inputs * inputs, axis=-1, keepdims=True) + EPSILON)
    unit_one = inputs * scale_one
    gains = gather_gains(jnp.stack([gain_attn, gain_mlp]), w).astype(F32)
    gain_one, gain_two = gains[0], gains[1]
    normed_one = (unit_one * gain_one).astype(BF16)
    one_pieces = plane(after(normed_one, first))

    gate_up_weight = after(gate_up_weight, one_pieces)
    gate_block, _ = eighth_block([(gate_up_weight, 0, ff_cols)], x, n)
    up_block, _ = eighth_block([(after(gate_up_weight, gate_block), FF, ff_cols)], x, n)
    down_block, _ = eighth_block([(after(down_weight, up_block), 0, ff_cols)], x, n)
    cot = cotangent[0]

    def to_units(own, other, parts):
        def split(flat):
            return flat.reshape(2, 2, rows_here, parts, 2, DK).transpose(1, 4, 0, 3, 2, 5)

        v = jnp.stack([split(own), split(other)], axis=2)
        v = by_bit([v[0], v[1]], x)
        v = v.transpose(1, 2, 3, 4, 0, 5, 6).reshape(GROUP, parts, 2 * rows_here, DK)
        blocks = []
        for d in range(zspan):
            block = lax.dynamic_slice_in_dim(v, (zi ^ d) * units, units, 0)
            given = block
            blocks.append(block if d == 0 else swap_z(block, d))
        v = by_index(blocks, zi)
        return v.transpose(1, 2, 0, 3, 4).reshape(units, parts, SEG, DK), given, blocks[-1]

    def from_units(v, parts):
        v = v.reshape(units, parts, zspan, 2 * rows_here, DK)
        blocks = []
        for d in range(zspan):
            block = lax.dynamic_slice_in_dim(v, zi ^ d, 1, 2)[:, :, 0]
            given = block
            blocks.append(block if d == 0 else swap_z(block, d))
        v = by_index(blocks, zi).reshape(2, 2, 2, parts, 2, rows_here, DK)
        v = by_bit([v[:, :, :, :, 0], v[:, :, :, :, 1]], x)
        v = v.transpose(2, 3, 0, 5, 4, 1, 6)
        return v.reshape(GROUP * rows_here, parts * head_cols), given, blocks[-1]

    half = 4 * rows_here
    one_all = join(both_cores(one_pieces))
    one_all, gate_block, up_block, down_block = lax.optimization_barrier(
        (one_all, gate_block, up_block, down_block)
    )
    projected = dot(one_all, qkv_c).astype(BF16)
    qkv_units, given, swapped = to_units(projected[:half], projected[half:], 3)
    gate_c = gather_rows(after(gate_block, swapped))
    out_pieces = plane(first_c[:, 3 * head_cols :])
    qkv_units, out_pieces = lax.optimization_barrier((qkv_units, out_pieces))
    out_full = assemble(both_cores(out_pieces), c, 1, BF16)
    queries, keys, values = qkv_units[:, 0], qkv_units[:, 1], qkv_units[:, 2]

    head_count = max(1, units // 4)
    seq_count = units // head_count
    first_head = (zi * units) // 4
    first_seq = (zi * units) % 4
    held = jnp.concatenate([memory_in[0], normalizer_in[0][:, None]], axis=1)
    fetched = []
    for offset in range(4):
        core, y = offset >> 1, offset & 1
        flip = y * 2 + core
        block = lax.dynamic_slice_in_dim(
            held, ((n ^ flip) * 2 + x) * 2 + first_head, head_count, 0
        )
        if flip:
            block = lax.ppermute(block, "narrow", [(i, i ^ flip) for i in range(4)])
        fetched.append(block)
    mem_in = jnp.stack(fetched, axis=1)
    mem_in = lax.dynamic_slice_in_dim(mem_in, first_seq, seq_count, 1)
    mem_in = mem_in.reshape(units, DK + 1, DK)

    query_f, key_f, value_f = (a.astype(F32) for a in (queries, keys, values))
    lift_q = jax.nn.elu(query_f) + 1.0
    lift_k = jax.nn.elu(key_f) + 1.0
    part_mem = jnp.einsum("utd,ute->ude", lift_k, value_f, preferred_element_type=F32)
    part_norm = jnp.sum(lift_k, axis=1)
    part = jnp.concatenate([part_mem, part_norm[:, None]], axis=1) / SEG
    direct = attention(after(qkv_units, part), scale)
    read = mem_in
    for k in range(1, segments):
        read = read + lax.ppermute(
            part, "wide", [(i, i + k * span) for i in range(wide - k * span)]
        )
    read_mem, read_norm = read[:, :DK], read[:, DK]
    numerator = jnp.einsum("utd,ude->ute", lift_q, read_mem, preferred_element_type=F32)
    denominator = jnp.sum(lift_q * read_norm[:, None], axis=-1, keepdims=True)
    recalled = numerator / denominator

    unit_heads = c * 2 + (zi * units + jnp.arange(units)) // 4
    mixing = jax.nn.sigmoid(gate_logit[unit_heads])
    mix = mixing[:, None, None]
    attended_units = (mix * recalled + (1.0 - mix) * direct).astype(BF16)
    attended_c, given, swapped = from_units(attended_units[:, None], 1)
    up_c = gather_rows(after(up_block, swapped))
    down_c = gather_rows(after(down_block, swapped))
    attended_c, out_full = lax.optimization_barrier((attended_c, out_full))
    attended_c = attended_c.reshape(GROUP, rows_here, head_cols)
    sent = exchange_group([attended_c[r] for r in range(GROUP)])
    attended = assemble_stacked(jnp.concatenate(sent, axis=0), c, BF16)

    middle = inputs + dot(attended, out_full)
    scale_two = lax.rsqrt(jnp.mean(middle * middle, axis=-1, keepdims=True) + EPSILON)
    unit_two = middle * scale_two
    normed_two = (unit_two * gain_two).astype(BF16)
    two_pieces = plane(normed_two)
    cot_pieces = plane(after(cot, two_pieces))
    two_all = join(both_cores(two_pieces))
    gate_short = dot(two_all, gate_c).astype(BF16)
    up_short = dot(after(two_all, gate_short), up_c).astype(BF16)
    cot_pieces, up_short, down_c = lax.optimization_barrier((cot_pieces, up_short, down_c))
    gate_part, up_part = gate_short.astype(F32), up_short.astype(F32)
    gate_sig = jax.nn.sigmoid(gate_part)
    activation = (gate_part * gate_sig * up_part).astype(BF16)
    cot_all = join(both_cores(cot_pieces))
    grad_down_part = t_dot(cot_all, activation).astype(BF16)
    grad_down_c = reduce_rows(grad_down_part)
    att_pieces = plane(after(attended, cot_all))
    grad_activ = dot(after(cot_all, grad_down_part), down_c)
    grad_gate = (
        grad_activ * up_part * gate_sig * (1.0 + gate_part * (1.0 - gate_sig))
    ).astype(BF16)
    grad_upper = (grad_activ * gate_part * gate_sig).astype(BF16)
    back = (dot_t(grad_gate, gate_c) + dot_t(grad_upper, up_c)).astype(BF16)
    back, att_pieces = lax.optimization_barrier((back, att_pieces))
    back_got = scatter_sends(scatter_start(back))
    grad_gate_part = t_dot(two_all, after(grad_gate, back)).astype(BF16)
    grad_gate_c = reduce_rows(grad_gate_part)
    grad_up_part = t_dot(two_all, after(grad_upper, grad_gate_part)).astype(BF16)
    grad_up_c = reduce_rows(grad_up_part)
    mlp_part = dot_t(after(activation, grad_up_part), down_c).astype(BF16)
    att_all = join(both_cores(att_pieces))
    mlp_sums = scatter_start(mlp_part)
    back_got, mlp_sums, att_all, grad_down_c = lax.optimization_barrier(
        (back_got, mlp_sums, att_all, grad_down_c)
    )
    mlp_got = scatter_sends(mlp_sums)
    grad_normed_two = scatter_total(back_got)
    grad_gain_two = jnp.sum(grad_normed_two * unit_two, axis=0)
    grad_middle = cot.astype(F32) + norm_back(grad_normed_two * gain_two, unit_two, scale_two)

    grad_branch = grad_middle.astype(BF16)
    grad_att_rows = dot_t(grad_branch, out_full).astype(BF16)
    sent = exchange_group(
        [
            lax.dynamic_slice_in_dim(grad_att_rows, (c ^ absolute(r)) * head_cols, head_cols, 1)
            for r in range(GROUP)
        ]
    )
    sent, mlp_got = lax.optimization_barrier((sent, mlp_got))
    grad_att_units, given, _ = to_units(
        jnp.concatenate(sent[:4], axis=0), jnp.concatenate(sent[4:], axis=0), 1
    )

    late_branch, late_down = after((grad_branch, grad_down_c), given)
    branch_pieces = exchange_group(
        [
            lax.dynamic_slice_in_dim(late_branch, (c ^ absolute(r)) * head_cols, head_cols, 1)
            for r in range(GROUP)
        ]
    )
    down_pair = spread_x(late_down, x)
    grad_att_units, branch_pieces = lax.optimization_barrier((grad_att_units, branch_pieces))
    grad_att = grad_att_units[:, 0].astype(F32)

    unit_logit = jnp.sum(grad_att * (recalled - direct), axis=(1, 2)) * mixing * (1.0 - mixing)
    grad_logit = jnp.sum(
        jnp.where(unit_heads[:, None] == jnp.arange(H)[None], unit_logit[:, None], 0.0), axis=0
    )
    grad_recall = (mix * grad_att).astype(BF16).astype(F32)
    grad_numer = grad_recall / denominator
    grad_denom = -jnp.sum(grad_recall * recalled, axis=-1, keepdims=True) / denominator
    grad_lift_q = (
        jnp.einsum("ute,ude->utd", grad_numer, read_mem, preferred_element_type=F32)
        + grad_denom * read_norm[:, None]
    )
    grad_read_mem = jnp.einsum("utd,ute->ude", lift_q, grad_numer, preferred_element_type=F32)
    grad_read_norm = jnp.sum(grad_denom * lift_q, axis=1)
    grad_read = jnp.concatenate([grad_read_mem, grad_read_norm[:, None]], axis=1)
    grad_direct = after((1.0 - mix) * grad_att, grad_read).astype(BF16)
    dots = attention_back(qkv_units, grad_direct, scale)
    later = jnp.zeros_like(grad_read)
    for k in range(1, segments):
        later = later + lax.ppermute(
            grad_read, "wide", [(i + k * span, i) for i in range(wide - k * span)]
        )
    later, dots, down_pair = lax.optimization_barrier((later / SEG, dots, down_pair))
    down_four = spread_y(down_pair)
    gate_up_pair = spread_x(
        jnp.concatenate(after([grad_gate_c, grad_up_c], dots), axis=1), x
    )
    grad_q_dot, grad_k_dot, grad_v_dot = dots[:, 0], dots[:, 1], dots[:, 2]
    later_mem, later_norm = later[:, :DK], later[:, DK]
    grad_lift_k = (
        jnp.einsum("ute,ude->utd", value_f, later_mem, preferred_element_type=F32)
        + later_norm[:, None]
    )
    grad_v_mem = jnp.einsum("utd,ude->ute", lift_k, later_mem, preferred_element_type=F32)
    grad_units = jnp.stack(
        [
            grad_q_dot + grad_lift_q * elu_slope(query_f),
            grad_k_dot + grad_lift_k * elu_slope(key_f),
            grad_v_dot + grad_v_mem,
        ],
        axis=1,
    ).astype(BF16)
    grad_projected, given, _ = from_units(grad_units, 3)
    grad_out_part = t_dot(
        after(att_all, given), jnp.concatenate(branch_pieces, axis=0)
    ).astype(BF16)
    grad_out_c = reduce_rows(grad_out_part)
    grad_projected, grad_out_part, down_four, gate_up_pair = lax.optimization_barrier(
        (grad_projected, grad_out_part, down_four, gate_up_pair)
    )
    grad_qkv_part = t_dot(one_all, grad_projected).astype(BF16)
    grad_qkv_c = reduce_rows(grad_qkv_part)
    one_part = dot_t(after(grad_projected, grad_qkv_part), qkv_c).astype(BF16)
    gate_up_y = swap_y(gate_up_pair[0])
    one_part, gate_up_y = lax.optimization_barrier((one_part, gate_up_y))
    one_sums = scatter_start(one_part)
    one_got = scatter_sends(one_sums)
    gate_up_four = gate_up_pair + [gate_up_y, swap_y(after(gate_up_pair[1], gate_up_y))]
    grad_down = assemble(both_cores(after(down_four, one_sums)), c, 1, F32)
    output = (middle + scatter_total(after(mlp_got, one_sums))).astype(BF16)[None]
    one_got, gate_up_four, grad_down, output = lax.optimization_barrier(
        (one_got, gate_up_four, grad_down, output)
    )
    grad_normed_one = scatter_total(one_got)
    grad_gain_one = jnp.sum(grad_normed_one * unit_one, axis=0)
    grad_tokens = (
        grad_middle + norm_back(grad_normed_one * gain_one, unit_one, scale_one)
    ).astype(BF16)[None]
    def finish(four, parts):
        return assemble(both_cores(four), c, parts, F32)

    out_four = spread_y(spread_x(after(grad_out_c, gate_up_four), x))
    grad_gate_up = finish(gate_up_four, 2)
    qkv_pair = spread_x(after(grad_qkv_c, out_four, grad_normed_one), x)
    qkv_four = spread_y(qkv_pair)
    grad_out = finish(out_four, 1)
    grad_qkv = finish(qkv_four, 3)

    placed = jnp.zeros((GROUP, DK + 1, DK), BF16)
    placed = lax.dynamic_update_slice_in_dim(placed, after(grad_read, one_sums).astype(BF16), zi * units, 0)
    placed = placed.reshape(2, 4, DK + 1, DK)
    got = []
    for flip in range(4):
        core, y = flip & 1, flip >> 1
        block = placed[:, core * 2 + y]
        if flip:
            block = lax.ppermute(block, "narrow", [(i, i ^ flip) for i in range(4)])
        got.append(block)
    mine = sum_z(by_index(after(got, grad_normed_one), n))
    heads = by_bit([mine, swap_x(mine)], x).transpose(1, 0, 2, 3, 4)
    heads = heads.reshape(H, DK + 1, DK).astype(F32)

    small = sum_all(jnp.concatenate([grad_gain_one, grad_gain_two, grad_logit]))
    gain_one_sum = lax.dynamic_slice_in_dim(small, w * shard, shard, 0)
    gain_two_sum = lax.dynamic_slice_in_dim(small, D + w * shard, shard, 0)
    return (
        output,
        grad_tokens,
        heads[None, :, :DK],
        heads[None, :, DK],
        grad_qkv,
        grad_out,
        gain_one_sum,
        grad_gate_up,
        grad_down,
        gain_two_sum,
        small[2 * D :],
    )


def solution(mesh):
    return jax.shard_map(
        body,
        mesh=mesh,
        in_specs=(
            P("narrow", "wide", None),
            P("narrow", "wide", None),
            P("wide", None),
            P("wide", None),
            P("wide"),
            P("wide", None),
            P("wide", None),
            P("wide"),
            P(),
            P("narrow", None, None, None),
            P("narrow", None, None),
        ),
        out_specs=(
            P("narrow", "wide", None),
            P("narrow", "wide", None),
            P("narrow", None, None, None),
            P("narrow", None, None),
            P("wide", None),
            P("wide", None),
            P("wide"),
            P("wide", None),
            P("wide", None),
            P("wide"),
            P(),
        ),
        check_vma=False,
    )
```

time: 1430 us -> 1060 us (0.74)
  starting transfers between devices: 228 us -> 131 us
  local copies, waits for them, and re-layouts: 174 us -> 90.4 us
  waiting for transfers between devices: 574 us -> 495 us
  blocking collectives: 62.3 us -> 0 us
  matrix products: 225 us -> 183 us
  other arithmetic: 97.2 us -> 69.1 us
  Pallas kernels: 44.7 us -> 68.4 us
    ppermute x21 -> x45, waiting for transfers between devices: 24.2 us -> 248 us  [send_offset(): return lax.ppermute(v, ('narrow', 'wide'), route)]
    ppermute x27 -> x7, waiting for transfers between devices: 222 us -> 3.45 us  [gather_gains(): blocks.append(lax.ppermute(v, 'wide', [(i, i ^ d) for i in range(n)]))]
    ppermute x22 -> x10, waiting for transfers between devices: 130 us -> 53 us  [swap_x(): return lax.ppermute(v, 'wide', [(i, i ^ 1) for i in range(n)])]
    ppermute x27 -> x7, starting transfers between devices: 80.1 us -> 15.4 us  [gather_gains(): blocks.append(lax.ppermute(v, 'wide', [(i, i ^ d) for i in range(n)]))]
    psum x1 -> x0, waiting for transfers between devices: 61.3 us -> none  [body(): heads = lax.psum(heads.reshape(H, DK + 1, DK), 'wide').astype(F32)]
    ppermute x4 -> x8, waiting for transfers between devices: 42 us -> 90.6 us  [swap_z(): return lax.ppermute(v, 'wide', [(i, i ^ 2 * d) for i in range(n)])]
    ppermute x4 -> x8, starting transfers between devices: 70.3 us -> 28.3 us  [swap_z(): return lax.ppermute(v, 'wide', [(i, i ^ 2 * d) for i in range(n)])]
    psum x1 -> x0, blocking collectives: 40.1 us -> none  [body(): lax.psum(jnp.concatenate([grad_gain_one, grad_gain_two, grad_logit]), ('n...]
  transfers between devices with their start and end apart: 113 -> 145, of which waited for: 53 -> 57; matrix products, arithmetic and copies ran while one was open for 26% -> 28% of each run, Pallas kernels for 3% -> 6%
where the time goes in v2:
time: 1060 us; the launch traced here: 1050 us
  waiting for transfers between devices  495 us (47%)
  matrix products  183 us (17%)
  starting transfers between devices  131 us (12%)
  local copies, waits for them, and re-layouts  90.4 us (9%)
  other arithmetic  69.1 us (7%)
  Pallas kernels  68.4 us (6%)
  between operations  16 us (2%)
    ppermute x45, waiting for transfers between devices, send_offset(): return lax.ppermute(v, ('narrow', 'wide'), route)  248 us
    ppermute x8, waiting for transfers between devices, swap_z(): return lax.ppermute(v, 'wide', [(i, i ^ 2 * d) for i in range(n)])  90.6 us
    dot_general x5, matrix products, dot(): return jnp.dot(a, b, preferred_element_type=F32)  59.2 us
    dot_general x5, matrix products, t_dot(): lax.dot_general(a, b, (((0,), (0,)), ((), ())), preferred_element_type=F32)  57.6 us
    dot_general x5, matrix products, dot_t(): lax.dot_general(a, b, (((1,), (1,)), ((), ())), preferred_element_type=F32)  55.1 us
    ppermute x10, waiting for transfers between devices, swap_x(): return lax.ppermute(v, 'wide', [(i, i ^ 1) for i in range(n)])  53 us
    ppermute x9, waiting for transfers between devices, swap_y(): return lax.ppermute(v, 'narrow', [(i, i ^ 2) for i in range(4)])  50.3 us
    ppermute x45, starting transfers between devices, send_offset(): return lax.ppermute(v, ('narrow', 'wide'), route)  49 us
  transfers between devices with their start and end apart: 145, of which 57 were waited for; matrix products, arithmetic and copies ran while one was open for 28% of the time, Pallas kernels for 6%

profile of v2, /device:TPU:0, one launch (start us, length us, event | category | flops | bytes accessed | tf_op | source)
XLA Modules:
  0.0 1052.2 jit_solution(15731187054979291115)
XLA Ops:
  18.9 4.8 collective-permute-done.7
  30.9 4.8 collective-permute-start.6
  41.3 23.5 %collective-permute-done.10.refs_3_ = bf16[256,2048]{1,0:T(8,128)(2,1)S(1)} collective-permute-done((bf16[256,2048]{1,0:T(8,128)(2,1)S(1)}, bf16[256,2048]{1,0:T(8,128)(2,1)S(1)}, u32[]{:S(2)}, u32[]{:S(2)}) %collective-permute-start.10) | collective-permute-done | bytes 1048608 | tf_op jit(solution)/shard_map/ppermute | solution.py:53
  64.8 17.6 %collective-permute-done.9.refs_2_ = bf16[256,2048]{1,0:T(8,128)(2,1)S(1)} collective-permute-done((bf16[256,2048]{1,0:T(8,128)(2,1)S(1)}, bf16[256,2048]{1,0:T(8,128)(2,1)S(1)}, u32[]{:S(2)}, u32[]{:S(2)}) %collective-permute-start.9) | collective-permute-done | bytes 1048608 | tf_op jit(solution)/shard_map/ppermute | solution.py:53
  85.9 13.0 %collective-permute-done.15 = bf16[256,1024]{1,0:T(8,128)(2,1)} collective-permute-done((bf16[256,1024]{1,0:T(8,128)(2,1)}, bf16[256,1024]{1,0:T(8,128)(2,1)}, u32[]{:S(2)}, u32[]{:S(2)}) %collective-permute-start.15) | collective-permute-done | bytes 524320 | tf_op jit(solution)/shard_map/ppermute | solution.py:23
  105.9 11.1 %collective-permute-done.16 = bf16[256,1024]{1,0:T(8,128)(2,1)} collective-permute-done((bf16[256,1024]{1,0:T(8,128)(2,1)}, bf16[256,1024]{1,0:T(8,128)(2,1)}, u32[]{:S(2)}, u32[]{:S(2)}) %collective-permute-start.16) | collective-permute-done | bytes 524320 | tf_op jit(solution)/shard_map/ppermute | solution.py:23
  123.1 3.8 shard_map.194
  130.3 4.0 collective-permute-done.17
  136.6 10.0 convolution_convert_fusion.7
  153.6 33.5 %collective-permute-done.18 = bf16[4,3,512,128]{3,2,1,0:T(8,128)(2,1)S(1)} collective-permute-done((bf16[4,3,512,128]{3,2,1,0:T(8,128)(2,1)S(1)}, bf16[4,3,512,128]{3,2,1,0:T(8,128)(2,1)S(1)}, u32[]{:S(2)}, u32[]{:S(2)}) %collective-permute-start.18) | collective-permute-done | bytes 1572896 | tf_op jit(solution)/shard_map/ppermute | solution.py:36
  197.4 19.6 %collective-permute-done.21.refs_3_ = bf16[2048,256]{1,0:T(8,128)(2,1)} collective-permute-done((bf16[2048,256]{1,0:T(8,128)(2,1)}, bf16[2048,256]{1,0:T(8,128)(2,1)}, u32[]{:S(2)}, u32[]{:S(2)}) %collective-permute-start.21) | collective-permute-done | bytes 1048608 | tf_op jit(solution)/shard_map/ppermute | solution.py:53
  217.0 17.9 %collective-permute-done.20.refs_2_ = bf16[2048,256]{1,0:T(8,128)(2,1)} collective-permute-done((bf16[2048,256]{1,0:T(8,128)(2,1)}, bf16[2048,256]{1,0:T(8,128)(2,1)}, u32[]{:S(2)}, u32[]{:S(2)}) %collective-permute-start.20) | collective-permute-done | bytes 1048608 | tf_op jit(solution)/shard_map/ppermute | solution.py:53
  237.8 4.6 collective-permute-start.25
  242.4 8.9 shard_map.195
  259.7 17.3 %collective-permute-start.26 = (bf16[4,1,512,128]{3,2,0,1:T(8,128)(2,1)S(1)}, bf16[4,1,512,128]{3,2,0,1:T(8,128)(2,1)S(1)}, u32[]{:S(2)}, u32[]{:S(2)}) collective-permute-start(bf16[4,1,512,128]{3,2,0,1:T(8,128)(2,1)S(1)} %get-tuple-element.340), channel_id=1, source_target_pairs={{0,2},{1,3},{2,0},{3,1},{4,6},{5,7},{6,4},{7,5},{8,10},{9,11},{10,... | collective-permute-start | bytes 1572872 | tf_op jit(solution)/shard_map/ppermute | solution.py:36
  277.0 12.2 %collective-permute-done.26 = bf16[4,1,512,128]{3,2,0,1:T(8,128)(2,1)S(1)} collective-permute-done((bf16[4,1,512,128]{3,2,0,1:T(8,128)(2,1)S(1)}, bf16[4,1,512,128]{3,2,0,1:T(8,128)(2,1)S(1)}, u32[]{:S(2)}, u32[]{:S(2)}) %collective-permute-start.26) | collective-permute-done | bytes 524320 | tf_op jit(solution)/shard_map/ppermute | solution.py:36
  296.7 5.9 shard_map.196
  313.5 4.6 collective-permute-done.33
  326.4 23.0 %collective-permute-done.40.refs_3_ = bf16[256,2048]{1,0:T(8,128)(2,1)} collective-permute-done((bf16[256,2048]{1,0:T(8,128)(2,1)S(1)}, bf16[256,2048]{1,0:T(8,128)(2,1)}, u32[]{:S(2)}, u32[]{:S(2)}) %collective-permute-start.40) | collective-permute-done | bytes 1048608 | tf_op jit(solution)/shard_map/ppermute | solution.py:53
  349.4 21.8 %collective-permute-done.39.refs_2_ = bf16[256,2048]{1,0:T(8,128)(2,1)} collective-permute-done((bf16[256,2048]{1,0:T(8,128)(2,1)S(1)}, bf16[256,2048]{1,0:T(8,128)(2,1)}, u32[]{:S(2)}, u32[]{:S(2)}) %collective-permute-start.39) | collective-permute-done | bytes 1048608 | tf_op jit(solution)/shard_map/ppermute | solution.py:53
  382.5 13.8 %convolution_convert_fusion.3 = bf16[2048,1024]{1,0:T(8,128)(2,1)} fusion(bf16[2048,2048]{1,0:T(8,128)(2,1)} %copy-done.8, bf16[2048,1024]{1,0:T(8,128)(2,1)} %all-gather.7.cloned.1.call-done), kind=kOutput, calls=%fused_computation.26 | convolution fusion | flops 8592031744 | bytes 16777216 | tf_op jit(solution)/shard_map/dot_general | solution.py:314
  396.3 13.8 %convolution_convert_fusion.2 = bf16[2048,1024]{1,0:T(8,128)(2,1)} fusion(bf16[2048,2048]{1,0:T(8,128)(2,1)} %copy-done.8, bf16[2048,1024]{1,0:T(8,128)(2,1)} %all-gather.9.cloned.1.call-done), kind=kOutput, calls=%fused_computation.25 | convolution fusion | flops 8592031744 | bytes 16777216 | tf_op jit(solution)/shard_map/dot_general | solution.py:314
  410.1 10.2 collective-permute-done.42.refs_2_
  420.3 32.6 %all-gather.11.cloned.1.call-done = bf16[2048,1024]{1,0:T(8,128)(2,1)} async-done(((bf16[512,1024]{1,0:T(8,128)(2,1)}), bf16[2048,1024]{1,0:T(8,128)(2,1)}) %all-gather.11.cloned.1.call-update) | async-done | bytes 4194320 | tf_op jit(solution)/shard_map/all_gather | solution.py:142
  454.0 4.8 fusion
  467.3 10.7 %convolution_convert_fusion.6 = bf16[2048,1024]{1,0:T(8,128)(2,1)} fusion(bf16[2048,2048]{1,0:T(8,128)(2,1)S(1)} %shard_map.199, bf16[2048,1024]{1,0:T(8,128)(2,1)S(1)} %fusion), kind=kOutput, calls=%fused_computation.29 | convolution fusion | flops 8592031744 | bytes 16777216 | tf_op jit(solution)/shard_map/dot_general | solution.py:322
  478.0 19.0 %fusion.3 = (bf16[2048,1024]{1,0:T(8,128)(2,1)}, bf16[2048,1024]{1,0:T(8,128)(2,1)S(1)}) fusion(bf16[2048,1024]{1,0:T(8,128)(2,1)} %convolution_convert_fusion.2, bf16[2048,1024]{1,0:T(8,128)(2,1)} %convolution_convert_fusion.3, bf16[2048,2048]{1,0:T(8,128)(2,1)} %copy-done.9, bf16[2048,1024]{1,0:T(8,128)(2,1)} %all-gather.11.cloned.1.call-done), kind=kOutput, calls=%fused_computation.11 | convolution fusion | flops 8621391872 | bytes 29360128 | tf_op jit(solution)/shard_map/dot_general | solution.py:314
  497.1 11.9 %fusion.122 = f32[2048,2048]{1,0:T(8,128)} fusion(bf16[2048,1024]{1,0:T(8,128)(2,1)S(1)} %get-tuple-element.156, bf16[2048,1024]{1,0:T(8,128)(2,1)S(1)} %copy-done.84), kind=kOutput, calls=%fused_computation.339 | convolution fusion | flops 8589934592 | bytes 25165824 | tf_op jit(solution)/shard_map/dot_general | solution.py:318
  508.9 16.0 %add_convert_fusion = bf16[2048,2048]{1,0:T(8,128)(2,1)} fusion(f32[2048,2048]{1,0:T(8,128)} %fusion.122, bf16[2048,1024]{1,0:T(8,128)(2,1)} %get-tuple-element.155, bf16[2048,1024]{1,0:T(8,128)(2,1)S(1)} %copy-done.83), kind=kOutput, calls=%fused_computation.1 | convolution fusion | flops 8598323200 | bytes 33554432 | tf_op jit(solution)/shard_map/dot_general | solution.py:318
  524.9 14.4 %convolution_convert_fusion.5 = bf16[2048,1024]{1,0:T(8,128)(2,1)} fusion(bf16[2048,2048]{1,0:T(8,128)(2,1)} %copy-done.8, bf16[2048,1024]{1,0:T(8,128)(2,1)} %get-tuple-element.155), kind=kOutput, calls=%fused_computation.28 | convolution fusion | flops 8592031744 | bytes 16777216 | tf_op jit(solution)/shard_map/dot_general | solution.py:322
  539.3 14.0 %convolution_convert_fusion.4 = bf16[2048,1024]{1,0:T(8,128)(2,1)} fusion(bf16[2048,2048]{1,0:T(8,128)(2,1)} %copy-done.8, bf16[2048,1024]{1,0:T(8,128)(2,1)} %copy-done.90), kind=kOutput, calls=%fused_computation.27 | convolution fusion | flops 8592031744 | bytes 16777216 | tf_op jit(solution)/shard_map/dot_general | solution.py:322
  554.1 4.7 fusion.116
  561.8 11.6 %convolution_convert_fusion.1 = bf16[2048,2048]{1,0:T(8,128)(2,1)S(1)} fusion(bf16[2048,1024]{1,0:T(8,128)(2,1)S(1)} %copy-done.44, bf16[2048,1024]{1,0:T(8,128)(2,1)} %all-gather.11.cloned.1.call-done), kind=kOutput, calls=%fused_computation.19 | convolution fusion | flops 8594128896 | bytes 16777216 | tf_op jit(solution)/shard_map/dot_general | solution.py:318
  578.6 5.8 add_convert_fusion.8
  593.9 3.7 shard_map.200
  600.9 6.2 add_convert_fusion.5
  607.1 5.5 collective-permute-done.61
  612.6 22.0 %collective-permute-done.59 = bf16[256,2048]{1,0:T(8,128)(2,1)} collective-permute-done((bf16[256,2048]{1,0:T(8,128)(2,1)}, bf16[256,2048]{1,0:T(8,128)(2,1)}, u32[]{:S(2)}, u32[]{:S(2)}) %collective-permute-start.59) | collective-permute-done | bytes 1048608 | tf_op jit(solution)/shard_map/ppermute | solution.py:53
  634.7 4.3 multiply_reduce_fusion
  643.2 6.1 convolution_convert_fusion.10
  652.1 37.2 %collective-permute-done.76 = bf16[256,256]{1,0:T(8,128)(2,1)S(1)} collective-permute-done((bf16[256,256]{1,0:T(8,128)(2,1)S(1)}, bf16[256,256]{1,0:T(8,128)(2,1)S(1)}, u32[]{:S(2)}, u32[]{:S(2)}) %collective-permute-start.76) | collective-permute-done | bytes 131104 | tf_op jit(solution)/shard_map/ppermute | solution.py:53
  696.3 5.1 collective-permute-done.72
  738.8 15.0 %shard_map.201 = f32[4,3,1024,128]{3,2,1,0:T(8,128)} custom-call(bf16[4,3,1024,128]{3,2,1,0:T(8,128)(2,1)S(1)} %bitcast.269, bf16[4,1024,128]{2,1,0:T(8,128)(2,1)S(1)} %convert_multiply_fusion.6.grad_ref), custom_call_target="tpu_custom_call" | custom-call | flops 5368709120 | bytes 10485760 | tf_op jit(solution)/shard_map/pallas_call | solution.py:296
  768.5 7.1 convolution_convert_fusion.9
  779.7 34.5 %collective-permute-done.90 = bf16[4,3,512,128]{3,2,1,0:T(8,128)(2,1)} collective-permute-done((bf16[4,3,512,128]{3,2,1,0:T(8,128)(2,1)}, bf16[4,3,512,128]{3,2,1,0:T(8,128)(2,1)}, u32[]{:S(2)}, u32[]{:S(2)}) %collective-permute-start.90) | collective-permute-done | bytes 1572896 | tf_op jit(solution)/shard_map/ppermute | solution.py:36
  818.2 4.9 copy.132
  823.1 8.0 reshape.519
  831.1 11.4 %convolution_convert_fusion.8 = bf16[2048,768]{1,0:T(8,128)(2,1)} fusion(bf16[2048,2048]{1,0:T(8,128)(2,1)} %copy-done.6, bf16[2048,768]{1,0:T(8,128)(2,1)} %reshape.519), kind=kOutput, calls=%fused_computation.39 | convolution fusion | flops 6444023808 | bytes 14680064 | tf_op jit(solution)/shard_map/dot_general | solution.py:322
  843.3 9.5 convolution_convert_fusion
  852.8 6.0 collective-permute-done.94.refs_2_
  879.4 4.4 fusion.59
  884.4 6.4 shard_map.202
  890.7 30.4 %collective-permute-done.102.refs_3_ = bf16[256,2048]{1,0:T(8,128)(2,1)S(1)} collective-permute-done((bf16[256,2048]{1,0:T(8,128)(2,1)}, bf16[256,2048]{1,0:T(8,128)(2,1)S(1)}, u32[]{:S(2)}, u32[]{:S(2)}) %collective-permute-start.102) | collective-permute-done | bytes 1048608 | tf_op jit(solution)/shard_map/ppermute | solution.py:27
  921.5 22.0 %collective-permute-done.99 = bf16[256,2048]{1,0:T(8,128)(2,1)S(1)} collective-permute-done((bf16[256,2048]{1,0:T(8,128)(2,1)}, bf16[256,2048]{1,0:T(8,128)(2,1)S(1)}, u32[]{:S(2)}, u32[]{:S(2)}) %collective-permute-start.99) | collective-permute-done | bytes 1048608 | tf_op jit(solution)/shard_map/ppermute | solution.py:53
  951.9 4.2 collective-permute-done.113.refs_1_
  957.2 7.8 collective-permute-start.111
  968.8 3.8 collective-permute-done.129
  977.4 4.0 collective-permute-done.131
  990.8 12.2 %collective-permute-done.112 = bf16[4,2,129,128]{3,2,1,0:T(8,128)(2,1)} collective-permute-done((bf16[4,2,129,128]{3,2,1,0:T(8,128)(2,1)}, bf16[4,2,129,128]{3,2,1,0:T(8,128)(2,1)}, u32[]{:S(2)}, u32[]{:S(2)}) %collective-permute-start.112) | collective-permute-done | bytes 264224 | tf_op jit(solution)/shard_map/ppermute | solution.py:23
  1005.2 5.4 fusion.60
  1011.1 3.9 collective-permute-done.117.refs_2_
  1015.0 8.0 collective-permute-done.118.refs_3_
  1031.3 9.7 shard_map.205
  1041.0 4.4 shard_map.203
  (609 shorter events, 278.1 us)
Async XLA Ops:
  7.2 129.4 %all-gather.5.cloned.1.call-start = ((), (), s32[]{:S(2)}) async-start(), calls=%async_computation.5 | async-start | bytes 5242880 | tf_op jit(solution)/shard_map/all_gather | solution.py:142
  11.8 23.9 %collective-permute-start.5 = (bf16[2,256]{1,0:T(2,128)(2,1)S(1)}, bf16[2,256]{1,0:T(2,128)(2,1)S(1)}, u32[]{:S(2)}, u32[]{:S(2)}) collective-permute-start(bf16[2,256]{1,0:T(2,128)(2,1)S(1)} %get-tuple-element.250), channel_id=1, source_target_pairs={{0,6},{1,7},{2,4},{3,5},{4,2},{5,3},{6,0},{7,1},{8,14},{9,15},{10,... | collective-permute-start | bytes 3080 | tf_op jit(solution)/shard_map/ppermute | solution.py:155
  26.6 355.8 %all-gather.7.cloned.1.call-start = ((), (), s32[]{:S(2)}) async-start(), calls=%async_computation.6 | async-start | bytes 5242880 | tf_op jit(solution)/shard_map/all_gather | solution.py:142
  37.8 27.0 %collective-permute-start.10 = (bf16[256,2048]{1,0:T(8,128)(2,1)S(1)}, bf16[256,2048]{1,0:T(8,128)(2,1)S(1)}, u32[]{:S(2)}, u32[]{:S(2)}) collective-permute-start(bf16[256,2048]{1,0:T(8,128)(2,1)S(1)} %fusion.22.refs_0_), channel_id=1, source_target_pairs={{0,17},{1,16},{2,19},{3,18},{4,21},{5,20},{6,23},{7,22},{8,25},{9,... | collective-permute-start | bytes 3145736 | tf_op jit(solution)/shard_map/ppermute | solution.py:53
  40.5 41.9 %collective-permute-start.9 = (bf16[256,2048]{1,0:T(8,128)(2,1)S(1)}, bf16[256,2048]{1,0:T(8,128)(2,1)S(1)}, u32[]{:S(2)}, u32[]{:S(2)}) collective-permute-start(bf16[256,2048]{1,0:T(8,128)(2,1)S(1)} %fusion.22.refs_0_), channel_id=1, source_target_pairs={{0,16},{1,17},{2,18},{3,19},{4,20},{5,21},{6,22},{7,23},{8,24},{9,... | collective-permute-start | bytes 3145736 | tf_op jit(solution)/shard_map/ppermute | solution.py:53
  41.0 41.6 %collective-permute-start.8 = (bf16[256,2048]{1,0:T(8,128)(2,1)S(1)}, bf16[256,2048]{1,0:T(8,128)(2,1)}, u32[]{:S(2)}, u32[]{:S(2)}) collective-permute-start(bf16[256,2048]{1,0:T(8,128)(2,1)S(1)} %fusion.22.refs_0_), channel_id=1, source_target_pairs={{0,1},{1,0},{2,3},{3,2},{4,5},{5,4},{6,7},{7,6},{8,9},{9,8},{10,11... | collective-permute-start | bytes 3145736 | tf_op jit(solution)/shard_map/ppermute | solution.py:53
  153.6 33.6 %collective-permute-start.18 = (bf16[4,3,512,128]{3,2,1,0:T(8,128)(2,1)S(1)}, bf16[4,3,512,128]{3,2,1,0:T(8,128)(2,1)S(1)}, u32[]{:S(2)}, u32[]{:S(2)}) collective-permute-start(bf16[4,3,512,128]{3,2,1,0:T(8,128)(2,1)S(1)} %get-tuple-element.290), channel_id=1, source_target_pairs={{0,2},{1,3},{2,0},{3,1},{4,6},{5,7},{6,4},{7,5},{8,10},{9,11},{10,... | collective-permute-start | bytes 4718600 | tf_op jit(solution)/shard_map/ppermute | solution.py:36
  187.2 209.1 %all-gather.9.cloned.1.call-start = ((), (), s32[]{:S(2)}) async-start(), calls=%async_computation.7 | async-start | bytes 5242880 | tf_op jit(solution)/shard_map/all_gather | solution.py:142
  189.7 27.3 %collective-permute-start.21 = (bf16[2048,256]{1,0:T(8,128)(2,1)}, bf16[2048,256]{1,0:T(8,128)(2,1)}, u32[]{:S(2)}, u32[]{:S(2)}) collective-permute-start(bf16[2048,256]{1,0:T(8,128)(2,1)} %slice.274.refs_0_), channel_id=1, source_target_pairs={{0,17},{1,16},{2,19},{3,18},{4,21},{5,20},{6,23},{7,22},{8,25},{9,... | collective-permute-start | bytes 3145736 | tf_op jit(solution)/shard_map/ppermute | solution.py:53
  190.6 44.2 %collective-permute-start.20 = (bf16[2048,256]{1,0:T(8,128)(2,1)}, bf16[2048,256]{1,0:T(8,128)(2,1)}, u32[]{:S(2)}, u32[]{:S(2)}) collective-permute-start(bf16[2048,256]{1,0:T(8,128)(2,1)} %slice.274.refs_0_), channel_id=1, source_target_pairs={{0,16},{1,17},{2,18},{3,19},{4,20},{5,21},{6,22},{7,23},{8,24},{9,... | collective-permute-start | bytes 3145736 | tf_op jit(solution)/shard_map/ppermute | solution.py:53
  192.2 42.7 %collective-permute-start.19 = (bf16[2048,256]{1,0:T(8,128)(2,1)}, bf16[2048,256]{1,0:T(8,128)(2,1)}, u32[]{:S(2)}, u32[]{:S(2)}) collective-permute-start(bf16[2048,256]{1,0:T(8,128)(2,1)} %slice.274.refs_0_), channel_id=1, source_target_pairs={{0,1},{1,0},{2,3},{3,2},{4,5},{5,4},{6,7},{7,6},{8,9},{9,8},{10,11... | collective-permute-start | bytes 3145736 | tf_op jit(solution)/shard_map/ppermute | solution.py:53
  194.8 56.5 %collective-permute-start.22 = (f32[1,129,128]{2,1,0:T(8,128)}, f32[1,129,128]{2,1,0:T(8,128)}, u32[]{:S(2)}, u32[]{:S(2)}) collective-permute-start(f32[1,129,128]{2,1,0:T(8,128)} %get-tuple-element.304), channel_id=1, source_target_pairs={{0,16},{8,24},{16,0},{24,8},{1,17},{9,25},{17,1},{25,9},{2,18},{10... | collective-permute-start | bytes 198152 | tf_op jit(solution)/shard_map/ppermute | solution.py:438
  196.0 55.4 %collective-permute-start.23 = (f32[1,129,128]{2,1,0:T(8,128)}, f32[1,129,128]{2,1,0:T(8,128)}, u32[]{:S(2)}, u32[]{:S(2)}) collective-permute-start(f32[1,129,128]{2,1,0:T(8,128)} %get-tuple-element.305), channel_id=1, source_target_pairs={{0,8},{8,0},{16,24},{24,16},{1,9},{9,1},{17,25},{25,17},{2,10},{10... | collective-permute-start | bytes 198152 | tf_op jit(solution)/shard_map/ppermute | solution.py:438
  217.0 34.4 %collective-permute-start.24 = (f32[1,129,128]{2,1,0:T(8,128)}, f32[1,129,128]{2,1,0:T(8,128)}, u32[]{:S(2)}, u32[]{:S(2)}) collective-permute-start(f32[1,129,128]{2,1,0:T(8,128)} %get-tuple-element.306), channel_id=1, source_target_pairs={{0,24},{8,16},{16,8},{24,0},{1,25},{9,17},{17,9},{25,1},{2,26},{10... | collective-permute-start | bytes 198152 | tf_op jit(solution)/shard_map/ppermute | solution.py:438
  259.7 29.5 %collective-permute-start.26 = (bf16[4,1,512,128]{3,2,0,1:T(8,128)(2,1)S(1)}, bf16[4,1,512,128]{3,2,0,1:T(8,128)(2,1)S(1)}, u32[]{:S(2)}, u32[]{:S(2)}) collective-permute-start(bf16[4,1,512,128]{3,2,0,1:T(8,128)(2,1)S(1)} %get-tuple-element.340), channel_id=1, source_target_pairs={{0,2},{1,3},{2,0},{3,1},{4,6},{5,7},{6,4},{7,5},{8,10},{9,11},{10,... | collective-permute-start | bytes 1572872 | tf_op jit(solution)/shard_map/ppermute | solution.py:36
  289.2 163.7 %all-gather.11.cloned.1.call-start = ((), (), s32[]{:S(2)}) async-start(), calls=%async_computation.8 | async-start | bytes 5242880 | tf_op jit(solution)/shard_map/all_gather | solution.py:142
  322.3 27.1 %collective-permute-start.40 = (bf16[256,2048]{1,0:T(8,128)(2,1)S(1)}, bf16[256,2048]{1,0:T(8,128)(2,1)}, u32[]{:S(2)}, u32[]{:S(2)}) collective-permute-start(bf16[256,2048]{1,0:T(8,128)(2,1)S(1)} %multiply_convert_fusion.refs_0_), channel_id=1, source_target_pairs={{0,17},{1,16},{2,19},{3,18},{4,21},{5,20},{6,23},{7,22},{8,25},{9,... | collective-permute-start | bytes 3145736 | tf_op jit(solution)/shard_map/ppermute | solution.py:53
  323.8 47.3 %collective-permute-start.39 = (bf16[256,2048]{1,0:T(8,128)(2,1)S(1)}, bf16[256,2048]{1,0:T(8,128)(2,1)}, u32[]{:S(2)}, u32[]{:S(2)}) collective-permute-start(bf16[256,2048]{1,0:T(8,128)(2,1)S(1)} %multiply_convert_fusion.refs_0_), channel_id=1, source_target_pairs={{0,16},{1,17},{2,18},{3,19},{4,20},{5,21},{6,22},{7,23},{8,24},{9,... | collective-permute-start | bytes 3145736 | tf_op jit(solution)/shard_map/ppermute | solution.py:53
  324.2 47.0 %collective-permute-start.38 = (bf16[256,2048]{1,0:T(8,128)(2,1)S(1)}, bf16[256,2048]{1,0:T(8,128)(2,1)}, u32[]{:S(2)}, u32[]{:S(2)}) collective-permute-start(bf16[256,2048]{1,0:T(8,128)(2,1)S(1)} %multiply_convert_fusion.refs_0_), channel_id=1, source_target_pairs={{0,1},{1,0},{2,3},{3,2},{4,5},{5,4},{6,7},{7,6},{8,9},{9,8},{10,11... | collective-permute-start | bytes 3145736 | tf_op jit(solution)/shard_map/ppermute | solution.py:53
  325.9 308.7 %reduce-scatter.6.cloned.1.call-start = ((), (), s32[]{:S(2)}) async-start(), calls=%async_computation.9 | async-start | bytes 5242880 | tf_op jit(solution)/shard_map/reduce_scatter | solution.py:146
  326.3 46.8 %collective-permute-start.44 = (bf16[256,2048]{1,0:T(8,128)(2,1)S(1)}, bf16[256,2048]{1,0:T(8,128)(2,1)S(1)}, u32[]{:S(2)}, u32[]{:S(2)}) collective-permute-start(bf16[256,2048]{1,0:T(8,128)(2,1)S(1)} %multiply_convert_fusion.refs_0_), channel_id=1, source_target_pairs={{0,8},{8,0},{16,24},{24,16},{1,9},{9,1},{17,25},{25,17},{2,10},{10... | collective-permute-start | bytes 3145736 | tf_op jit(solution)/shard_map/ppermute | solution.py:31
  349.4 24.3 %collective-permute-start.47 = (bf16[256,2048]{1,0:T(8,128)(2,1)}, bf16[256,2048]{1,0:T(8,128)(2,1)S(1)}, u32[]{:S(2)}, u32[]{:S(2)}) collective-permute-start(bf16[256,2048]{1,0:T(8,128)(2,1)} %collective-permute-done.40.refs_3_), channel_id=1, source_target_pairs={{0,8},{8,0},{16,24},{24,16},{1,9},{9,1},{17,25},{25,17},{2,10},{10... | collective-permute-start | bytes 3145736 | tf_op jit(solution)/shard_map/ppermute | solution.py:31
  371.7 38.4 %collective-permute-start.43 = (bf16[256,2048]{1,0:T(8,128)(2,1)S(1)}, bf16[256,2048]{1,0:T(8,128)(2,1)}, u32[]{:S(2)}, u32[]{:S(2)}) collective-permute-start(bf16[256,2048]{1,0:T(8,128)(2,1)S(1)} %bitcast.273), channel_id=1, source_target_pairs={{0,17},{1,16},{2,19},{3,18},{4,21},{5,20},{6,23},{7,22},{8,25},{9,... | collective-permute-start | bytes 3145736 | tf_op jit(solution)/shard_map/ppermute | solution.py:53
  373.1 47.1 %collective-permute-start.42 = (bf16[256,2048]{1,0:T(8,128)(2,1)S(1)}, bf16[256,2048]{1,0:T(8,128)(2,1)}, u32[]{:S(2)}, u32[]{:S(2)}) collective-permute-start(bf16[256,2048]{1,0:T(8,128)(2,1)S(1)} %bitcast.274), channel_id=1, source_target_pairs={{0,16},{1,17},{2,18},{3,19},{4,20},{5,21},{6,22},{7,23},{8,24},{9,... | collective-permute-start | bytes 3145736 | tf_op jit(solution)/shard_map/ppermute | solution.py:53
  373.7 46.6 %collective-permute-start.41 = (bf16[256,2048]{1,0:T(8,128)(2,1)S(1)}, bf16[256,2048]{1,0:T(8,128)(2,1)}, u32[]{:S(2)}, u32[]{:S(2)}) collective-permute-start(bf16[256,2048]{1,0:T(8,128)(2,1)S(1)} %bitcast.275), channel_id=1, source_target_pairs={{0,1},{1,0},{2,3},{3,2},{4,5},{5,4},{6,7},{7,6},{8,9},{9,8},{10,11... | collective-permute-start | bytes 3145736 | tf_op jit(solution)/shard_map/ppermute | solution.py:53
  463.7 61.2 %collective-permute-start.54 = (bf16[256,2048]{1,0:T(8,128)(2,1)S(1)}, bf16[256,2048]{1,0:T(8,128)(2,1)S(1)}, u32[]{:S(2)}, u32[]{:S(2)}) collective-permute-start(bf16[256,2048]{1,0:T(8,128)(2,1)S(1)} %shard_map.197.refs_0_), channel_id=1, source_target_pairs={{0,17},{1,16},{2,19},{3,18},{4,21},{5,20},{6,23},{7,22},{8,25},{9,... | collective-permute-start | bytes 3145736 | tf_op jit(solution)/shard_map/ppermute | solution.py:53
  466.2 58.7 %collective-permute-start.53 = (bf16[256,2048]{1,0:T(8,128)(2,1)S(1)}, bf16[256,2048]{1,0:T(8,128)(2,1)}, u32[]{:S(2)}, u32[]{:S(2)}) collective-permute-start(bf16[256,2048]{1,0:T(8,128)(2,1)S(1)} %shard_map.197.refs_0_), channel_id=1, source_target_pairs={{0,16},{1,17},{2,18},{3,19},{4,20},{5,21},{6,22},{7,23},{8,24},{9,... | collective-permute-start | bytes 3145736 | tf_op jit(solution)/shard_map/ppermute | solution.py:53
  466.7 58.2 %collective-permute-start.52 = (bf16[256,2048]{1,0:T(8,128)(2,1)S(1)}, bf16[256,2048]{1,0:T(8,128)(2,1)}, u32[]{:S(2)}, u32[]{:S(2)}) collective-permute-start(bf16[256,2048]{1,0:T(8,128)(2,1)S(1)} %shard_map.197.refs_0_), channel_id=1, source_target_pairs={{0,1},{1,0},{2,3},{3,2},{4,5},{5,4},{6,7},{7,6},{8,9},{9,8},{10,11... | collective-permute-start | bytes 3145736 | tf_op jit(solution)/shard_map/ppermute | solution.py:53
  478.0 288.5 %reduce-scatter.10.cloned.1.call-start = ((), (), s32[]{:S(2)}) async-start(), calls=%async_computation.11 | async-start | bytes 5242880 | tf_op jit(solution)/shard_map/reduce_scatter | solution.py:146
  553.4 213.1 %reduce-scatter.8.cloned.1.call-start = ((), (), s32[]{:S(2)}) async-start(), calls=%async_computation.10 | async-start | bytes 5242880 | tf_op jit(solution)/shard_map/reduce_scatter | solution.py:146
  554.0 23.5 %collective-permute-start.68 = (bf16[256,2048]{1,0:T(8,128)(2,1)}, bf16[256,2048]{1,0:T(8,128)(2,1)S(1)}, u32[]{:S(2)}, u32[]{:S(2)}) collective-permute-start(bf16[256,2048]{1,0:T(8,128)(2,1)} %collective-permute-done.53.refs_2_), channel_id=1, source_target_pairs={{0,8},{8,0},{16,24},{24,16},{1,9},{9,1},{17,25},{25,17},{2,10},{10... | collective-permute-start | bytes 3145736 | tf_op jit(solution)/shard_map/ppermute | solution.py:31
  578.1 22.8 %collective-permute-start.63 = (bf16[256,2048]{1,0:T(8,128)(2,1)}, bf16[256,2048]{1,0:T(8,128)(2,1)}, u32[]{:S(2)}, u32[]{:S(2)}) collective-permute-start(bf16[256,2048]{1,0:T(8,128)(2,1)} %get-tuple-element.267), channel_id=1, source_target_pairs={{0,8},{8,0},{16,24},{24,16},{1,9},{9,1},{17,25},{25,17},{2,10},{10... | collective-permute-start | bytes 3145736 | tf_op jit(solution)/shard_map/ppermute | solution.py:31
  578.5 22.3 %collective-permute-start.62 = (bf16[256,2048]{1,0:T(8,128)(2,1)}, bf16[256,2048]{1,0:T(8,128)(2,1)}, u32[]{:S(2)}, u32[]{:S(2)}) collective-permute-start(bf16[256,2048]{1,0:T(8,128)(2,1)} %get-tuple-element.268), channel_id=1, source_target_pairs={{0,8},{8,0},{16,24},{24,16},{1,9},{9,1},{17,25},{25,17},{2,10},{10... | collective-permute-start | bytes 3145736 | tf_op jit(solution)/shard_map/ppermute | solution.py:31
  585.4 27.2 %collective-permute-start.61 = (bf16[256,2048]{1,0:T(8,128)(2,1)}, bf16[256,2048]{1,0:T(8,128)(2,1)}, u32[]{:S(2)}, u32[]{:S(2)}) collective-permute-start(bf16[256,2048]{1,0:T(8,128)(2,1)} %get-tuple-element.269), channel_id=1, source_target_pairs={{0,17},{1,16},{2,19},{3,18},{4,21},{5,20},{6,23},{7,22},{8,25},{9,... | collective-permute-start | bytes 3145736 | tf_op jit(solution)/shard_map/ppermute | solution.py:53
  587.6 47.0 %collective-permute-start.59 = (bf16[256,2048]{1,0:T(8,128)(2,1)}, bf16[256,2048]{1,0:T(8,128)(2,1)}, u32[]{:S(2)}, u32[]{:S(2)}) collective-permute-start(bf16[256,2048]{1,0:T(8,128)(2,1)} %get-tuple-element.270), channel_id=1, source_target_pairs={{0,16},{1,17},{2,18},{3,19},{4,20},{5,21},{6,22},{7,23},{8,24},{9,... | collective-permute-start | bytes 3145736 | tf_op jit(solution)/shard_map/ppermute | solution.py:53
  588.1 46.5 %collective-permute-start.57 = (bf16[256,2048]{1,0:T(8,128)(2,1)}, bf16[256,2048]{1,0:T(8,128)(2,1)}, u32[]{:S(2)}, u32[]{:S(2)}) collective-permute-start(bf16[256,2048]{1,0:T(8,128)(2,1)} %get-tuple-element.271), channel_id=1, source_target_pairs={{0,1},{1,0},{2,3},{3,2},{4,5},{5,4},{6,7},{7,6},{8,9},{9,8},{10,11... | collective-permute-start | bytes 3145736 | tf_op jit(solution)/shard_map/ppermute | solution.py:53
  588.9 357.4 %reduce-scatter.14.cloned.1.call-start = ((), (), s32[]{:S(2)}) async-start(), calls=%async_computation.13 | async-start | bytes 1310720 | tf_op jit(solution)/shard_map/reduce_scatter | solution.py:146
  639.0 67.9 %collective-permute-start.77 = (bf16[256,2048]{1,0:T(8,128)(2,1)S(1)}, bf16[256,2048]{1,0:T(8,128)(2,1)S(1)}, u32[]{:S(2)}, u32[]{:S(2)}) collective-permute-start(bf16[256,2048]{1,0:T(8,128)(2,1)S(1)} %copy-done.56), channel_id=1, source_target_pairs={{0,1},{1,0},{2,3},{3,2},{4,5},{5,4},{6,7},{7,6},{8,9},{9,8},{10,11... | collective-permute-start | bytes 3145736 | tf_op jit(solution)/shard_map/ppermute | solution.py:53
  640.3 66.5 %collective-permute-start.78 = (bf16[256,2048]{1,0:T(8,128)(2,1)S(1)}, bf16[256,2048]{1,0:T(8,128)(2,1)S(1)}, u32[]{:S(2)}, u32[]{:S(2)}) collective-permute-start(bf16[256,2048]{1,0:T(8,128)(2,1)S(1)} %copy-done.55), channel_id=1, source_target_pairs={{0,16},{1,17},{2,18},{3,19},{4,20},{5,21},{6,22},{7,23},{8,24},{9,... | collective-permute-start | bytes 3145736 | tf_op jit(solution)/shard_map/ppermute | solution.py:53
  641.3 65.5 %collective-permute-start.79 = (bf16[256,2048]{1,0:T(8,128)(2,1)S(1)}, bf16[256,2048]{1,0:T(8,128)(2,1)S(1)}, u32[]{:S(2)}, u32[]{:S(2)}) collective-permute-start(bf16[256,2048]{1,0:T(8,128)(2,1)S(1)} %copy-done.54), channel_id=1, source_target_pairs={{0,17},{1,16},{2,19},{3,18},{4,21},{5,20},{6,23},{7,22},{8,25},{9,... | collective-permute-start | bytes 3145736 | tf_op jit(solution)/shard_map/ppermute | solution.py:53
  649.5 39.8 %collective-permute-start.76 = (bf16[256,256]{1,0:T(8,128)(2,1)S(1)}, bf16[256,256]{1,0:T(8,128)(2,1)S(1)}, u32[]{:S(2)}, u32[]{:S(2)}) collective-permute-start(bf16[256,256]{1,0:T(8,128)(2,1)S(1)} %get-tuple-element.321), channel_id=1, source_target_pairs={{0,25},{1,24},{2,27},{3,26},{4,29},{5,28},{6,31},{7,30},{8,17},{9,... | collective-permute-start | bytes 393224 | tf_op jit(solution)/shard_map/ppermute | solution.py:53
  650.2 41.7 %collective-permute-start.75 = (bf16[256,256]{1,0:T(8,128)(2,1)S(1)}, bf16[256,256]{1,0:T(8,128)(2,1)S(1)}, u32[]{:S(2)}, u32[]{:S(2)}) collective-permute-start(bf16[256,256]{1,0:T(8,128)(2,1)S(1)} %get-tuple-element.322), channel_id=1, source_target_pairs={{0,24},{1,25},{2,26},{3,27},{4,28},{5,29},{6,30},{7,31},{8,16},{9,... | collective-permute-start | bytes 393224 | tf_op jit(solution)/shard_map/ppermute | solution.py:53
  726.0 29.7 %collective-permute-start.89 = (bf16[256,1024]{1,0:T(8,128)(2,1)S(1)}, bf16[256,1024]{1,0:T(8,128)(2,1)S(1)}, u32[]{:S(2)}, u32[]{:S(2)}) collective-permute-start(bf16[256,1024]{1,0:T(8,128)(2,1)S(1)} %get-tuple-element.307), channel_id=1, source_target_pairs={{0,1},{1,0},{2,3},{3,2},{4,5},{5,4},{6,7},{7,6},{8,9},{9,8},{10,11... | collective-permute-start | bytes 1572872 | tf_op jit(solution)/shard_map/ppermute | solution.py:23
  765.1 49.1 %collective-permute-start.90 = (bf16[4,3,512,128]{3,2,1,0:T(8,128)(2,1)}, bf16[4,3,512,128]{3,2,1,0:T(8,128)(2,1)}, u32[]{:S(2)}, u32[]{:S(2)}) collective-permute-start(bf16[4,3,512,128]{3,2,1,0:T(8,128)(2,1)} %bitcast.251), channel_id=1, source_target_pairs={{0,2},{1,3},{2,0},{3,1},{4,6},{5,7},{6,4},{7,5},{8,10},{9,11},{10,... | collective-permute-start | bytes 4718600 | tf_op jit(solution)/shard_map/ppermute | solution.py:36
  766.5 64.6 %collective-permute-start.91 = (bf16[256,1024]{1,0:T(8,128)(2,1)S(1)}, bf16[256,1024]{1,0:T(8,128)(2,1)}, u32[]{:S(2)}, u32[]{:S(2)}) collective-permute-start(bf16[256,1024]{1,0:T(8,128)(2,1)S(1)} %get-tuple-element.210.refs_0_), channel_id=1, source_target_pairs={{0,16},{8,24},{16,0},{24,8},{1,17},{9,25},{17,1},{25,9},{2,18},{10... | collective-permute-start | bytes 1572872 | tf_op jit(solution)/shard_map/ppermute | solution.py:27
  767.3 63.8 %collective-permute-start.92 = (bf16[256,1024]{1,0:T(8,128)(2,1)S(1)}, bf16[256,1024]{1,0:T(8,128)(2,1)}, u32[]{:S(2)}, u32[]{:S(2)}) collective-permute-start(bf16[256,1024]{1,0:T(8,128)(2,1)S(1)} %collective-permute-done.89.refs_1_), channel_id=1, source_target_pairs={{0,16},{8,24},{16,0},{24,8},{1,17},{9,25},{17,1},{25,9},{2,18},{10... | collective-permute-start | bytes 1572872 | tf_op jit(solution)/shard_map/ppermute | solution.py:27
  775.6 201.7 %reduce-scatter.12.cloned.1.call-start = ((), (), s32[]{:S(2)}) async-start(), calls=%async_computation.12 | async-start | bytes 3932160 | tf_op jit(solution)/shard_map/reduce_scatter | solution.py:146
  778.4 52.7 %collective-permute-start.93 = (bf16[256,2048]{1,0:T(8,128)(2,1)}, bf16[256,2048]{1,0:T(8,128)(2,1)}, u32[]{:S(2)}, u32[]{:S(2)}) collective-permute-start(bf16[256,2048]{1,0:T(8,128)(2,1)} %get-tuple-element.301), channel_id=1, source_target_pairs={{0,1},{1,0},{2,3},{3,2},{4,5},{5,4},{6,7},{7,6},{8,9},{9,8},{10,11... | collective-permute-start | bytes 3145736 | tf_op jit(solution)/shard_map/ppermute | solution.py:23
  872.4 48.7 %collective-permute-start.102 = (bf16[256,2048]{1,0:T(8,128)(2,1)}, bf16[256,2048]{1,0:T(8,128)(2,1)S(1)}, u32[]{:S(2)}, u32[]{:S(2)}) collective-permute-start(bf16[256,2048]{1,0:T(8,128)(2,1)} %collective-permute-done.93.refs_1_), channel_id=1, source_target_pairs={{0,16},{8,24},{16,0},{24,8},{1,17},{9,25},{17,1},{25,9},{2,18},{10... | collective-permute-start | bytes 3145736 | tf_op jit(solution)/shard_map/ppermute | solution.py:27
  872.7 48.7 %collective-permute-start.101 = (bf16[256,2048]{1,0:T(8,128)(2,1)}, bf16[256,2048]{1,0:T(8,128)(2,1)S(1)}, u32[]{:S(2)}, u32[]{:S(2)}) collective-permute-start(bf16[256,2048]{1,0:T(8,128)(2,1)} %get-tuple-element.253), channel_id=1, source_target_pairs={{0,17},{1,16},{2,19},{3,18},{4,21},{5,20},{6,23},{7,22},{8,25},{9,... | collective-permute-start | bytes 3145736 | tf_op jit(solution)/shard_map/ppermute | solution.py:53
  873.4 70.1 %collective-permute-start.99 = (bf16[256,2048]{1,0:T(8,128)(2,1)}, bf16[256,2048]{1,0:T(8,128)(2,1)S(1)}, u32[]{:S(2)}, u32[]{:S(2)}) collective-permute-start(bf16[256,2048]{1,0:T(8,128)(2,1)} %get-tuple-element.254), channel_id=1, source_target_pairs={{0,16},{1,17},{2,18},{3,19},{4,20},{5,21},{6,22},{7,23},{8,24},{9,... | collective-permute-start | bytes 3145736 | tf_op jit(solution)/shard_map/ppermute | solution.py:53
  874.6 69.0 %collective-permute-start.97 = (bf16[256,2048]{1,0:T(8,128)(2,1)}, bf16[256,2048]{1,0:T(8,128)(2,1)S(1)}, u32[]{:S(2)}, u32[]{:S(2)}) collective-permute-start(bf16[256,2048]{1,0:T(8,128)(2,1)} %get-tuple-element.255), channel_id=1, source_target_pairs={{0,1},{1,0},{2,3},{3,2},{4,5},{5,4},{6,7},{7,6},{8,9},{9,8},{10,11... | collective-permute-start | bytes 3145736 | tf_op jit(solution)/shard_map/ppermute | solution.py:53
  883.8 62.5 %collective-permute-start.107 = (bf16[2,129,128]{2,1,0:T(8,128)(2,1)}, bf16[2,129,128]{2,1,0:T(8,128)(2,1)}, u32[]{:S(2)}, u32[]{:S(2)}) collective-permute-start(bf16[2,129,128]{2,1,0:T(8,128)(2,1)} %bitcast.260), channel_id=1, source_target_pairs={{0,8},{8,0},{16,24},{24,16},{1,9},{9,1},{17,25},{25,17},{2,10},{10... | collective-permute-start | bytes 198152 | tf_op jit(solution)/shard_map/ppermute | solution.py:622
  921.1 25.2 %collective-permute-start.108 = (bf16[2,129,128]{2,1,0:T(8,128)(2,1)}, bf16[2,129,128]{2,1,0:T(8,128)(2,1)S(1)}, u32[]{:S(2)}, u32[]{:S(2)}) collective-permute-start(bf16[2,129,128]{2,1,0:T(8,128)(2,1)} %bitcast.259), channel_id=1, source_target_pairs={{0,16},{8,24},{16,0},{24,8},{1,17},{9,25},{17,1},{25,9},{2,18},{10... | collective-permute-start | bytes 198152 | tf_op jit(solution)/shard_map/ppermute | solution.py:622
  921.4 24.9 %collective-permute-start.109 = (bf16[2,129,128]{2,1,0:T(8,128)(2,1)}, bf16[2,129,128]{2,1,0:T(8,128)(2,1)S(1)}, u32[]{:S(2)}, u32[]{:S(2)}) collective-permute-start(bf16[2,129,128]{2,1,0:T(8,128)(2,1)} %bitcast.258), channel_id=1, source_target_pairs={{0,24},{8,16},{16,8},{24,0},{1,25},{9,17},{17,9},{25,1},{2,26},{10... | collective-permute-start | bytes 198152 | tf_op jit(solution)/shard_map/ppermute | solution.py:622
  951.1 51.9 %collective-permute-start.132 = (bf16[256,2048]{1,0:T(8,128)(2,1)S(1)}, bf16[256,2048]{1,0:T(8,128)(2,1)}, u32[]{:S(2)}, u32[]{:S(2)}) collective-permute-start(bf16[256,2048]{1,0:T(8,128)(2,1)S(1)} %get-tuple-element.232.refs_0_), channel_id=1, source_target_pairs={{0,8},{8,0},{16,24},{24,16},{1,9},{9,1},{17,25},{25,17},{2,10},{10... | collective-permute-start | bytes 3145736 | tf_op jit(solution)/shard_map/ppermute | solution.py:31
  951.2 25.7 %collective-permute-start.114 = (bf16[256,256]{1,0:T(8,128)(2,1)}, bf16[256,256]{1,0:T(8,128)(2,1)}, u32[]{:S(2)}, u32[]{:S(2)}) collective-permute-start(bf16[256,256]{1,0:T(8,128)(2,1)} %get-tuple-element.350.refs_0_), channel_id=1, source_target_pairs={{0,16},{8,24},{16,0},{24,8},{1,17},{9,25},{17,1},{25,9},{2,18},{10... | collective-permute-start | bytes 393224 | tf_op jit(solution)/shard_map/ppermute | solution.py:27
  957.2 28.5 %collective-permute-start.111 = (bf16[4,2,129,128]{3,2,1,0:T(8,128)(2,1)}, bf16[4,2,129,128]{3,2,1,0:T(8,128)(2,1)}, u32[]{:S(2)}, u32[]{:S(2)}) collective-permute-start(bf16[4,2,129,128]{3,2,1,0:T(8,128)(2,1)} %add_convert_fusion.13), channel_id=1, source_target_pairs={{0,4},{1,5},{2,6},{3,7},{4,0},{5,1},{6,2},{7,3},{8,12},{9,13},{10,... | collective-permute-start | bytes 792584 | tf_op jit(solution)/shard_map/ppermute | solution.py:36
  983.9 26.6 %collective-permute-start.133 = (bf16[256,2048]{1,0:T(8,128)(2,1)}, bf16[256,2048]{1,0:T(8,128)(2,1)}, u32[]{:S(2)}, u32[]{:S(2)}) collective-permute-start(bf16[256,2048]{1,0:T(8,128)(2,1)} %collective-permute-done.93.refs_1_), channel_id=1, source_target_pairs={{0,8},{8,0},{16,24},{24,16},{1,9},{9,1},{17,25},{25,17},{2,10},{10... | collective-permute-start | bytes 3145736 | tf_op jit(solution)/shard_map/ppermute | solution.py:31
  984.5 26.2 %collective-permute-start.134 = (bf16[256,2048]{1,0:T(8,128)(2,1)S(1)}, bf16[256,2048]{1,0:T(8,128)(2,1)}, u32[]{:S(2)}, u32[]{:S(2)}) collective-permute-start(bf16[256,2048]{1,0:T(8,128)(2,1)S(1)} %copy-done.13), channel_id=1, source_target_pairs={{0,8},{8,0},{16,24},{24,16},{1,9},{9,1},{17,25},{25,17},{2,10},{10... | collective-permute-start | bytes 3145736 | tf_op jit(solution)/shard_map/ppermute | solution.py:31
  1003.0 28.2 %collective-permute-start.135 = (bf16[256,2048]{1,0:T(8,128)(2,1)}, bf16[256,2048]{1,0:T(8,128)(2,1)S(1)}, u32[]{:S(2)}, u32[]{:S(2)}) collective-permute-start(bf16[256,2048]{1,0:T(8,128)(2,1)} %copy-done.14), channel_id=1, source_target_pairs={{0,8},{8,0},{16,24},{24,16},{1,9},{9,1},{17,25},{25,17},{2,10},{10... | collective-permute-start | bytes 3145736 | tf_op jit(solution)/shard_map/ppermute | solution.py:31
  1010.5 30.5 %collective-permute-start.119 = (bf16[256,768]{1,0:T(8,128)(2,1)S(1)}, bf16[256,768]{1,0:T(8,128)(2,1)S(1)}, u32[]{:S(2)}, u32[]{:S(2)}) collective-permute-start(bf16[256,768]{1,0:T(8,128)(2,1)S(1)} %get-tuple-element.344.refs_0_), channel_id=1, source_target_pairs={{0,8},{8,0},{16,24},{24,16},{1,9},{9,1},{17,25},{25,17},{2,10},{10... | collective-permute-start | bytes 1179656 | tf_op jit(solution)/shard_map/ppermute | solution.py:31
  1010.6 30.4 %collective-permute-start.120 = (bf16[256,768]{1,0:T(8,128)(2,1)}, bf16[256,768]{1,0:T(8,128)(2,1)S(1)}, u32[]{:S(2)}, u32[]{:S(2)}) collective-permute-start(bf16[256,768]{1,0:T(8,128)(2,1)} %collective-permute-done.116.refs_1_), channel_id=1, source_target_pairs={{0,8},{8,0},{16,24},{24,16},{1,9},{9,1},{17,25},{25,17},{2,10},{10... | collective-permute-start | bytes 1179656 | tf_op jit(solution)/shard_map/ppermute | solution.py:31
  1015.0 26.0 %collective-permute-start.121 = (bf16[256,768]{1,0:T(8,128)(2,1)S(1)}, bf16[256,768]{1,0:T(8,128)(2,1)S(1)}, u32[]{:S(2)}, u32[]{:S(2)}) collective-permute-start(bf16[256,768]{1,0:T(8,128)(2,1)S(1)} %collective-permute-done.117.refs_2_), channel_id=1, source_target_pairs={{0,8},{8,0},{16,24},{24,16},{1,9},{9,1},{17,25},{25,17},{2,10},{10... | collective-permute-start | bytes 1179656 | tf_op jit(solution)/shard_map/ppermute | solution.py:31
  (174 other events, 2433.9 us)
Sparse Core Ops, SparseCore 0:
  26.8 81.0 all-gather.4
  187.3 82.8 all-gather.6
  289.3 82.2 all-gather.8
  373.6 79.2 all-gather.10
  478.1 75.2 reduce-scatter.5
  555.7 77.2 reduce-scatter.9
  635.3 77.2 reduce-scatter.7
  775.8 40.8 reduce-scatter.13
  842.6 61.8 reduce-scatter.11

commit v3 on v2

--- a/solution.py
+++ b/solution.py
@@ -99,7 +99,9 @@
 
 
 def exchange_group(blocks):
-    return [blocks[0]] + [send_offset(blocks[r], r) for r in range(1, GROUP)]
+    return lax.optimization_barrier(
+        [blocks[0]] + [send_offset(blocks[r], r) for r in range(1, GROUP)]
+    )
 
 
 def by_bit(pair, bit):
@@ -142,6 +144,11 @@
     return lax.all_gather(block, "wide", axis=0, tiled=True, axis_index_groups=z_lines())
 
 
+def plane_groups():
+    n = lax.axis_size("wide")
+    return [[a * n + z * 2 + x for a in range(4) for x in range(2)] for z in range(n // 2)]
+
+
 def reduce_rows(partial):
     return lax.psum_scatter(
         partial, "wide", scatter_dimension=0, tiled=True, axis_index_groups=z_lines()
@@ -180,6 +187,28 @@
 
 def spread_y(pair):
     return pair + [swap_y(p) for p in pair]
+
+
+def reorder_kernel(order, in_ref, out_ref):
+    del order
+    out_ref[...] = in_ref[...]
+
+
+def reorder(rows_by_offset, c):
+    rows, columns = rows_by_offset.shape[0] // GROUP, rows_by_offset.shape[1]
+    d = c ^ jnp.arange(GROUP, dtype=jnp.int32)
+    order = ((d >> 1) & 1) * 4 + ((d >> 2) & 1) * 2 + (d & 1)
+    return pl.pallas_call(
+        reorder_kernel,
+        grid_spec=pltpu.PrefetchScalarGridSpec(
+            num_scalar_prefetch=1,
+            grid=(GROUP,),
+            in_specs=[pl.BlockSpec((rows, columns), lambda i, o: (o[i], 0))],
+            out_specs=pl.BlockSpec((rows, columns), lambda i, o: (i, 0)),
+        ),
+        out_shape=jax.ShapeDtypeStruct(rows_by_offset.shape, rows_by_offset.dtype),
+        compiler_params=pltpu.CompilerParams(vmem_limit_bytes=24 * 2**20),
+    )(order, rows_by_offset)
 
 
 def assemble_kernel(width, place, *refs):
@@ -225,6 +254,57 @@
         out_shape=jax.ShapeDtypeStruct((rows, GROUP * width), dtype),
         compiler_params=pltpu.CompilerParams(vmem_limit_bytes=24 * 2**20),
     )(place, *[stacked] * GROUP)
+
+
+def pack_kernel(parts, where, in_ref, keep_ref, give_ref):
+    for part in range(parts):
+        keep = pl.multiple_of(part * 2 * DK + where[1] * DK, DK)
+        give = pl.multiple_of(part * 2 * DK + (1 - where[1]) * DK, DK)
+        keep_ref[0, part] = in_ref[:, pl.ds(keep, DK)]
+        give_ref[0, part] = in_ref[:, pl.ds(give, DK)]
+
+
+def pack(flat, x, zi):
+    step = flat.shape[0] // GROUP
+    parts = flat.shape[1] // (2 * DK)
+    block = pl.BlockSpec((1, parts, step, DK), lambda u, d, w: (u, 0, w[0] ^ d, 0))
+    shape = jax.ShapeDtypeStruct((4, parts, 2 * step, DK), flat.dtype)
+    return pl.pallas_call(
+        functools.partial(pack_kernel, parts),
+        grid_spec=pltpu.PrefetchScalarGridSpec(
+            num_scalar_prefetch=1,
+            grid=(4, 2),
+            in_specs=[pl.BlockSpec((step, parts * 2 * DK), lambda u, d, w: (u * 2 + d, 0))],
+            out_specs=[block, block],
+        ),
+        out_shape=[shape, shape],
+        compiler_params=pltpu.CompilerParams(vmem_limit_bytes=24 * 2**20),
+    )(jnp.stack([x, zi]).astype(jnp.int32), flat)
+
+
+def unpack_kernel(parts, where, own_ref, other_ref, out_ref):
+    for part in range(parts):
+        own = pl.multiple_of(part * 2 * DK + where[1] * DK, DK)
+        other = pl.multiple_of(part * 2 * DK + (1 - where[1]) * DK, DK)
+        out_ref[:, pl.ds(own, DK)] = own_ref[0, part]
+        out_ref[:, pl.ds(other, DK)] = other_ref[0, part]
+
+
+def unpack(own, other, x, zi):
+    units, parts, rows = own.shape[:3]
+    step = rows // 2
+    block = pl.BlockSpec((1, parts, step, DK), lambda u, d, w: (u, 0, w[0] ^ d, 0))
+    return pl.pallas_call(
+        functools.partial(unpack_kernel, parts),
+        grid_spec=pltpu.PrefetchScalarGridSpec(
+            num_scalar_prefetch=1,
+            grid=(units, 2),
+            in_specs=[block, block],
+            out_specs=pl.BlockSpec((step, parts * 2 * DK), lambda u, d, w: (u * 2 + d, 0)),
+        ),
+        out_shape=jax.ShapeDtypeStruct((units * rows, parts * 2 * DK), own.dtype),
+        compiler_params=pltpu.CompilerParams(vmem_limit_bytes=24 * 2**20),
+    )(jnp.stack([x, zi]).astype(jnp.int32), own, other)
 
 
 ROWS = 256
@@ -376,50 +456,56 @@
     normed_one = (unit_one * gain_one).astype(BF16)
     one_pieces = plane(after(normed_one, first))
 
-    gate_up_weight = after(gate_up_weight, one_pieces)
-    gate_block, _ = eighth_block([(gate_up_weight, 0, ff_cols)], x, n)
-    up_block, _ = eighth_block([(after(gate_up_weight, gate_block), FF, ff_cols)], x, n)
-    down_block, _ = eighth_block([(after(down_weight, up_block), 0, ff_cols)], x, n)
     cot = cotangent[0]
 
-    def to_units(own, other, parts):
-        def split(flat):
-            return flat.reshape(2, 2, rows_here, parts, 2, DK).transpose(1, 4, 0, 3, 2, 5)
-
-        v = jnp.stack([split(own), split(other)], axis=2)
-        v = by_bit([v[0], v[1]], x)
-        v = v.transpose(1, 2, 3, 4, 0, 5, 6).reshape(GROUP, parts, 2 * rows_here, DK)
-        blocks = []
-        for d in range(zspan):
-            block = lax.dynamic_slice_in_dim(v, (zi ^ d) * units, units, 0)
-            given = block
-            blocks.append(block if d == 0 else swap_z(block, d))
+    def to_units(flat, parts, beside=()):
+        if zspan == 2:
+            keep, given = pack(flat, x, zi)
+            blocks = [keep, swap_z(given, 1)]
+        else:
+            v = flat.reshape(2, 2, 2, rows_here, parts, 2, DK).transpose(2, 5, 0, 1, 4, 3, 6)
+            v = by_bit([v[0], v[1]], x)
+            v = v.transpose(1, 2, 3, 4, 0, 5, 6).reshape(GROUP, parts, 2 * rows_here, DK)
+            blocks = []
+            for d in range(zspan):
+                block = lax.dynamic_slice_in_dim(v, (zi ^ d) * units, units, 0)
+                given = block
+                blocks.append(block if d == 0 else swap_z(block, d))
+        if callable(beside):
+            beside = beside(given)
+        blocks, beside = lax.optimization_barrier((blocks, beside))
         v = by_index(blocks, zi)
-        return v.transpose(1, 2, 0, 3, 4).reshape(units, parts, SEG, DK), given, blocks[-1]
-
-    def from_units(v, parts):
+        return v.transpose(1, 2, 0, 3, 4).reshape(units, parts, SEG, DK), given, blocks[-1], beside
+
+    def from_units(v, parts, beside=()):
         v = v.reshape(units, parts, zspan, 2 * rows_here, DK)
         blocks = []
         for d in range(zspan):
             block = lax.dynamic_slice_in_dim(v, zi ^ d, 1, 2)[:, :, 0]
             given = block
             blocks.append(block if d == 0 else swap_z(block, d))
+        if callable(beside):
+            beside = beside(given)
+        blocks, beside = lax.optimization_barrier((blocks, beside))
+        if zspan == 2:
+            return unpack(blocks[0], blocks[1], x, zi), blocks[-1], beside
         v = by_index(blocks, zi).reshape(2, 2, 2, parts, 2, rows_here, DK)
         v = by_bit([v[:, :, :, :, 0], v[:, :, :, :, 1]], x)
         v = v.transpose(2, 3, 0, 5, 4, 1, 6)
-        return v.reshape(GROUP * rows_here, parts * head_cols), given, blocks[-1]
-
-    half = 4 * rows_here
+        return v.reshape(GROUP * rows_here, parts * head_cols), blocks[-1], beside
+
     one_all = join(both_cores(one_pieces))
-    one_all, gate_block, up_block, down_block = lax.optimization_barrier(
-        (one_all, gate_block, up_block, down_block)
-    )
     projected = dot(one_all, qkv_c).astype(BF16)
-    qkv_units, given, swapped = to_units(projected[:half], projected[half:], 3)
+
+    def late_blocks(given):
+        late_weight = after(gate_up_weight, given)
+        return [eighth_block([(late_weight, s, ff_cols)], x, n)[0] for s in (0, FF)]
+
+    qkv_units, given, swapped, (gate_block, up_block) = to_units(
+        projected, 3, late_blocks
+    )
     gate_c = gather_rows(after(gate_block, swapped))
-    out_pieces = plane(first_c[:, 3 * head_cols :])
-    qkv_units, out_pieces = lax.optimization_barrier((qkv_units, out_pieces))
-    out_full = assemble(both_cores(out_pieces), c, 1, BF16)
+    up_c = gather_rows(after(up_block, swapped))
     queries, keys, values = qkv_units[:, 0], qkv_units[:, 1], qkv_units[:, 2]
 
     head_count = max(1, units // 4)
@@ -462,12 +548,18 @@
     mixing = jax.nn.sigmoid(gate_logit[unit_heads])
     mix = mixing[:, None, None]
     attended_units = (mix * recalled + (1.0 - mix) * direct).astype(BF16)
-    attended_c, given, swapped = from_units(attended_units[:, None], 1)
-    up_c = gather_rows(after(up_block, swapped))
-    down_c = gather_rows(after(down_block, swapped))
-    attended_c, out_full = lax.optimization_barrier((attended_c, out_full))
+
+    def late_out(given):
+        out_late, down_late = after((first_c[:, 3 * head_cols :], down_weight), given)
+        return plane(out_late), eighth_block([(down_late, 0, ff_cols)], x, n)[0]
+
+    attended_c, swapped, (out_pieces, down_block) = from_units(
+        attended_units[:, None], 1, late_out
+    )
+    down_c = gather_rows(down_block)
     attended_c = attended_c.reshape(GROUP, rows_here, head_cols)
     sent = exchange_group([attended_c[r] for r in range(GROUP)])
+    out_full = assemble(both_cores(out_pieces), c, 1, BF16)
     attended = assemble_stacked(jnp.concatenate(sent, axis=0), c, BF16)
 
     middle = inputs + dot(attended, out_full)
@@ -479,7 +571,7 @@
     two_all = join(both_cores(two_pieces))
     gate_short = dot(two_all, gate_c).astype(BF16)
     up_short = dot(after(two_all, gate_short), up_c).astype(BF16)
-    cot_pieces, up_short, down_c = lax.optimization_barrier((cot_pieces, up_short, down_c))
+    cot_pieces, up_short = lax.optimization_barrier((cot_pieces, up_short))
     gate_part, up_part = gate_short.astype(F32), up_short.astype(F32)
     gate_sig = jax.nn.sigmoid(gate_part)
     activation = (gate_part * gate_sig * up_part).astype(BF16)
@@ -494,18 +586,16 @@
     grad_upper = (grad_activ * gate_part * gate_sig).astype(BF16)
     back = (dot_t(grad_gate, gate_c) + dot_t(grad_upper, up_c)).astype(BF16)
     back, att_pieces = lax.optimization_barrier((back, att_pieces))
-    back_got = scatter_sends(scatter_start(back))
     grad_gate_part = t_dot(two_all, after(grad_gate, back)).astype(BF16)
+    back_sums, grad_gate_part = lax.optimization_barrier((scatter_start(back), grad_gate_part))
+    back_got = scatter_sends(back_sums)
     grad_gate_c = reduce_rows(grad_gate_part)
     grad_up_part = t_dot(two_all, after(grad_upper, grad_gate_part)).astype(BF16)
     grad_up_c = reduce_rows(grad_up_part)
-    mlp_part = dot_t(after(activation, grad_up_part), down_c).astype(BF16)
-    att_all = join(both_cores(att_pieces))
-    mlp_sums = scatter_start(mlp_part)
-    back_got, mlp_sums, att_all, grad_down_c = lax.optimization_barrier(
-        (back_got, mlp_sums, att_all, grad_down_c)
-    )
-    mlp_got = scatter_sends(mlp_sums)
+    mlp_part = reorder(dot_t(after(activation, grad_up_part), down_c).astype(BF16), c)
+    back_got, mlp_part, grad_down_c = lax.optimization_barrier(
+        (back_got, mlp_part, grad_down_c)
+    )
     grad_normed_two = scatter_total(back_got)
     grad_gain_two = jnp.sum(grad_normed_two * unit_two, axis=0)
     grad_middle = cot.astype(F32) + norm_back(grad_normed_two * gain_two, unit_two, scale_two)
@@ -518,20 +608,25 @@
             for r in range(GROUP)
         ]
     )
-    sent, mlp_got = lax.optimization_barrier((sent, mlp_got))
-    grad_att_units, given, _ = to_units(
-        jnp.concatenate(sent[:4], axis=0), jnp.concatenate(sent[4:], axis=0), 1
-    )
-
-    late_branch, late_down = after((grad_branch, grad_down_c), given)
-    branch_pieces = exchange_group(
-        [
-            lax.dynamic_slice_in_dim(late_branch, (c ^ absolute(r)) * head_cols, head_cols, 1)
-            for r in range(GROUP)
-        ]
-    )
-    down_pair = spread_x(late_down, x)
-    grad_att_units, branch_pieces = lax.optimization_barrier((grad_att_units, branch_pieces))
+
+    def late_beside(given):
+        late_branch, late_down = after((grad_branch, grad_down_c), given)
+        pieces = exchange_group(
+            [
+                lax.dynamic_slice_in_dim(late_branch, (c ^ absolute(r)) * head_cols, head_cols, 1)
+                for r in range(GROUP)
+            ]
+        )
+        return spread_x(late_down, x), pieces
+
+    grad_att_units, _, _, (down_pair, branch_pieces) = to_units(
+        jnp.concatenate(sent, axis=0), 1, late_beside
+    )
+    mlp_out = lax.psum_scatter(
+        mlp_part, ("narrow", "wide"), scatter_dimension=0, tiled=True,
+        axis_index_groups=plane_groups(),
+    )
+    down_four = spread_y(down_pair)
     grad_att = grad_att_units[:, 0].astype(F32)
 
     unit_logit = jnp.sum(grad_att * (recalled - direct), axis=(1, 2)) * mixing * (1.0 - mixing)
@@ -553,13 +648,9 @@
     later = jnp.zeros_like(grad_read)
     for k in range(1, segments):
         later = later + lax.ppermute(
-            grad_read, "wide", [(i + k * span, i) for i in range(wide - k * span)]
-        )
-    later, dots, down_pair = lax.optimization_barrier((later / SEG, dots, down_pair))
-    down_four = spread_y(down_pair)
-    gate_up_pair = spread_x(
-        jnp.concatenate(after([grad_gate_c, grad_up_c], dots), axis=1), x
-    )
+            grad_read.astype(BF16), "wide", [(i + k * span, i) for i in range(wide - k * span)]
+        )
+    later, dots, down_four = lax.optimization_barrier((later / SEG, dots, down_four))
     grad_q_dot, grad_k_dot, grad_v_dot = dots[:, 0], dots[:, 1], dots[:, 2]
     later_mem, later_norm = later[:, :DK], later[:, DK]
     grad_lift_k = (
@@ -575,14 +666,21 @@
         ],
         axis=1,
     ).astype(BF16)
-    grad_projected, given, _ = from_units(grad_units, 3)
+    late = {}
+
+    def spread_late(given):
+        late["given"] = given
+        parts = after([grad_gate_c, grad_up_c], given)
+        return spread_x(jnp.concatenate(parts, axis=1), x)
+
+    grad_projected, _, gate_up_pair = from_units(grad_units, 3, spread_late)
+    given = late["given"]
+    att_all = join(both_cores(after(att_pieces, given)))
     grad_out_part = t_dot(
-        after(att_all, given), jnp.concatenate(branch_pieces, axis=0)
+        att_all, jnp.concatenate(branch_pieces, axis=0)
     ).astype(BF16)
     grad_out_c = reduce_rows(grad_out_part)
-    grad_projected, grad_out_part, down_four, gate_up_pair = lax.optimization_barrier(
-        (grad_projected, grad_out_part, down_four, gate_up_pair)
-    )
+    grad_projected, grad_out_part = lax.optimization_barrier((grad_projected, grad_out_part))
     grad_qkv_part = t_dot(one_all, grad_projected).astype(BF16)
     grad_qkv_c = reduce_rows(grad_qkv_part)
     one_part = dot_t(after(grad_projected, grad_qkv_part), qkv_c).astype(BF16)
@@ -592,9 +690,10 @@
     one_got = scatter_sends(one_sums)
     gate_up_four = gate_up_pair + [gate_up_y, swap_y(after(gate_up_pair[1], gate_up_y))]
     grad_down = assemble(both_cores(after(down_four, one_sums)), c, 1, F32)
-    output = (middle + scatter_total(after(mlp_got, one_sums))).astype(BF16)[None]
-    one_got, gate_up_four, grad_down, output = lax.optimization_barrier(
-        (one_got, gate_up_four, grad_down, output)
+    grad_gate_up = assemble(both_cores(after(gate_up_four, one_sums)), c, 2, F32)
+    output = (middle + after(mlp_out, one_sums).astype(F32)).astype(BF16)[None]
+    one_got, grad_down, grad_gate_up, output = lax.optimization_barrier(
+        (one_got, grad_down, grad_gate_up, output)
     )
     grad_normed_one = scatter_total(one_got)
     grad_gain_one = jnp.sum(grad_normed_one * unit_one, axis=0)
@@ -604,10 +703,9 @@
     def finish(four, parts):
         return assemble(both_cores(four), c, parts, F32)
 
-    out_four = spread_y(spread_x(after(grad_out_c, gate_up_four), x))
-    grad_gate_up = finish(gate_up_four, 2)
-    qkv_pair = spread_x(after(grad_qkv_c, out_four, grad_normed_one), x)
+    qkv_pair = spread_x(after(grad_qkv_c, grad_normed_one), x)
     qkv_four = spread_y(qkv_pair)
+    out_four = spread_y(spread_x(after(grad_out_c, qkv_pair), x))
     grad_out = finish(out_four, 1)
     grad_qkv = finish(qkv_four, 3)
 
@@ -621,7 +719,13 @@
         if flip:
             block = lax.ppermute(block, "narrow", [(i, i ^ flip) for i in range(4)])
         got.append(block)
-    mine = sum_z(by_index(after(got, grad_normed_one), n))
+    mine = by_index(after(got, grad_normed_one), n)
+    if zspan == 2 and segments == 2:
+        mine = lax.dynamic_slice_in_dim(mine, zi, 1, 1)
+        mine = (mine.astype(F32) + swap_z(mine, 2).astype(F32)).astype(BF16)
+        mine = by_bit([mine[:, 0], swap_z(mine, 1)[:, 0]], zi).transpose(1, 0, 2, 3)
+    else:
+        mine = sum_z(mine)
     heads = by_bit([mine, swap_x(mine)], x).transpose(1, 0, 2, 3, 4)
     heads = heads.reshape(H, DK + 1, DK).astype(F32)
 

time: 1060 us -> 917 us (0.87)
  waiting for transfers between devices: 495 us -> 410 us
  local copies, waits for them, and re-layouts: 90.4 us -> 54.1 us
  other arithmetic: 69.1 us -> 46.9 us
    ppermute x45 -> x42, waiting for transfers between devices: 248 us -> 178 us  [send_offset(): return lax.ppermute(v, ('narrow', 'wide'), route)]
    ppermute x8, waiting for transfers between devices: 90.6 us -> 25.3 us  [swap_z(): return lax.ppermute(v, 'wide', [(i, i ^ 2 * d) for i in range(n)])]
    ppermute x10, waiting for transfers between devices: 53 us -> 74.1 us  [swap_x(): return lax.ppermute(v, 'wide', [(i, i ^ 1) for i in range(n)])]
    reduce_scatter x5, waiting for transfers between devices: 0.01 us -> 18.6 us  [reduce_rows(): lax.psum_scatter(partial, 'wide', scatter_dimension=0, tiled=True, axis_i...]
    reshape x9 -> x0, local copies, waits for them, and re-layouts: 12.8 us -> none  [the longest x1 8.03 us: from_units(): return (v.reshape(GROUP * rows_here, parts * head_cols), given, blocks[-1])]
    unnamed x203 -> x184, local copies, waits for them, and re-layouts: 35.2 us -> 28.4 us
    ppermute x45 -> x42, starting transfers between devices: 49 us -> 49.3 us  [send_offset(): return lax.ppermute(v, ('narrow', 'wide'), route)]
  transfers between devices with their start and end apart: 145 -> 139, of which waited for: 57 -> 60; matrix products, arithmetic and copies ran while one was open for 28% -> 26% of each run, Pallas kernels for 6% -> 8%
where the time goes in v3:
time: 917 us; the launch traced here: 908 us
  waiting for transfers between devices  410 us (45%)
  matrix products  177 us (19%)
  starting transfers between devices  126 us (14%)
  Pallas kernels  77.3 us (8%)
  local copies, waits for them, and re-layouts  54.1 us (6%)
  other arithmetic  46.9 us (5%)
  between operations  16.7 us (2%)
    ppermute x42, waiting for transfers between devices, send_offset(): return lax.ppermute(v, ('narrow', 'wide'), route)  178 us
    ppermute x10, waiting for transfers between devices, swap_x(): return lax.ppermute(v, 'wide', [(i, i ^ 1) for i in range(n)])  74.1 us
    dot_general x5, matrix products, dot(): return jnp.dot(a, b, preferred_element_type=F32)  57.7 us
    dot_general x5, matrix products, dot_t(): lax.dot_general(a, b, (((1,), (1,)), ((), ())), preferred_element_type=F32)  55.7 us
    ppermute x9, waiting for transfers between devices, swap_y(): return lax.ppermute(v, 'narrow', [(i, i ^ 2) for i in range(4)])  52.8 us
    dot_general x5, matrix products, t_dot(): lax.dot_general(a, b, (((0,), (0,)), ((), ())), preferred_element_type=F32)  51.2 us
    ppermute x42, starting transfers between devices, send_offset(): return lax.ppermute(v, ('narrow', 'wide'), route)  49.3 us
    all_gather x4, waiting for transfers between devices, gather_rows(): lax.all_gather(block, 'wide', axis=0, tiled=True, axis_index_groups=z_lin...  28.7 us
  transfers between devices with their start and end apart: 139, of which 60 were waited for; matrix products, arithmetic and copies ran while one was open for 26% of the time, Pallas kernels for 8%

profile of v3, /device:TPU:0, one launch (start us, length us, event | category | flops | bytes accessed | tf_op | source)
XLA Modules:
  0.0 907.6 jit_solution(16157945401539770710)
XLA Ops:
  11.8 11.9 %collective-permute-done.7 = bf16[256,1024]{1,0:T(8,128)(2,1)S(1)} collective-permute-done((bf16[256,1024]{1,0:T(8,128)(2,1)S(1)}, bf16[256,1024]{1,0:T(8,128)(2,1)S(1)}, u32[]{:S(2)}, u32[]{:S(2)}) %collective-permute-start.7) | collective-permute-done | bytes 524320 | tf_op jit(solution)/shard_map/ppermute | solution.py:23
  25.0 3.9 collective-permute-start.5
  29.2 3.5 collective-permute-start.3
  42.3 3.9 collective-permute-done.6
  50.4 23.5 %collective-permute-done.10.refs_3_ = bf16[256,2048]{1,0:T(8,128)(2,1)S(1)} collective-permute-done((bf16[256,2048]{1,0:T(8,128)(2,1)S(1)}, bf16[256,2048]{1,0:T(8,128)(2,1)S(1)}, u32[]{:S(2)}, u32[]{:S(2)}) %collective-permute-start.10) | collective-permute-done | bytes 1048608 | tf_op jit(solution)/shard_map/ppermute | solution.py:53
  73.9 16.4 %collective-permute-done.9.refs_2_ = bf16[256,2048]{1,0:T(8,128)(2,1)S(1)} collective-permute-done((bf16[256,2048]{1,0:T(8,128)(2,1)S(1)}, bf16[256,2048]{1,0:T(8,128)(2,1)S(1)}, u32[]{:S(2)}, u32[]{:S(2)}) %collective-permute-start.9) | collective-permute-done | bytes 1048608 | tf_op jit(solution)/shard_map/ppermute | solution.py:53
  94.7 3.7 shard_map.194
  98.5 3.4 copy-done.7
  101.9 5.4 all-gather.5.cloned.1.call-done
  107.3 10.0 %convolution_convert_fusion.7.in_ref = bf16[2048,768]{1,0:T(8,128)(2,1)S(1)} fusion(bf16[2048,2048]{1,0:T(8,128)(2,1)} %copy-done.7, bf16[2048,1024]{1,0:T(8,128)(2,1)} %all-gather.5.cloned.1.call-done), kind=kOutput, calls=%fused_computation.33 | convolution fusion | flops 6444023808 | bytes 14680064 | tf_op jit(solution)/shard_map/dot_general | solution.py:394
  122.9 12.8 %collective-permute-done.17 = bf16[256,1024]{1,0:T(8,128)(2,1)S(1)} collective-permute-done((bf16[256,1024]{1,0:T(8,128)(2,1)S(1)}, bf16[256,1024]{1,0:T(8,128)(2,1)S(1)}, u32[]{:S(2)}, u32[]{:S(2)}) %collective-permute-start.17) | collective-permute-done | bytes 524320 | tf_op jit(solution)/shard_map/ppermute | solution.py:23
  136.8 9.0 collective-permute-done.16
  146.9 8.3 collective-permute-done.15
  170.6 9.0 shard_map.196
  183.6 3.6 add_convert_fusion.8
  195.0 19.0 %collective-permute-start.22 = (bf16[4,1,512,128]{3,2,1,0:T(8,128)(2,1)S(1)}, bf16[4,1,512,128]{3,2,1,0:T(8,128)(2,1)S(1)}, u32[]{:S(2)}, u32[]{:S(2)}) collective-permute-start(bf16[4,1,512,128]{3,2,1,0:T(8,128)(2,1)S(1)} %copy-done.46), channel_id=1, source_target_pairs={{0,2},{1,3},{2,0},{3,1},{4,6},{5,7},{6,4},{7,5},{8,10},{9,11},{10,... | collective-permute-start | bytes 1572872 | tf_op jit(solution)/shard_map/ppermute | solution.py:36
  214.0 34.0 %collective-permute-done.26 = bf16[256,1024]{1,0:T(8,128)(2,1)S(1)} collective-permute-done((bf16[256,1024]{1,0:T(8,128)(2,1)S(1)}, bf16[256,1024]{1,0:T(8,128)(2,1)S(1)}, u32[]{:S(2)}, u32[]{:S(2)}) %collective-permute-start.26) | collective-permute-done | bytes 524320 | tf_op jit(solution)/shard_map/ppermute | solution.py:23
  268.0 5.2 shard_map.199
  280.3 23.6 %collective-permute-done.40.refs_3_ = bf16[256,2048]{1,0:T(8,128)(2,1)} collective-permute-done((bf16[256,2048]{1,0:T(8,128)(2,1)S(1)}, bf16[256,2048]{1,0:T(8,128)(2,1)}, u32[]{:S(2)}, u32[]{:S(2)}) %collective-permute-start.40) | collective-permute-done | bytes 1048608 | tf_op jit(solution)/shard_map/ppermute | solution.py:53
  303.9 21.3 %collective-permute-done.39.refs_2_ = bf16[256,2048]{1,0:T(8,128)(2,1)} collective-permute-done((bf16[256,2048]{1,0:T(8,128)(2,1)S(1)}, bf16[256,2048]{1,0:T(8,128)(2,1)}, u32[]{:S(2)}, u32[]{:S(2)}) %collective-permute-start.39) | collective-permute-done | bytes 1048608 | tf_op jit(solution)/shard_map/ppermute | solution.py:53
  329.6 4.3 shard_map.200
  333.9 3.3 copy-done.8
  337.3 13.8 %convolution_convert_fusion.3 = bf16[2048,1024]{1,0:T(8,128)(2,1)} fusion(bf16[2048,2048]{1,0:T(8,128)(2,1)} %copy-done.8, bf16[2048,1024]{1,0:T(8,128)(2,1)} %all-gather.7.cloned.1.call-done), kind=kOutput, calls=%fused_computation.21 | convolution fusion | flops 8592031744 | bytes 16777216 | tf_op jit(solution)/shard_map/dot_general | solution.py:394
  351.0 12.9 %convolution_convert_fusion.2 = bf16[2048,1024]{1,0:T(8,128)(2,1)S(1)} fusion(bf16[2048,2048]{1,0:T(8,128)(2,1)} %copy-done.8, bf16[2048,1024]{1,0:T(8,128)(2,1)} %all-gather.9.cloned.1.call-done), kind=kOutput, calls=%fused_computation.20 | convolution fusion | flops 8592031744 | bytes 16777216 | tf_op jit(solution)/shard_map/dot_general | solution.py:394
  363.9 10.5 %collective-permute-done.42.refs_2_ = bf16[256,2048]{1,0:T(8,128)(2,1)} collective-permute-done((bf16[256,2048]{1,0:T(8,128)(2,1)S(1)}, bf16[256,2048]{1,0:T(8,128)(2,1)}, u32[]{:S(2)}, u32[]{:S(2)}) %collective-permute-start.42) | collective-permute-done | bytes 1048608 | tf_op jit(solution)/shard_map/ppermute | solution.py:53
  381.8 3.4 shard_map.201
  388.8 10.8 %convolution_convert_fusion.6 = bf16[2048,1024]{1,0:T(8,128)(2,1)} fusion(bf16[2048,2048]{1,0:T(8,128)(2,1)S(1)} %shard_map.201, bf16[2048,1024]{1,0:T(8,128)(2,1)S(1)} %fusion), kind=kOutput, calls=%fused_computation.24 | convolution fusion | flops 8592031744 | bytes 16777216 | tf_op jit(solution)/shard_map/dot_general | solution.py:402
  399.7 23.3 %all-gather.11.cloned.1.call-done = bf16[2048,1024]{1,0:T(8,128)(2,1)} async-done(((bf16[512,1024]{1,0:T(8,128)(2,1)}), bf16[2048,1024]{1,0:T(8,128)(2,1)}) %all-gather.11.cloned.1.call-update) | async-done | bytes 4194320 | tf_op jit(solution)/shard_map/all_gather | solution.py:144
  423.0 18.4 %fusion.3 = (bf16[2048,1024]{1,0:T(8,128)(2,1)}, bf16[2048,1024]{1,0:T(8,128)(2,1)S(1)}) fusion(bf16[2048,1024]{1,0:T(8,128)(2,1)} %copy-done.41, bf16[2048,1024]{1,0:T(8,128)(2,1)} %convolution_convert_fusion.3, bf16[2048,2048]{1,0:T(8,128)(2,1)} %copy-done.9, bf16[2048,1024]{1,0:T(8,128)(2,1)} %all-gather.11.cloned.1.call-done), kind=kOutput, calls=%fused_computation.11 | convolution fusion | flops 8621391872 | bytes 29360128 | tf_op jit(solution)/shard_map/dot_general | solution.py:394
  441.4 11.9 %fusion.101 = f32[2048,2048]{1,0:T(8,128)} fusion(bf16[2048,1024]{1,0:T(8,128)(2,1)S(1)} %get-tuple-element.188, bf16[2048,1024]{1,0:T(8,128)(2,1)S(1)} %copy-done.73), kind=kOutput, calls=%fused_computation.300 | convolution fusion | flops 8589934592 | bytes 25165824 | tf_op jit(solution)/shard_map/dot_general | solution.py:398
  453.3 15.7 %add_convert_fusion = bf16[2048,2048]{1,0:T(8,128)(2,1)} fusion(f32[2048,2048]{1,0:T(8,128)} %fusion.101, bf16[2048,1024]{1,0:T(8,128)(2,1)} %get-tuple-element.182, bf16[2048,1024]{1,0:T(8,128)(2,1)S(1)} %copy-done.72), kind=kOutput, calls=%fused_computation.1 | convolution fusion | flops 8598323200 | bytes 33554432 | tf_op jit(solution)/shard_map/dot_general | solution.py:398
  469.0 4.6 fusion.96
  474.7 13.1 %convolution_convert_fusion.5 = bf16[2048,1024]{1,0:T(8,128)(2,1)} fusion(bf16[2048,2048]{1,0:T(8,128)(2,1)} %copy-done.8, bf16[2048,1024]{1,0:T(8,128)(2,1)S(1)} %copy-done.77), kind=kOutput, calls=%fused_computation.23 | convolution fusion | flops 8592031744 | bytes 16777216 | tf_op jit(solution)/shard_map/dot_general | solution.py:402
  487.8 6.8 add_convert_fusion.5
  494.6 12.9 %convolution_convert_fusion.4 = bf16[2048,1024]{1,0:T(8,128)(2,1)} fusion(bf16[2048,2048]{1,0:T(8,128)(2,1)} %copy-done.8, bf16[2048,1024]{1,0:T(8,128)(2,1)S(1)} %copy-done.79), kind=kOutput, calls=%fused_computation.22 | convolution fusion | flops 8592031744 | bytes 16777216 | tf_op jit(solution)/shard_map/dot_general | solution.py:402
  511.9 12.5 %convolution_convert_fusion.1.in_ref = bf16[2048,2048]{1,0:T(8,128)(2,1)S(1)} fusion(bf16[2048,1024]{1,0:T(8,128)(2,1)} %copy-done.39, bf16[2048,1024]{1,0:T(8,128)(2,1)} %all-gather.11.cloned.1.call-done), kind=kOutput, calls=%fused_computation.19 | convolution fusion | flops 8594128896 | bytes 16777216 | tf_op jit(solution)/shard_map/dot_general | solution.py:398
  525.6 3.3 copy-done.2
  529.0 5.8 collective-permute-done.59
  534.8 22.7 %collective-permute-done.60 = bf16[256,2048]{1,0:T(8,128)(2,1)} collective-permute-done((bf16[256,2048]{1,0:T(8,128)(2,1)}, bf16[256,2048]{1,0:T(8,128)(2,1)}, u32[]{:S(2)}, u32[]{:S(2)}) %collective-permute-start.60) | collective-permute-done | bytes 1048608 | tf_op jit(solution)/shard_map/ppermute | solution.py:53
  557.6 3.5 multiply_reduce_fusion.1
  563.2 6.2 convolution_convert_fusion.10
  591.3 12.4 %collective-permute-done.77 = bf16[256,256]{1,0:T(8,128)(2,1)S(1)} collective-permute-done((bf16[256,256]{1,0:T(8,128)(2,1)S(1)}, bf16[256,256]{1,0:T(8,128)(2,1)S(1)}, u32[]{:S(2)}, u32[]{:S(2)}) %collective-permute-start.77) | collective-permute-done | bytes 131104 | tf_op jit(solution)/shard_map/ppermute | solution.py:53
  609.1 3.8 collective-permute-done.73
  625.8 15.0 %shard_map.204 = f32[4,3,1024,128]{3,2,1,0:T(8,128)} custom-call(bf16[4,3,1024,128]{3,2,1,0:T(8,128)(2,1)S(1)} %bitcast.225, bf16[4,1024,128]{2,1,0:T(8,128)(2,1)S(1)} %broadcast_multiply_fusion.grad_ref), custom_call_target="tpu_custom_call" | custom-call | flops 5368709120 | bytes 10485760 | tf_op jit(solution)/shard_map/pallas_call | solution.py:376
  640.8 4.2 collective-permute-done.78
  657.3 18.6 %reduce-scatter.9.cloned.1.call-done = bf16[512,1024]{1,0:T(8,128)(2,1)} async-done(((bf16[2048,1024]{1,0:T(8,128)(2,1)}), bf16[512,1024]{1,0:T(8,128)(2,1)}) %reduce-scatter.9.cloned.1.call-update) | async-done | bytes 1048592 | tf_op jit(solution)/shard_map/reduce_scatter | solution.py:153
  681.2 4.3 shard_map.206
  685.4 3.6 convolution_convert_fusion.9
  689.1 14.3 %collective-permute-done.81.other_ref = bf16[4,3,512,128]{3,2,1,0:T(8,128)(2,1)} collective-permute-done((bf16[4,3,512,128]{3,2,1,0:T(8,128)(2,1)}, bf16[4,3,512,128]{3,2,1,0:T(8,128)(2,1)}, u32[]{:S(2)}, u32[]{:S(2)}) %collective-permute-start.81) | collective-permute-done | bytes 1572896 | tf_op jit(solution)/shard_map/ppermute | solution.py:36
  704.7 5.0 shard_map.205
  711.4 10.7 %convolution_convert_fusion.8 = bf16[2048,768]{1,0:T(8,128)(2,1)} fusion(bf16[2048,2048]{1,0:T(8,128)(2,1)} %copy-done.7, bf16[2048,768]{1,0:T(8,128)(2,1)S(1)} %shard_map.205), kind=kOutput, calls=%fused_computation.34 | convolution fusion | flops 6444023808 | bytes 14680064 | tf_op jit(solution)/shard_map/dot_general | solution.py:402
  724.5 9.4 %convolution_convert_fusion = bf16[2048,2048]{1,0:T(8,128)(2,1)S(1)} fusion(bf16[2048,768]{1,0:T(8,128)(2,1)} %copy-done.15, bf16[2048,1024]{1,0:T(8,128)(2,1)} %all-gather.5.cloned.1.call-done), kind=kOutput, calls=%fused_computation.18 | convolution fusion | flops 6446645248 | bytes 14680064 | tf_op jit(solution)/shard_map/dot_general | solution.py:398
  734.0 27.5 %collective-permute-done.87.refs_2_ = bf16[256,2048]{1,0:T(8,128)(2,1)} collective-permute-done((bf16[256,2048]{1,0:T(8,128)(2,1)S(1)}, bf16[256,2048]{1,0:T(8,128)(2,1)}, u32[]{:S(2)}, u32[]{:S(2)}) %collective-permute-start.87) | collective-permute-done | bytes 1048608 | tf_op jit(solution)/shard_map/ppermute | solution.py:27
  769.0 3.7 add_convert_fusion.2
  772.9 15.9 %collective-permute-done.99.refs_3_ = bf16[256,2048]{1,0:T(8,128)(2,1)} collective-permute-done((bf16[256,2048]{1,0:T(8,128)(2,1)}, bf16[256,2048]{1,0:T(8,128)(2,1)}, u32[]{:S(2)}, u32[]{:S(2)}) %collective-permute-start.99) | collective-permute-done | bytes 1048608 | tf_op jit(solution)/shard_map/ppermute | solution.py:27
  790.7 3.7 collective-permute-done.96.refs_5_
  801.8 5.7 shard_map.207
  807.9 10.8 %shard_map.208 = f32[256,16384]{1,0:T(8,128)} custom-call(s32[8]{0:T(128)S(1)} %copy-done.30, bf16[256,2048]{1,0:T(8,128)(2,1)S(1)} %copy-done.13, bf16[256,2048]{1,0:T(8,128)(2,1)} %collective-permute-done.82.refs_1_, bf16[256,2048]{1,0:T(8,128)(2,1)} %collective-permute-done.87.refs_2_, bf16[256,2048]{1,0:T(8,128)(2,1)} %collective-permute-done.99.refs_3_, ...), custom_call_target="tpu_custom_call" | custom-call | tf_op jit(solution)/shard_map/pallas_call | solution.py:227
  823.9 21.7 %collective-permute-done.92 = bf16[256,2048]{1,0:T(8,128)(2,1)} collective-permute-done((bf16[256,2048]{1,0:T(8,128)(2,1)}, bf16[256,2048]{1,0:T(8,128)(2,1)}, u32[]{:S(2)}, u32[]{:S(2)}) %collective-permute-start.92) | collective-permute-done | bytes 1048608 | tf_op jit(solution)/shard_map/ppermute | solution.py:53
  845.7 4.0 fusion.26
  860.1 5.2 collective-permute-done.126
  877.4 5.4 fusion.52
  883.5 5.8 collective-permute-done.112.refs_3_
  896.7 3.7 shard_map.209
  (555 shorter events, 225.4 us)
Async XLA Ops:
  7.2 100.1 %all-gather.5.cloned.1.call-start = ((), (), s32[]{:S(2)}) async-start(), calls=%async_computation.6 | async-start | bytes 5242880 | tf_op jit(solution)/shard_map/all_gather | solution.py:144
  24.8 312.4 %all-gather.7.cloned.1.call-start = ((), (), s32[]{:S(2)}) async-start(), calls=%async_computation.7 | async-start | bytes 5242880 | tf_op jit(solution)/shard_map/all_gather | solution.py:144
  25.0 17.4 %collective-permute-start.5 = (bf16[2,256]{1,0:T(2,128)(2,1)S(1)}, bf16[2,256]{1,0:T(2,128)(2,1)S(1)}, u32[]{:S(2)}, u32[]{:S(2)}) collective-permute-start(bf16[2,256]{1,0:T(2,128)(2,1)S(1)} %get-tuple-element.289), channel_id=1, source_target_pairs={{0,6},{1,7},{2,4},{3,5},{4,2},{5,3},{6,0},{7,1},{8,14},{9,15},{10,... | collective-permute-start | bytes 3080 | tf_op jit(solution)/shard_map/ppermute | solution.py:162
  46.9 27.0 %collective-permute-start.10 = (bf16[256,2048]{1,0:T(8,128)(2,1)S(1)}, bf16[256,2048]{1,0:T(8,128)(2,1)S(1)}, u32[]{:S(2)}, u32[]{:S(2)}) collective-permute-start(bf16[256,2048]{1,0:T(8,128)(2,1)S(1)} %fusion.20.refs_0_), channel_id=1, source_target_pairs={{0,17},{1,16},{2,19},{3,18},{4,21},{5,20},{6,23},{7,22},{8,25},{9,... | collective-permute-start | bytes 3145736 | tf_op jit(solution)/shard_map/ppermute | solution.py:53
  49.3 41.0 %collective-permute-start.9 = (bf16[256,2048]{1,0:T(8,128)(2,1)S(1)}, bf16[256,2048]{1,0:T(8,128)(2,1)S(1)}, u32[]{:S(2)}, u32[]{:S(2)}) collective-permute-start(bf16[256,2048]{1,0:T(8,128)(2,1)S(1)} %fusion.20.refs_0_), channel_id=1, source_target_pairs={{0,16},{1,17},{2,18},{3,19},{4,20},{5,21},{6,22},{7,23},{8,24},{9,... | collective-permute-start | bytes 3145736 | tf_op jit(solution)/shard_map/ppermute | solution.py:53
  49.8 40.6 %collective-permute-start.8 = (bf16[256,2048]{1,0:T(8,128)(2,1)S(1)}, bf16[256,2048]{1,0:T(8,128)(2,1)}, u32[]{:S(2)}, u32[]{:S(2)}) collective-permute-start(bf16[256,2048]{1,0:T(8,128)(2,1)S(1)} %fusion.20.refs_0_), channel_id=1, source_target_pairs={{0,1},{1,0},{2,3},{3,2},{4,5},{5,4},{6,7},{7,6},{8,9},{9,8},{10,11... | collective-permute-start | bytes 3145736 | tf_op jit(solution)/shard_map/ppermute | solution.py:53
  50.4 40.5 %collective-permute-start.11 = (bf16[256,2048]{1,0:T(8,128)(2,1)S(1)}, bf16[256,2048]{1,0:T(8,128)(2,1)}, u32[]{:S(2)}, u32[]{:S(2)}) collective-permute-start(bf16[256,2048]{1,0:T(8,128)(2,1)S(1)} %fusion.20.refs_0_), channel_id=1, source_target_pairs={{0,8},{8,0},{16,24},{24,16},{1,9},{9,1},{17,25},{25,17},{2,10},{10... | collective-permute-start | bytes 3145736 | tf_op jit(solution)/shard_map/ppermute | solution.py:31
  73.9 16.9 %collective-permute-start.14 = (bf16[256,2048]{1,0:T(8,128)(2,1)S(1)}, bf16[256,2048]{1,0:T(8,128)(2,1)}, u32[]{:S(2)}, u32[]{:S(2)}) collective-permute-start(bf16[256,2048]{1,0:T(8,128)(2,1)S(1)} %collective-permute-done.10.refs_3_), channel_id=1, source_target_pairs={{0,8},{8,0},{16,24},{24,16},{1,9},{9,1},{17,25},{25,17},{2,10},{10... | collective-permute-start | bytes 3145736 | tf_op jit(solution)/shard_map/ppermute | solution.py:31
  118.9 36.3 %collective-permute-start.15 = (bf16[4,3,512,128]{3,2,1,0:T(8,128)(2,1)S(1)}, bf16[4,3,512,128]{3,2,1,0:T(8,128)(2,1)}, u32[]{:S(2)}, u32[]{:S(2)}) collective-permute-start(bf16[4,3,512,128]{3,2,1,0:T(8,128)(2,1)S(1)} %get-tuple-element.146), channel_id=1, source_target_pairs={{0,2},{1,3},{2,0},{3,1},{4,6},{5,7},{6,4},{7,5},{8,10},{9,11},{10,... | collective-permute-start | bytes 4718600 | tf_op jit(solution)/shard_map/ppermute | solution.py:36
  122.4 23.4 %collective-permute-start.16 = (bf16[256,1024]{1,0:T(8,128)(2,1)S(1)}, bf16[256,1024]{1,0:T(8,128)(2,1)S(1)}, u32[]{:S(2)}, u32[]{:S(2)}) collective-permute-start(bf16[256,1024]{1,0:T(8,128)(2,1)S(1)} %get-tuple-element.310), channel_id=1, source_target_pairs={{0,1},{1,0},{2,3},{3,2},{4,5},{5,4},{6,7},{7,6},{8,9},{9,8},{10,11... | collective-permute-start | bytes 1572872 | tf_op jit(solution)/shard_map/ppermute | solution.py:23
  155.3 195.8 %all-gather.9.cloned.1.call-start = ((), (), s32[]{:S(2)}) async-start(), calls=%async_computation.8 | async-start | bytes 5242880 | tf_op jit(solution)/shard_map/all_gather | solution.py:144
  157.0 24.4 %collective-permute-start.18 = (f32[1,129,128]{2,1,0:T(8,128)}, f32[1,129,128]{2,1,0:T(8,128)}, u32[]{:S(2)}, u32[]{:S(2)}) collective-permute-start(f32[1,129,128]{2,1,0:T(8,128)} %get-tuple-element.325), channel_id=1, source_target_pairs={{0,16},{8,24},{16,0},{24,8},{1,17},{9,25},{17,1},{25,9},{2,18},{10... | collective-permute-start | bytes 198152 | tf_op jit(solution)/shard_map/ppermute | solution.py:524
  158.5 22.9 %collective-permute-start.19 = (f32[1,129,128]{2,1,0:T(8,128)}, f32[1,129,128]{2,1,0:T(8,128)}, u32[]{:S(2)}, u32[]{:S(2)}) collective-permute-start(f32[1,129,128]{2,1,0:T(8,128)} %get-tuple-element.326), channel_id=1, source_target_pairs={{0,8},{8,0},{16,24},{24,16},{1,9},{9,1},{17,25},{25,17},{2,10},{10... | collective-permute-start | bytes 198152 | tf_op jit(solution)/shard_map/ppermute | solution.py:524
  158.5 22.9 %collective-permute-start.20 = (f32[1,129,128]{2,1,0:T(8,128)}, f32[1,129,128]{2,1,0:T(8,128)}, u32[]{:S(2)}, u32[]{:S(2)}) collective-permute-start(f32[1,129,128]{2,1,0:T(8,128)} %get-tuple-element.327), channel_id=1, source_target_pairs={{0,24},{8,16},{16,8},{24,0},{1,25},{9,17},{17,9},{25,1},{2,26},{10... | collective-permute-start | bytes 198152 | tf_op jit(solution)/shard_map/ppermute | solution.py:524
  165.5 15.9 %collective-permute-start.21 = (f32[4,129,128]{2,1,0:T(8,128)}, f32[4,129,128]{2,1,0:T(8,128)S(1)}, u32[]{:S(2)}, u32[]{:S(2)}) collective-permute-start(f32[4,129,128]{2,1,0:T(8,128)} %maximum_multiply_fusion), channel_id=1, source_target_pairs={{0,4},{1,5},{2,6},{3,7},{8,12},{9,13},{10,14},{11,15},{16,20},{17,... | collective-permute-start | bytes 792584 | tf_op jit(solution)/shard_map/ppermute | solution.py:539
  181.0 242.0 %all-gather.11.cloned.1.call-start = ((), (), s32[]{:S(2)}) async-start(), calls=%async_computation.9 | async-start | bytes 5242880 | tf_op jit(solution)/shard_map/all_gather | solution.py:144
  188.6 60.6 %collective-permute-start.25 = (bf16[2048,256]{1,0:T(8,128)(2,1)S(1)}, bf16[2048,256]{1,0:T(8,128)(2,1)S(1)}, u32[]{:S(2)}, u32[]{:S(2)}) collective-permute-start(bf16[2048,256]{1,0:T(8,128)(2,1)S(1)} %copy-done.14), channel_id=1, source_target_pairs={{0,17},{1,16},{2,19},{3,18},{4,21},{5,20},{6,23},{7,22},{8,25},{9,... | collective-permute-start | bytes 3145736 | tf_op jit(solution)/shard_map/ppermute | solution.py:53
  191.0 58.2 %collective-permute-start.24 = (bf16[2048,256]{1,0:T(8,128)(2,1)S(1)}, bf16[2048,256]{1,0:T(8,128)(2,1)}, u32[]{:S(2)}, u32[]{:S(2)}) collective-permute-start(bf16[2048,256]{1,0:T(8,128)(2,1)S(1)} %copy-done.14), channel_id=1, source_target_pairs={{0,16},{1,17},{2,18},{3,19},{4,20},{5,21},{6,22},{7,23},{8,24},{9,... | collective-permute-start | bytes 3145736 | tf_op jit(solution)/shard_map/ppermute | solution.py:53
  191.5 57.6 %collective-permute-start.23 = (bf16[2048,256]{1,0:T(8,128)(2,1)S(1)}, bf16[2048,256]{1,0:T(8,128)(2,1)}, u32[]{:S(2)}, u32[]{:S(2)}) collective-permute-start(bf16[2048,256]{1,0:T(8,128)(2,1)S(1)} %copy-done.14), channel_id=1, source_target_pairs={{0,1},{1,0},{2,3},{3,2},{4,5},{5,4},{6,7},{7,6},{8,9},{9,8},{10,11... | collective-permute-start | bytes 3145736 | tf_op jit(solution)/shard_map/ppermute | solution.py:53
  193.4 54.6 %collective-permute-start.26 = (bf16[256,1024]{1,0:T(8,128)(2,1)S(1)}, bf16[256,1024]{1,0:T(8,128)(2,1)S(1)}, u32[]{:S(2)}, u32[]{:S(2)}) collective-permute-start(bf16[256,1024]{1,0:T(8,128)(2,1)S(1)} %get-tuple-element.313), channel_id=1, source_target_pairs={{0,1},{1,0},{2,3},{3,2},{4,5},{5,4},{6,7},{7,6},{8,9},{9,8},{10,11... | collective-permute-start | bytes 1572872 | tf_op jit(solution)/shard_map/ppermute | solution.py:23
  195.0 54.2 %collective-permute-start.22 = (bf16[4,1,512,128]{3,2,1,0:T(8,128)(2,1)S(1)}, bf16[4,1,512,128]{3,2,1,0:T(8,128)(2,1)S(1)}, u32[]{:S(2)}, u32[]{:S(2)}) collective-permute-start(bf16[4,1,512,128]{3,2,1,0:T(8,128)(2,1)S(1)} %copy-done.46), channel_id=1, source_target_pairs={{0,2},{1,3},{2,0},{3,1},{4,6},{5,7},{6,4},{7,5},{8,10},{9,11},{10,... | collective-permute-start | bytes 1572872 | tf_op jit(solution)/shard_map/ppermute | solution.py:36
  276.8 27.1 %collective-permute-start.40 = (bf16[256,2048]{1,0:T(8,128)(2,1)S(1)}, bf16[256,2048]{1,0:T(8,128)(2,1)}, u32[]{:S(2)}, u32[]{:S(2)}) collective-permute-start(bf16[256,2048]{1,0:T(8,128)(2,1)S(1)} %multiply_convert_fusion.1.refs_0_), channel_id=1, source_target_pairs={{0,17},{1,16},{2,19},{3,18},{4,21},{5,20},{6,23},{7,22},{8,25},{9,... | collective-permute-start | bytes 3145736 | tf_op jit(solution)/shard_map/ppermute | solution.py:53
  277.6 47.5 %collective-permute-start.39 = (bf16[256,2048]{1,0:T(8,128)(2,1)S(1)}, bf16[256,2048]{1,0:T(8,128)(2,1)}, u32[]{:S(2)}, u32[]{:S(2)}) collective-permute-start(bf16[256,2048]{1,0:T(8,128)(2,1)S(1)} %multiply_convert_fusion.1.refs_0_), channel_id=1, source_target_pairs={{0,16},{1,17},{2,18},{3,19},{4,20},{5,21},{6,22},{7,23},{8,24},{9,... | collective-permute-start | bytes 3145736 | tf_op jit(solution)/shard_map/ppermute | solution.py:53
  278.8 46.3 %collective-permute-start.38 = (bf16[256,2048]{1,0:T(8,128)(2,1)S(1)}, bf16[256,2048]{1,0:T(8,128)(2,1)}, u32[]{:S(2)}, u32[]{:S(2)}) collective-permute-start(bf16[256,2048]{1,0:T(8,128)(2,1)S(1)} %multiply_convert_fusion.1.refs_0_), channel_id=1, source_target_pairs={{0,1},{1,0},{2,3},{3,2},{4,5},{5,4},{6,7},{7,6},{8,9},{9,8},{10,11... | collective-permute-start | bytes 3145736 | tf_op jit(solution)/shard_map/ppermute | solution.py:53
  280.3 46.7 %collective-permute-start.44 = (bf16[256,2048]{1,0:T(8,128)(2,1)S(1)}, bf16[256,2048]{1,0:T(8,128)(2,1)}, u32[]{:S(2)}, u32[]{:S(2)}) collective-permute-start(bf16[256,2048]{1,0:T(8,128)(2,1)S(1)} %multiply_convert_fusion.1.refs_0_), channel_id=1, source_target_pairs={{0,8},{8,0},{16,24},{24,16},{1,9},{9,1},{17,25},{25,17},{2,10},{10... | collective-permute-start | bytes 3145736 | tf_op jit(solution)/shard_map/ppermute | solution.py:31
  303.9 24.3 %collective-permute-start.47 = (bf16[256,2048]{1,0:T(8,128)(2,1)}, bf16[256,2048]{1,0:T(8,128)(2,1)}, u32[]{:S(2)}, u32[]{:S(2)}) collective-permute-start(bf16[256,2048]{1,0:T(8,128)(2,1)} %collective-permute-done.40.refs_3_), channel_id=1, source_target_pairs={{0,8},{8,0},{16,24},{24,16},{1,9},{9,1},{17,25},{25,17},{2,10},{10... | collective-permute-start | bytes 3145736 | tf_op jit(solution)/shard_map/ppermute | solution.py:31
  325.7 231.8 %reduce-scatter.7.cloned.1.call-start = ((), (), s32[]{:S(2)}) async-start(), calls=%async_computation.10 | async-start | bytes 5242880 | tf_op jit(solution)/shard_map/reduce_scatter | solution.py:153
  325.8 38.2 %collective-permute-start.43 = (bf16[256,2048]{1,0:T(8,128)(2,1)S(1)}, bf16[256,2048]{1,0:T(8,128)(2,1)}, u32[]{:S(2)}, u32[]{:S(2)}) collective-permute-start(bf16[256,2048]{1,0:T(8,128)(2,1)S(1)} %bitcast.229), channel_id=1, source_target_pairs={{0,17},{1,16},{2,19},{3,18},{4,21},{5,20},{6,23},{7,22},{8,25},{9,... | collective-permute-start | bytes 3145736 | tf_op jit(solution)/shard_map/ppermute | solution.py:53
  327.0 47.4 %collective-permute-start.42 = (bf16[256,2048]{1,0:T(8,128)(2,1)S(1)}, bf16[256,2048]{1,0:T(8,128)(2,1)}, u32[]{:S(2)}, u32[]{:S(2)}) collective-permute-start(bf16[256,2048]{1,0:T(8,128)(2,1)S(1)} %bitcast.230), channel_id=1, source_target_pairs={{0,16},{1,17},{2,18},{3,19},{4,20},{5,21},{6,22},{7,23},{8,24},{9,... | collective-permute-start | bytes 3145736 | tf_op jit(solution)/shard_map/ppermute | solution.py:53
  328.2 46.2 %collective-permute-start.41 = (bf16[256,2048]{1,0:T(8,128)(2,1)S(1)}, bf16[256,2048]{1,0:T(8,128)(2,1)}, u32[]{:S(2)}, u32[]{:S(2)}) collective-permute-start(bf16[256,2048]{1,0:T(8,128)(2,1)S(1)} %bitcast.231), channel_id=1, source_target_pairs={{0,1},{1,0},{2,3},{3,2},{4,5},{5,4},{6,7},{7,6},{8,9},{9,8},{10,11... | collective-permute-start | bytes 3145736 | tf_op jit(solution)/shard_map/ppermute | solution.py:53
  385.2 83.8 %collective-permute-start.54 = (bf16[256,2048]{1,0:T(8,128)(2,1)S(1)}, bf16[256,2048]{1,0:T(8,128)(2,1)}, u32[]{:S(2)}, u32[]{:S(2)}) collective-permute-start(bf16[256,2048]{1,0:T(8,128)(2,1)S(1)} %shard_map.198.refs_0_), channel_id=1, source_target_pairs={{0,17},{1,16},{2,19},{3,18},{4,21},{5,20},{6,23},{7,22},{8,25},{9,... | collective-permute-start | bytes 3145736 | tf_op jit(solution)/shard_map/ppermute | solution.py:53
  386.5 82.6 %collective-permute-start.53 = (bf16[256,2048]{1,0:T(8,128)(2,1)S(1)}, bf16[256,2048]{1,0:T(8,128)(2,1)}, u32[]{:S(2)}, u32[]{:S(2)}) collective-permute-start(bf16[256,2048]{1,0:T(8,128)(2,1)S(1)} %shard_map.198.refs_0_), channel_id=1, source_target_pairs={{0,16},{1,17},{2,18},{3,19},{4,20},{5,21},{6,22},{7,23},{8,24},{9,... | collective-permute-start | bytes 3145736 | tf_op jit(solution)/shard_map/ppermute | solution.py:53
  387.6 81.4 %collective-permute-start.52 = (bf16[256,2048]{1,0:T(8,128)(2,1)S(1)}, bf16[256,2048]{1,0:T(8,128)(2,1)}, u32[]{:S(2)}, u32[]{:S(2)}) collective-permute-start(bf16[256,2048]{1,0:T(8,128)(2,1)S(1)} %shard_map.198.refs_0_), channel_id=1, source_target_pairs={{0,1},{1,0},{2,3},{3,2},{4,5},{5,4},{6,7},{7,6},{8,9},{9,8},{10,11... | collective-permute-start | bytes 3145736 | tf_op jit(solution)/shard_map/ppermute | solution.py:53
  399.6 257.7 %reduce-scatter.11.cloned.1.call-start = ((), (), s32[]{:S(2)}) async-start(), calls=%async_computation.12 | async-start | bytes 5242880 | tf_op jit(solution)/shard_map/reduce_scatter | solution.py:153
  507.5 168.4 %reduce-scatter.9.cloned.1.call-start = ((), (), s32[]{:S(2)}) async-start(), calls=%async_computation.11 | async-start | bytes 5242880 | tf_op jit(solution)/shard_map/reduce_scatter | solution.py:153
  508.2 310.5 %reduce-scatter.13.cloned.1.call-start = ((), (), s32[]{:S(2)}) async-start(), calls=%async_computation.13 | async-start | bytes 9437184 | tf_op jit(solution)/shard_map/reduce_scatter | solution.py:625
  508.3 26.4 %collective-permute-start.59 = (bf16[256,2048]{1,0:T(8,128)(2,1)}, bf16[256,2048]{1,0:T(8,128)(2,1)}, u32[]{:S(2)}, u32[]{:S(2)}) collective-permute-start(bf16[256,2048]{1,0:T(8,128)(2,1)} %get-tuple-element.184), channel_id=1, source_target_pairs={{0,1},{1,0},{2,3},{3,2},{4,5},{5,4},{6,7},{7,6},{8,9},{9,8},{10,11... | collective-permute-start | bytes 3145736 | tf_op jit(solution)/shard_map/ppermute | solution.py:53
  509.9 47.6 %collective-permute-start.60 = (bf16[256,2048]{1,0:T(8,128)(2,1)}, bf16[256,2048]{1,0:T(8,128)(2,1)}, u32[]{:S(2)}, u32[]{:S(2)}) collective-permute-start(bf16[256,2048]{1,0:T(8,128)(2,1)} %get-tuple-element.185), channel_id=1, source_target_pairs={{0,16},{1,17},{2,18},{3,19},{4,20},{5,21},{6,22},{7,23},{8,24},{9,... | collective-permute-start | bytes 3145736 | tf_op jit(solution)/shard_map/ppermute | solution.py:53
  511.4 46.1 %collective-permute-start.61 = (bf16[256,2048]{1,0:T(8,128)(2,1)}, bf16[256,2048]{1,0:T(8,128)(2,1)}, u32[]{:S(2)}, u32[]{:S(2)}) collective-permute-start(bf16[256,2048]{1,0:T(8,128)(2,1)} %get-tuple-element.186), channel_id=1, source_target_pairs={{0,17},{1,16},{2,19},{3,18},{4,21},{5,20},{6,23},{7,22},{8,25},{9,... | collective-permute-start | bytes 3145736 | tf_op jit(solution)/shard_map/ppermute | solution.py:53
  557.5 292.1 %reduce-scatter.15.cloned.1.call-start = ((), (), s32[]{:S(2)}) async-start(), calls=%async_computation.14 | async-start | bytes 3932160 | tf_op jit(solution)/shard_map/reduce_scatter | solution.py:153
  585.4 29.3 %collective-permute-start.69 = (bf16[4,1,512,128]{3,2,1,0:T(8,128)(2,1)S(1)}, bf16[4,1,512,128]{3,2,1,0:T(8,128)(2,1)S(1)}, u32[]{:S(2)}, u32[]{:S(2)}) collective-permute-start(bf16[4,1,512,128]{3,2,1,0:T(8,128)(2,1)S(1)} %get-tuple-element.203), channel_id=1, source_target_pairs={{0,2},{1,3},{2,0},{3,1},{4,6},{5,7},{6,4},{7,5},{8,10},{9,11},{10,... | collective-permute-start | bytes 1572872 | tf_op jit(solution)/shard_map/ppermute | solution.py:36
  586.8 28.0 %collective-permute-start.70 = (bf16[256,1024]{1,0:T(8,128)(2,1)S(1)}, bf16[256,1024]{1,0:T(8,128)(2,1)S(1)}, u32[]{:S(2)}, u32[]{:S(2)}) collective-permute-start(bf16[256,1024]{1,0:T(8,128)(2,1)S(1)} %get-tuple-element.336), channel_id=1, source_target_pairs={{0,1},{1,0},{2,3},{3,2},{4,5},{5,4},{6,7},{7,6},{8,9},{9,8},{10,11... | collective-permute-start | bytes 1572872 | tf_op jit(solution)/shard_map/ppermute | solution.py:23
  589.0 16.5 %collective-permute-start.76 = (bf16[256,256]{1,0:T(8,128)(2,1)S(1)}, bf16[256,256]{1,0:T(8,128)(2,1)S(1)}, u32[]{:S(2)}, u32[]{:S(2)}) collective-permute-start(bf16[256,256]{1,0:T(8,128)(2,1)S(1)} %get-tuple-element.329), channel_id=1, source_target_pairs={{0,24},{1,25},{2,26},{3,27},{4,28},{5,29},{6,30},{7,31},{8,16},{9,... | collective-permute-start | bytes 393224 | tf_op jit(solution)/shard_map/ppermute | solution.py:53
  590.3 17.1 %collective-permute-start.75 = (bf16[256,256]{1,0:T(8,128)(2,1)S(1)}, bf16[256,256]{1,0:T(8,128)(2,1)S(1)}, u32[]{:S(2)}, u32[]{:S(2)}) collective-permute-start(bf16[256,256]{1,0:T(8,128)(2,1)S(1)} %get-tuple-element.330), channel_id=1, source_target_pairs={{0,9},{1,8},{2,11},{3,10},{4,13},{5,12},{6,15},{7,14},{8,1},{9,0},... | collective-permute-start | bytes 393224 | tf_op jit(solution)/shard_map/ppermute | solution.py:53
  614.8 30.3 %collective-permute-start.79 = (bf16[256,1024]{1,0:T(8,128)(2,1)S(1)}, bf16[256,1024]{1,0:T(8,128)(2,1)S(1)}, u32[]{:S(2)}, u32[]{:S(2)}) collective-permute-start(bf16[256,1024]{1,0:T(8,128)(2,1)S(1)} %get-tuple-element.250.refs_0_), channel_id=1, source_target_pairs={{0,16},{8,24},{16,0},{24,8},{1,17},{9,25},{17,1},{25,9},{2,18},{10... | collective-permute-start | bytes 1572872 | tf_op jit(solution)/shard_map/ppermute | solution.py:27
  615.4 29.7 %collective-permute-start.80 = (bf16[256,1024]{1,0:T(8,128)(2,1)S(1)}, bf16[256,1024]{1,0:T(8,128)(2,1)}, u32[]{:S(2)}, u32[]{:S(2)}) collective-permute-start(bf16[256,1024]{1,0:T(8,128)(2,1)S(1)} %collective-permute-done.70.refs_1_), channel_id=1, source_target_pairs={{0,16},{8,24},{16,0},{24,8},{1,17},{9,25},{17,1},{25,9},{2,18},{10... | collective-permute-start | bytes 1572872 | tf_op jit(solution)/shard_map/ppermute | solution.py:27
  624.2 20.8 %collective-permute-start.78 = (bf16[4,129,128]{2,1,0:T(8,128)(2,1)S(1)}, bf16[4,129,128]{2,1,0:T(8,128)(2,1)S(1)}, u32[]{:S(2)}, u32[]{:S(2)}) collective-permute-start(bf16[4,129,128]{2,1,0:T(8,128)(2,1)S(1)} %pad_maximum_fusion.2), channel_id=1, source_target_pairs={{4,0},{5,1},{6,2},{7,3},{12,8},{13,9},{14,10},{15,11},{20,16},{21,... | collective-permute-start | bytes 396296 | tf_op jit(solution)/shard_map/ppermute | solution.py:650
  655.2 23.8 %collective-permute-start.83 = (bf16[256,2048]{1,0:T(8,128)(2,1)S(1)}, bf16[256,2048]{1,0:T(8,128)(2,1)}, u32[]{:S(2)}, u32[]{:S(2)}) collective-permute-start(bf16[256,2048]{1,0:T(8,128)(2,1)S(1)} %copy-done.11), channel_id=1, source_target_pairs={{0,8},{8,0},{16,24},{24,16},{1,9},{9,1},{17,25},{25,17},{2,10},{10... | collective-permute-start | bytes 3145736 | tf_op jit(solution)/shard_map/ppermute | solution.py:31
  655.2 25.9 %collective-permute-start.84 = (bf16[256,2048]{1,0:T(8,128)(2,1)}, bf16[256,2048]{1,0:T(8,128)(2,1)}, u32[]{:S(2)}, u32[]{:S(2)}) collective-permute-start(bf16[256,2048]{1,0:T(8,128)(2,1)} %collective-permute-done.52.refs_1_), channel_id=1, source_target_pairs={{0,8},{8,0},{16,24},{24,16},{1,9},{9,1},{17,25},{25,17},{2,10},{10... | collective-permute-start | bytes 3145736 | tf_op jit(solution)/shard_map/ppermute | solution.py:31
  655.8 25.3 %collective-permute-start.85 = (bf16[256,2048]{1,0:T(8,128)(2,1)}, bf16[256,2048]{1,0:T(8,128)(2,1)}, u32[]{:S(2)}, u32[]{:S(2)}) collective-permute-start(bf16[256,2048]{1,0:T(8,128)(2,1)} %collective-permute-done.53.refs_2_), channel_id=1, source_target_pairs={{0,8},{8,0},{16,24},{24,16},{1,9},{9,1},{17,25},{25,17},{2,10},{10... | collective-permute-start | bytes 3145736 | tf_op jit(solution)/shard_map/ppermute | solution.py:31
  655.9 25.3 %collective-permute-start.86 = (bf16[256,2048]{1,0:T(8,128)(2,1)}, bf16[256,2048]{1,0:T(8,128)(2,1)}, u32[]{:S(2)}, u32[]{:S(2)}) collective-permute-start(bf16[256,2048]{1,0:T(8,128)(2,1)} %collective-permute-done.54.refs_3_), channel_id=1, source_target_pairs={{0,8},{8,0},{16,24},{24,16},{1,9},{9,1},{17,25},{25,17},{2,10},{10... | collective-permute-start | bytes 3145736 | tf_op jit(solution)/shard_map/ppermute | solution.py:31
  657.3 46.1 %collective-permute-start.81 = (bf16[4,3,512,128]{3,2,1,0:T(8,128)(2,1)}, bf16[4,3,512,128]{3,2,1,0:T(8,128)(2,1)}, u32[]{:S(2)}, u32[]{:S(2)}) collective-permute-start(bf16[4,3,512,128]{3,2,1,0:T(8,128)(2,1)} %bitcast.211), channel_id=1, source_target_pairs={{0,2},{1,3},{2,0},{3,1},{4,6},{5,7},{6,4},{7,5},{8,10},{9,11},{10,... | collective-permute-start | bytes 4718600 | tf_op jit(solution)/shard_map/ppermute | solution.py:36
  679.0 25.7 %collective-permute-start.82 = (bf16[256,2048]{1,0:T(8,128)(2,1)}, bf16[256,2048]{1,0:T(8,128)(2,1)}, u32[]{:S(2)}, u32[]{:S(2)}) collective-permute-start(bf16[256,2048]{1,0:T(8,128)(2,1)} %get-tuple-element.322), channel_id=1, source_target_pairs={{0,1},{1,0},{2,3},{3,2},{4,5},{5,4},{6,7},{7,6},{8,9},{9,8},{10,11... | collective-permute-start | bytes 3145736 | tf_op jit(solution)/shard_map/ppermute | solution.py:23
  722.1 145.3 %reduce-scatter.17.cloned.1.call-start = ((), (), s32[]{:S(2)}) async-start(), calls=%async_computation.15 | async-start | bytes 1310720 | tf_op jit(solution)/shard_map/reduce_scatter | solution.py:153
  723.4 38.1 %collective-permute-start.87 = (bf16[256,2048]{1,0:T(8,128)(2,1)S(1)}, bf16[256,2048]{1,0:T(8,128)(2,1)}, u32[]{:S(2)}, u32[]{:S(2)}) collective-permute-start(bf16[256,2048]{1,0:T(8,128)(2,1)S(1)} %copy-done.13), channel_id=1, source_target_pairs={{0,16},{8,24},{16,0},{24,8},{1,17},{9,25},{17,1},{25,9},{2,18},{10... | collective-permute-start | bytes 3145736 | tf_op jit(solution)/shard_map/ppermute | solution.py:27
  762.9 25.9 %collective-permute-start.99 = (bf16[256,2048]{1,0:T(8,128)(2,1)}, bf16[256,2048]{1,0:T(8,128)(2,1)}, u32[]{:S(2)}, u32[]{:S(2)}) collective-permute-start(bf16[256,2048]{1,0:T(8,128)(2,1)} %collective-permute-done.82.refs_1_), channel_id=1, source_target_pairs={{0,16},{8,24},{16,0},{24,8},{1,17},{9,25},{17,1},{25,9},{2,18},{10... | collective-permute-start | bytes 3145736 | tf_op jit(solution)/shard_map/ppermute | solution.py:27
  772.8 17.1 %collective-permute-start.95 = (bf16[256,1024]{1,0:T(8,128)(2,1)S(1)}, bf16[256,1024]{1,0:T(8,128)(2,1)S(1)}, u32[]{:S(2)}, u32[]{:S(2)}) collective-permute-start(bf16[256,1024]{1,0:T(8,128)(2,1)S(1)} %get-tuple-element.250.refs_0_), channel_id=1, source_target_pairs={{0,8},{8,0},{16,24},{24,16},{1,9},{9,1},{17,25},{25,17},{2,10},{10... | collective-permute-start | bytes 1572872 | tf_op jit(solution)/shard_map/ppermute | solution.py:31
  796.6 27.3 %collective-permute-start.94 = (bf16[256,2048]{1,0:T(8,128)(2,1)}, bf16[256,2048]{1,0:T(8,128)(2,1)}, u32[]{:S(2)}, u32[]{:S(2)}) collective-permute-start(bf16[256,2048]{1,0:T(8,128)(2,1)} %get-tuple-element.292), channel_id=1, source_target_pairs={{0,17},{1,16},{2,19},{3,18},{4,21},{5,20},{6,23},{7,22},{8,25},{9,... | collective-permute-start | bytes 3145736 | tf_op jit(solution)/shard_map/ppermute | solution.py:53
  798.1 47.5 %collective-permute-start.92 = (bf16[256,2048]{1,0:T(8,128)(2,1)}, bf16[256,2048]{1,0:T(8,128)(2,1)}, u32[]{:S(2)}, u32[]{:S(2)}) collective-permute-start(bf16[256,2048]{1,0:T(8,128)(2,1)} %get-tuple-element.293), channel_id=1, source_target_pairs={{0,16},{1,17},{2,18},{3,19},{4,20},{5,21},{6,22},{7,23},{8,24},{9,... | collective-permute-start | bytes 3145736 | tf_op jit(solution)/shard_map/ppermute | solution.py:53
  799.6 46.0 %collective-permute-start.90 = (bf16[256,2048]{1,0:T(8,128)(2,1)}, bf16[256,2048]{1,0:T(8,128)(2,1)}, u32[]{:S(2)}, u32[]{:S(2)}) collective-permute-start(bf16[256,2048]{1,0:T(8,128)(2,1)} %get-tuple-element.294), channel_id=1, source_target_pairs={{0,1},{1,0},{2,3},{3,2},{4,5},{5,4},{6,7},{7,6},{8,9},{9,8},{10,11... | collective-permute-start | bytes 3145736 | tf_op jit(solution)/shard_map/ppermute | solution.py:53
  807.5 42.2 %collective-permute-start.104 = (bf16[2,129,128]{2,1,0:T(8,128)(2,1)}, bf16[2,129,128]{2,1,0:T(8,128)(2,1)S(1)}, u32[]{:S(2)}, u32[]{:S(2)}) collective-permute-start(bf16[2,129,128]{2,1,0:T(8,128)(2,1)} %bitcast.216), channel_id=1, source_target_pairs={{0,8},{8,0},{16,24},{24,16},{1,9},{9,1},{17,25},{25,17},{2,10},{10... | collective-permute-start | bytes 198152 | tf_op jit(solution)/shard_map/ppermute | solution.py:720
  807.5 42.1 %collective-permute-start.105 = (bf16[2,129,128]{2,1,0:T(8,128)(2,1)S(1)}, bf16[2,129,128]{2,1,0:T(8,128)(2,1)S(1)}, u32[]{:S(2)}, u32[]{:S(2)}) collective-permute-start(bf16[2,129,128]{2,1,0:T(8,128)(2,1)S(1)} %bitcast.269), channel_id=1, source_target_pairs={{0,16},{8,24},{16,0},{24,8},{1,17},{9,25},{17,1},{25,9},{2,18},{10... | collective-permute-start | bytes 198152 | tf_op jit(solution)/shard_map/ppermute | solution.py:720
  823.9 25.8 %collective-permute-start.106 = (bf16[2,129,128]{2,1,0:T(8,128)(2,1)S(1)}, bf16[2,129,128]{2,1,0:T(8,128)(2,1)S(1)}, u32[]{:S(2)}, u32[]{:S(2)}) collective-permute-start(bf16[2,129,128]{2,1,0:T(8,128)(2,1)S(1)} %bitcast.268), channel_id=1, source_target_pairs={{0,24},{8,16},{16,8},{24,0},{1,25},{9,17},{17,9},{25,1},{2,26},{10... | collective-permute-start | bytes 198152 | tf_op jit(solution)/shard_map/ppermute | solution.py:720
  859.5 15.8 %collective-permute-start.111 = (bf16[256,768]{1,0:T(8,128)(2,1)S(1)}, bf16[256,768]{1,0:T(8,128)(2,1)S(1)}, u32[]{:S(2)}, u32[]{:S(2)}) collective-permute-start(bf16[256,768]{1,0:T(8,128)(2,1)S(1)} %get-tuple-element.359.refs_0_), channel_id=1, source_target_pairs={{0,16},{8,24},{16,0},{24,8},{1,17},{9,25},{17,1},{25,9},{2,18},{10... | collective-permute-start | bytes 1179656 | tf_op jit(solution)/shard_map/ppermute | solution.py:27
  (155 other events, 1895.6 us)
Sparse Core Ops, SparseCore 0:
  25.0 82.2 all-gather.4
  155.4 92.5 all-gather.6
  250.1 81.2 all-gather.8
  333.4 89.5 all-gather.10
  425.1 75.2 reduce-scatter.6
  507.6 75.0 reduce-scatter.10
  585.5 90.3 reduce-scatter.8
  679.7 88.1 reduce-scatter.12
  770.3 60.3 reduce-scatter.14
  832.8 29.7 reduce-scatter.16

commit v4 on v3

--- a/solution.py
+++ b/solution.py
@@ -671,9 +671,10 @@
     def spread_late(given):
         late["given"] = given
         parts = after([grad_gate_c, grad_up_c], given)
-        return spread_x(jnp.concatenate(parts, axis=1), x)
-
-    grad_projected, _, gate_up_pair = from_units(grad_units, 3, spread_late)
+        pair = spread_x(jnp.concatenate(parts, axis=1), x)
+        return pair, swap_y(pair[0])
+
+    grad_projected, _, (gate_up_pair, gate_up_y) = from_units(grad_units, 3, spread_late)
     given = late["given"]
     att_all = join(both_cores(after(att_pieces, given)))
     grad_out_part = t_dot(
@@ -684,11 +685,11 @@
     grad_qkv_part = t_dot(one_all, grad_projected).astype(BF16)
     grad_qkv_c = reduce_rows(grad_qkv_part)
     one_part = dot_t(after(grad_projected, grad_qkv_part), qkv_c).astype(BF16)
-    gate_up_y = swap_y(gate_up_pair[0])
-    one_part, gate_up_y = lax.optimization_barrier((one_part, gate_up_y))
+    gate_up_last = swap_y(gate_up_pair[1])
+    one_part, gate_up_last = lax.optimization_barrier((one_part, gate_up_last))
     one_sums = scatter_start(one_part)
     one_got = scatter_sends(one_sums)
-    gate_up_four = gate_up_pair + [gate_up_y, swap_y(after(gate_up_pair[1], gate_up_y))]
+    gate_up_four = gate_up_pair + [gate_up_y, gate_up_last]
     grad_down = assemble(both_cores(after(down_four, one_sums)), c, 1, F32)
     grad_gate_up = assemble(both_cores(after(gate_up_four, one_sums)), c, 2, F32)
     output = (middle + after(mlp_out, one_sums).astype(F32)).astype(BF16)[None]

time: 917 us -> 915 us (level)
    ppermute x9, waiting for transfers between devices: 52.8 us -> 37.6 us  [swap_y(): return lax.ppermute(v, 'narrow', [(i, i ^ 2) for i in range(4)])]
    reduce_scatter x5, waiting for transfers between devices: 18.6 us -> 30.1 us  [reduce_rows(): lax.psum_scatter(partial, 'wide', scatter_dimension=0, tiled=True, axis_i...]
    unnamed x184 -> x182, local copies, waits for them, and re-layouts: 28.4 us -> 27.2 us
  transfers between devices with their start and end apart: 139 -> 139, of which waited for: 60 -> 64; matrix products, arithmetic and copies ran while one was open for 26% -> 27% of each run, Pallas kernels for 8% -> 8%
where the time goes in v4:
time: 915 us; the launch traced here: 905 us
  waiting for transfers between devices  407 us (44%)
  matrix products  177 us (19%)
  starting transfers between devices  126 us (14%)
  Pallas kernels  77.5 us (8%)
  local copies, waits for them, and re-layouts  52.9 us (6%)
  other arithmetic  46.9 us (5%)
  between operations  16.7 us (2%)
    ppermute x42, waiting for transfers between devices, send_offset(): return lax.ppermute(v, ('narrow', 'wide'), route)  178 us
    ppermute x10, waiting for transfers between devices, swap_x(): return lax.ppermute(v, 'wide', [(i, i ^ 1) for i in range(n)])  74.1 us
    dot_general x5, matrix products, dot(): return jnp.dot(a, b, preferred_element_type=F32)  57.7 us
    dot_general x5, matrix products, dot_t(): lax.dot_general(a, b, (((1,), (1,)), ((), ())), preferred_element_type=F32)  55.7 us
    dot_general x5, matrix products, t_dot(): lax.dot_general(a, b, (((0,), (0,)), ((), ())), preferred_element_type=F32)  51.4 us
    ppermute x42, starting transfers between devices, send_offset(): return lax.ppermute(v, ('narrow', 'wide'), route)  49.2 us
    ppermute x9, waiting for transfers between devices, swap_y(): return lax.ppermute(v, 'narrow', [(i, i ^ 2) for i in range(4)])  37.6 us
    reduce_scatter x5, waiting for transfers between devices, reduce_rows(): lax.psum_scatter(partial, 'wide', scatter_dimension=0, tiled=True, axis_i...  30.1 us
  transfers between devices with their start and end apart: 139, of which 64 were waited for; matrix products, arithmetic and copies ran while one was open for 27% of the time, Pallas kernels for 8%

profile of v4, /device:TPU:0, one launch (start us, length us, event | category | flops | bytes accessed | tf_op | source)
XLA Modules:
  0.0 904.8 jit_solution(246173837861138714)
XLA Ops:
  11.8 11.9 %collective-permute-done.7 = bf16[256,1024]{1,0:T(8,128)(2,1)S(1)} collective-permute-done((bf16[256,1024]{1,0:T(8,128)(2,1)S(1)}, bf16[256,1024]{1,0:T(8,128)(2,1)S(1)}, u32[]{:S(2)}, u32[]{:S(2)}) %collective-permute-start.7) | collective-permute-done | bytes 524320 | tf_op jit(solution)/shard_map/ppermute | solution.py:23
  25.0 3.9 collective-permute-start.5
  29.2 3.5 collective-permute-start.3
  42.3 3.9 collective-permute-done.6
  50.4 23.5 %collective-permute-done.10.refs_3_ = bf16[256,2048]{1,0:T(8,128)(2,1)S(1)} collective-permute-done((bf16[256,2048]{1,0:T(8,128)(2,1)S(1)}, bf16[256,2048]{1,0:T(8,128)(2,1)S(1)}, u32[]{:S(2)}, u32[]{:S(2)}) %collective-permute-start.10) | collective-permute-done | bytes 1048608 | tf_op jit(solution)/shard_map/ppermute | solution.py:53
  73.9 16.4 %collective-permute-done.9.refs_2_ = bf16[256,2048]{1,0:T(8,128)(2,1)S(1)} collective-permute-done((bf16[256,2048]{1,0:T(8,128)(2,1)S(1)}, bf16[256,2048]{1,0:T(8,128)(2,1)S(1)}, u32[]{:S(2)}, u32[]{:S(2)}) %collective-permute-start.9) | collective-permute-done | bytes 1048608 | tf_op jit(solution)/shard_map/ppermute | solution.py:53
  94.7 3.7 shard_map.194
  98.5 3.4 copy-done.7
  101.9 5.4 all-gather.5.cloned.1.call-done
  107.3 10.0 %convolution_convert_fusion.7.in_ref = bf16[2048,768]{1,0:T(8,128)(2,1)S(1)} fusion(bf16[2048,2048]{1,0:T(8,128)(2,1)} %copy-done.7, bf16[2048,1024]{1,0:T(8,128)(2,1)} %all-gather.5.cloned.1.call-done), kind=kOutput, calls=%fused_computation.33 | convolution fusion | flops 6444023808 | bytes 14680064 | tf_op jit(solution)/shard_map/dot_general | solution.py:394
  122.9 12.8 %collective-permute-done.17 = bf16[256,1024]{1,0:T(8,128)(2,1)S(1)} collective-permute-done((bf16[256,1024]{1,0:T(8,128)(2,1)S(1)}, bf16[256,1024]{1,0:T(8,128)(2,1)S(1)}, u32[]{:S(2)}, u32[]{:S(2)}) %collective-permute-start.17) | collective-permute-done | bytes 524320 | tf_op jit(solution)/shard_map/ppermute | solution.py:23
  136.8 9.0 collective-permute-done.16
  146.9 8.3 collective-permute-done.15
  170.6 9.0 shard_map.196
  183.6 3.6 add_convert_fusion.8
  194.9 19.1 %collective-permute-start.22 = (bf16[4,1,512,128]{3,2,1,0:T(8,128)(2,1)S(1)}, bf16[4,1,512,128]{3,2,1,0:T(8,128)(2,1)S(1)}, u32[]{:S(2)}, u32[]{:S(2)}) collective-permute-start(bf16[4,1,512,128]{3,2,1,0:T(8,128)(2,1)S(1)} %copy-done.45), channel_id=1, source_target_pairs={{0,2},{1,3},{2,0},{3,1},{4,6},{5,7},{6,4},{7,5},{8,10},{9,11},{10,... | collective-permute-start | bytes 1572872 | tf_op jit(solution)/shard_map/ppermute | solution.py:36
  214.0 34.0 %collective-permute-done.26 = bf16[256,1024]{1,0:T(8,128)(2,1)S(1)} collective-permute-done((bf16[256,1024]{1,0:T(8,128)(2,1)S(1)}, bf16[256,1024]{1,0:T(8,128)(2,1)S(1)}, u32[]{:S(2)}, u32[]{:S(2)}) %collective-permute-start.26) | collective-permute-done | bytes 524320 | tf_op jit(solution)/shard_map/ppermute | solution.py:23
  268.0 5.2 shard_map.199
  280.3 23.6 %collective-permute-done.40.refs_3_ = bf16[256,2048]{1,0:T(8,128)(2,1)} collective-permute-done((bf16[256,2048]{1,0:T(8,128)(2,1)S(1)}, bf16[256,2048]{1,0:T(8,128)(2,1)}, u32[]{:S(2)}, u32[]{:S(2)}) %collective-permute-start.40) | collective-permute-done | bytes 1048608 | tf_op jit(solution)/shard_map/ppermute | solution.py:53
  303.8 21.3 %collective-permute-done.39.refs_2_ = bf16[256,2048]{1,0:T(8,128)(2,1)} collective-permute-done((bf16[256,2048]{1,0:T(8,128)(2,1)S(1)}, bf16[256,2048]{1,0:T(8,128)(2,1)}, u32[]{:S(2)}, u32[]{:S(2)}) %collective-permute-start.39) | collective-permute-done | bytes 1048608 | tf_op jit(solution)/shard_map/ppermute | solution.py:53
  329.6 4.3 shard_map.200
  333.9 3.3 copy-done.8
  337.2 13.8 %convolution_convert_fusion.3 = bf16[2048,1024]{1,0:T(8,128)(2,1)} fusion(bf16[2048,2048]{1,0:T(8,128)(2,1)} %copy-done.8, bf16[2048,1024]{1,0:T(8,128)(2,1)} %all-gather.7.cloned.1.call-done), kind=kOutput, calls=%fused_computation.21 | convolution fusion | flops 8592031744 | bytes 16777216 | tf_op jit(solution)/shard_map/dot_general | solution.py:394
  351.0 12.9 %convolution_convert_fusion.2 = bf16[2048,1024]{1,0:T(8,128)(2,1)S(1)} fusion(bf16[2048,2048]{1,0:T(8,128)(2,1)} %copy-done.8, bf16[2048,1024]{1,0:T(8,128)(2,1)} %all-gather.9.cloned.1.call-done), kind=kOutput, calls=%fused_computation.20 | convolution fusion | flops 8592031744 | bytes 16777216 | tf_op jit(solution)/shard_map/dot_general | solution.py:394
  363.9 10.5 %collective-permute-done.42.refs_2_ = bf16[256,2048]{1,0:T(8,128)(2,1)} collective-permute-done((bf16[256,2048]{1,0:T(8,128)(2,1)S(1)}, bf16[256,2048]{1,0:T(8,128)(2,1)}, u32[]{:S(2)}, u32[]{:S(2)}) %collective-permute-start.42) | collective-permute-done | bytes 1048608 | tf_op jit(solution)/shard_map/ppermute | solution.py:53
  381.8 3.4 shard_map.201
  388.7 10.9 %convolution_convert_fusion.6 = bf16[2048,1024]{1,0:T(8,128)(2,1)} fusion(bf16[2048,2048]{1,0:T(8,128)(2,1)S(1)} %shard_map.201, bf16[2048,1024]{1,0:T(8,128)(2,1)S(1)} %fusion), kind=kOutput, calls=%fused_computation.24 | convolution fusion | flops 8592031744 | bytes 16777216 | tf_op jit(solution)/shard_map/dot_general | solution.py:402
  399.7 23.2 %all-gather.11.cloned.1.call-done = bf16[2048,1024]{1,0:T(8,128)(2,1)} async-done(((bf16[512,1024]{1,0:T(8,128)(2,1)}), bf16[2048,1024]{1,0:T(8,128)(2,1)}) %all-gather.11.cloned.1.call-update) | async-done | bytes 4194320 | tf_op jit(solution)/shard_map/all_gather | solution.py:144
  422.9 18.4 %fusion.3 = (bf16[2048,1024]{1,0:T(8,128)(2,1)}, bf16[2048,1024]{1,0:T(8,128)(2,1)S(1)}) fusion(bf16[2048,1024]{1,0:T(8,128)(2,1)} %copy-done.40, bf16[2048,1024]{1,0:T(8,128)(2,1)} %convolution_convert_fusion.3, bf16[2048,2048]{1,0:T(8,128)(2,1)} %copy-done.9, bf16[2048,1024]{1,0:T(8,128)(2,1)} %all-gather.11.cloned.1.call-done), kind=kOutput, calls=%fused_computation.11 | convolution fusion | flops 8621391872 | bytes 29360128 | tf_op jit(solution)/shard_map/dot_general | solution.py:394
  441.4 11.9 %fusion.101 = f32[2048,2048]{1,0:T(8,128)} fusion(bf16[2048,1024]{1,0:T(8,128)(2,1)S(1)} %get-tuple-element.188, bf16[2048,1024]{1,0:T(8,128)(2,1)S(1)} %copy-done.72), kind=kOutput, calls=%fused_computation.300 | convolution fusion | flops 8589934592 | bytes 25165824 | tf_op jit(solution)/shard_map/dot_general | solution.py:398
  453.2 15.7 %add_convert_fusion = bf16[2048,2048]{1,0:T(8,128)(2,1)} fusion(f32[2048,2048]{1,0:T(8,128)} %fusion.101, bf16[2048,1024]{1,0:T(8,128)(2,1)} %get-tuple-element.182, bf16[2048,1024]{1,0:T(8,128)(2,1)S(1)} %copy-done.71), kind=kOutput, calls=%fused_computation.1 | convolution fusion | flops 8598323200 | bytes 33554432 | tf_op jit(solution)/shard_map/dot_general | solution.py:398
  469.0 4.6 fusion.96
  474.6 13.1 %convolution_convert_fusion.5 = bf16[2048,1024]{1,0:T(8,128)(2,1)} fusion(bf16[2048,2048]{1,0:T(8,128)(2,1)} %copy-done.8, bf16[2048,1024]{1,0:T(8,128)(2,1)S(1)} %copy-done.76), kind=kOutput, calls=%fused_computation.23 | convolution fusion | flops 8592031744 | bytes 16777216 | tf_op jit(solution)/shard_map/dot_general | solution.py:402
  487.8 6.8 add_convert_fusion.5
  494.6 12.9 %convolution_convert_fusion.4 = bf16[2048,1024]{1,0:T(8,128)(2,1)} fusion(bf16[2048,2048]{1,0:T(8,128)(2,1)} %copy-done.8, bf16[2048,1024]{1,0:T(8,128)(2,1)S(1)} %copy-done.78), kind=kOutput, calls=%fused_computation.22 | convolution fusion | flops 8592031744 | bytes 16777216 | tf_op jit(solution)/shard_map/dot_general | solution.py:402
  511.9 12.5 %convolution_convert_fusion.1.in_ref = bf16[2048,2048]{1,0:T(8,128)(2,1)S(1)} fusion(bf16[2048,1024]{1,0:T(8,128)(2,1)} %copy-done.38, bf16[2048,1024]{1,0:T(8,128)(2,1)} %all-gather.11.cloned.1.call-done), kind=kOutput, calls=%fused_computation.19 | convolution fusion | flops 8594128896 | bytes 16777216 | tf_op jit(solution)/shard_map/dot_general | solution.py:398
  525.6 3.3 copy-done.2
  528.9 5.8 collective-permute-done.59
  534.7 22.7 %collective-permute-done.60 = bf16[256,2048]{1,0:T(8,128)(2,1)} collective-permute-done((bf16[256,2048]{1,0:T(8,128)(2,1)}, bf16[256,2048]{1,0:T(8,128)(2,1)}, u32[]{:S(2)}, u32[]{:S(2)}) %collective-permute-start.60) | collective-permute-done | bytes 1048608 | tf_op jit(solution)/shard_map/ppermute | solution.py:53
  557.6 3.5 multiply_reduce_fusion.1
  563.2 6.2 convolution_convert_fusion.10
  591.3 12.4 %collective-permute-done.77 = bf16[256,256]{1,0:T(8,128)(2,1)S(1)} collective-permute-done((bf16[256,256]{1,0:T(8,128)(2,1)S(1)}, bf16[256,256]{1,0:T(8,128)(2,1)S(1)}, u32[]{:S(2)}, u32[]{:S(2)}) %collective-permute-start.77) | collective-permute-done | bytes 131104 | tf_op jit(solution)/shard_map/ppermute | solution.py:53
  609.0 3.8 collective-permute-done.73
  625.8 15.0 %shard_map.204 = f32[4,3,1024,128]{3,2,1,0:T(8,128)} custom-call(bf16[4,3,1024,128]{3,2,1,0:T(8,128)(2,1)S(1)} %bitcast.225, bf16[4,1024,128]{2,1,0:T(8,128)(2,1)S(1)} %broadcast_multiply_fusion.grad_ref), custom_call_target="tpu_custom_call" | custom-call | flops 5368709120 | bytes 10485760 | tf_op jit(solution)/shard_map/pallas_call | solution.py:376
  640.8 4.2 collective-permute-done.78
  657.3 18.6 %reduce-scatter.9.cloned.1.call-done = bf16[512,1024]{1,0:T(8,128)(2,1)} async-done(((bf16[2048,1024]{1,0:T(8,128)(2,1)}), bf16[512,1024]{1,0:T(8,128)(2,1)}) %reduce-scatter.9.cloned.1.call-update) | async-done | bytes 1048592 | tf_op jit(solution)/shard_map/reduce_scatter | solution.py:153
  681.1 4.3 shard_map.206
  685.4 3.6 convolution_convert_fusion.9
  689.1 14.3 %collective-permute-done.81.other_ref = bf16[4,3,512,128]{3,2,1,0:T(8,128)(2,1)} collective-permute-done((bf16[4,3,512,128]{3,2,1,0:T(8,128)(2,1)}, bf16[4,3,512,128]{3,2,1,0:T(8,128)(2,1)}, u32[]{:S(2)}, u32[]{:S(2)}) %collective-permute-start.81) | collective-permute-done | bytes 1572896 | tf_op jit(solution)/shard_map/ppermute | solution.py:36
  706.1 5.0 shard_map.205
  712.8 11.0 %convolution_convert_fusion.8 = bf16[2048,768]{1,0:T(8,128)(2,1)} fusion(bf16[2048,2048]{1,0:T(8,128)(2,1)} %copy-done.7, bf16[2048,768]{1,0:T(8,128)(2,1)S(1)} %shard_map.205), kind=kOutput, calls=%fused_computation.34 | convolution fusion | flops 6444023808 | bytes 14680064 | tf_op jit(solution)/shard_map/dot_general | solution.py:402
  723.9 9.4 %convolution_convert_fusion = bf16[2048,2048]{1,0:T(8,128)(2,1)S(1)} fusion(bf16[2048,768]{1,0:T(8,128)(2,1)} %copy-done.14, bf16[2048,1024]{1,0:T(8,128)(2,1)} %all-gather.5.cloned.1.call-done), kind=kOutput, calls=%fused_computation.18 | convolution fusion | flops 6446645248 | bytes 14680064 | tf_op jit(solution)/shard_map/dot_general | solution.py:398
  733.3 27.5 %collective-permute-done.88.refs_3_ = bf16[256,2048]{1,0:T(8,128)(2,1)S(1)} collective-permute-done((bf16[256,2048]{1,0:T(8,128)(2,1)}, bf16[256,2048]{1,0:T(8,128)(2,1)S(1)}, u32[]{:S(2)}, u32[]{:S(2)}) %collective-permute-start.88) | collective-permute-done | bytes 1048608 | tf_op jit(solution)/shard_map/ppermute | solution.py:27
  768.3 3.7 add_convert_fusion.2
  784.8 5.7 shard_map.207
  790.6 10.9 %shard_map.208 = f32[256,16384]{1,0:T(8,128)} custom-call(s32[8]{0:T(128)S(1)} %copy-done.29, bf16[256,2048]{1,0:T(8,128)(2,1)} %get-tuple-element.257.refs_0_, bf16[256,2048]{1,0:T(8,128)(2,1)} %collective-permute-done.82.refs_1_, bf16[256,2048]{1,0:T(8,128)(2,1)} %collective-permute-done.83.refs_2_, bf16[256,2048]{1,0:T(8,128)(2,1)S(1)} %collective-permute-done.88.refs_3_, ...), custom_call_target="tpu_custom_call" | custom-call | tf_op jit(solution)/shard_map/pallas_call | solution.py:227
  801.6 3.3 fusion.51
  806.8 21.7 %collective-permute-done.93 = bf16[256,2048]{1,0:T(8,128)(2,1)} collective-permute-done((bf16[256,2048]{1,0:T(8,128)(2,1)}, bf16[256,2048]{1,0:T(8,128)(2,1)}, u32[]{:S(2)}, u32[]{:S(2)}) %collective-permute-start.93) | collective-permute-done | bytes 1048608 | tf_op jit(solution)/shard_map/ppermute | solution.py:53
  828.6 4.0 fusion.26
  842.8 5.3 collective-permute-done.126
  852.1 11.6 %reduce-scatter.17.cloned.1.call-done = bf16[512,256]{1,0:T(8,128)(2,1)} async-done(((bf16[2048,256]{1,0:T(8,128)(2,1)}), bf16[512,256]{1,0:T(8,128)(2,1)}) %reduce-scatter.17.cloned.1.call-update) | async-done | bytes 262160 | tf_op jit(solution)/shard_map/reduce_scatter | solution.py:153
  875.3 5.4 fusion.52
  881.4 4.8 collective-permute-done.112.refs_3_
  893.9 3.7 shard_map.209
  (553 shorter events, 227.9 us)
Async XLA Ops:
  7.2 100.1 %all-gather.5.cloned.1.call-start = ((), (), s32[]{:S(2)}) async-start(), calls=%async_computation.6 | async-start | bytes 5242880 | tf_op jit(solution)/shard_map/all_gather | solution.py:144
  24.8 312.4 %all-gather.7.cloned.1.call-start = ((), (), s32[]{:S(2)}) async-start(), calls=%async_computation.7 | async-start | bytes 5242880 | tf_op jit(solution)/shard_map/all_gather | solution.py:144
  25.0 17.4 %collective-permute-start.5 = (bf16[2,256]{1,0:T(2,128)(2,1)S(1)}, bf16[2,256]{1,0:T(2,128)(2,1)S(1)}, u32[]{:S(2)}, u32[]{:S(2)}) collective-permute-start(bf16[2,256]{1,0:T(2,128)(2,1)S(1)} %get-tuple-element.289), channel_id=1, source_target_pairs={{0,6},{1,7},{2,4},{3,5},{4,2},{5,3},{6,0},{7,1},{8,14},{9,15},{10,... | collective-permute-start | bytes 3080 | tf_op jit(solution)/shard_map/ppermute | solution.py:162
  46.9 27.0 %collective-permute-start.10 = (bf16[256,2048]{1,0:T(8,128)(2,1)S(1)}, bf16[256,2048]{1,0:T(8,128)(2,1)S(1)}, u32[]{:S(2)}, u32[]{:S(2)}) collective-permute-start(bf16[256,2048]{1,0:T(8,128)(2,1)S(1)} %fusion.20.refs_0_), channel_id=1, source_target_pairs={{0,17},{1,16},{2,19},{3,18},{4,21},{5,20},{6,23},{7,22},{8,25},{9,... | collective-permute-start | bytes 3145736 | tf_op jit(solution)/shard_map/ppermute | solution.py:53
  49.3 41.0 %collective-permute-start.9 = (bf16[256,2048]{1,0:T(8,128)(2,1)S(1)}, bf16[256,2048]{1,0:T(8,128)(2,1)S(1)}, u32[]{:S(2)}, u32[]{:S(2)}) collective-permute-start(bf16[256,2048]{1,0:T(8,128)(2,1)S(1)} %fusion.20.refs_0_), channel_id=1, source_target_pairs={{0,16},{1,17},{2,18},{3,19},{4,20},{5,21},{6,22},{7,23},{8,24},{9,... | collective-permute-start | bytes 3145736 | tf_op jit(solution)/shard_map/ppermute | solution.py:53
  49.8 40.6 %collective-permute-start.8 = (bf16[256,2048]{1,0:T(8,128)(2,1)S(1)}, bf16[256,2048]{1,0:T(8,128)(2,1)}, u32[]{:S(2)}, u32[]{:S(2)}) collective-permute-start(bf16[256,2048]{1,0:T(8,128)(2,1)S(1)} %fusion.20.refs_0_), channel_id=1, source_target_pairs={{0,1},{1,0},{2,3},{3,2},{4,5},{5,4},{6,7},{7,6},{8,9},{9,8},{10,11... | collective-permute-start | bytes 3145736 | tf_op jit(solution)/shard_map/ppermute | solution.py:53
  50.4 40.5 %collective-permute-start.11 = (bf16[256,2048]{1,0:T(8,128)(2,1)S(1)}, bf16[256,2048]{1,0:T(8,128)(2,1)}, u32[]{:S(2)}, u32[]{:S(2)}) collective-permute-start(bf16[256,2048]{1,0:T(8,128)(2,1)S(1)} %fusion.20.refs_0_), channel_id=1, source_target_pairs={{0,8},{8,0},{16,24},{24,16},{1,9},{9,1},{17,25},{25,17},{2,10},{10... | collective-permute-start | bytes 3145736 | tf_op jit(solution)/shard_map/ppermute | solution.py:31
  73.9 16.9 %collective-permute-start.14 = (bf16[256,2048]{1,0:T(8,128)(2,1)S(1)}, bf16[256,2048]{1,0:T(8,128)(2,1)}, u32[]{:S(2)}, u32[]{:S(2)}) collective-permute-start(bf16[256,2048]{1,0:T(8,128)(2,1)S(1)} %collective-permute-done.10.refs_3_), channel_id=1, source_target_pairs={{0,8},{8,0},{16,24},{24,16},{1,9},{9,1},{17,25},{25,17},{2,10},{10... | collective-permute-start | bytes 3145736 | tf_op jit(solution)/shard_map/ppermute | solution.py:31
  118.9 36.3 %collective-permute-start.15 = (bf16[4,3,512,128]{3,2,1,0:T(8,128)(2,1)S(1)}, bf16[4,3,512,128]{3,2,1,0:T(8,128)(2,1)}, u32[]{:S(2)}, u32[]{:S(2)}) collective-permute-start(bf16[4,3,512,128]{3,2,1,0:T(8,128)(2,1)S(1)} %get-tuple-element.146), channel_id=1, source_target_pairs={{0,2},{1,3},{2,0},{3,1},{4,6},{5,7},{6,4},{7,5},{8,10},{9,11},{10,... | collective-permute-start | bytes 4718600 | tf_op jit(solution)/shard_map/ppermute | solution.py:36
  122.4 23.4 %collective-permute-start.16 = (bf16[256,1024]{1,0:T(8,128)(2,1)S(1)}, bf16[256,1024]{1,0:T(8,128)(2,1)S(1)}, u32[]{:S(2)}, u32[]{:S(2)}) collective-permute-start(bf16[256,1024]{1,0:T(8,128)(2,1)S(1)} %get-tuple-element.310), channel_id=1, source_target_pairs={{0,1},{1,0},{2,3},{3,2},{4,5},{5,4},{6,7},{7,6},{8,9},{9,8},{10,11... | collective-permute-start | bytes 1572872 | tf_op jit(solution)/shard_map/ppermute | solution.py:23
  155.3 195.7 %all-gather.9.cloned.1.call-start = ((), (), s32[]{:S(2)}) async-start(), calls=%async_computation.8 | async-start | bytes 5242880 | tf_op jit(solution)/shard_map/all_gather | solution.py:144
  157.0 24.3 %collective-permute-start.18 = (f32[1,129,128]{2,1,0:T(8,128)}, f32[1,129,128]{2,1,0:T(8,128)}, u32[]{:S(2)}, u32[]{:S(2)}) collective-permute-start(f32[1,129,128]{2,1,0:T(8,128)} %get-tuple-element.325), channel_id=1, source_target_pairs={{0,16},{8,24},{16,0},{24,8},{1,17},{9,25},{17,1},{25,9},{2,18},{10... | collective-permute-start | bytes 198152 | tf_op jit(solution)/shard_map/ppermute | solution.py:524
  158.5 22.9 %collective-permute-start.19 = (f32[1,129,128]{2,1,0:T(8,128)}, f32[1,129,128]{2,1,0:T(8,128)}, u32[]{:S(2)}, u32[]{:S(2)}) collective-permute-start(f32[1,129,128]{2,1,0:T(8,128)} %get-tuple-element.326), channel_id=1, source_target_pairs={{0,8},{8,0},{16,24},{24,16},{1,9},{9,1},{17,25},{25,17},{2,10},{10... | collective-permute-start | bytes 198152 | tf_op jit(solution)/shard_map/ppermute | solution.py:524
  158.5 22.9 %collective-permute-start.20 = (f32[1,129,128]{2,1,0:T(8,128)}, f32[1,129,128]{2,1,0:T(8,128)}, u32[]{:S(2)}, u32[]{:S(2)}) collective-permute-start(f32[1,129,128]{2,1,0:T(8,128)} %get-tuple-element.327), channel_id=1, source_target_pairs={{0,24},{8,16},{16,8},{24,0},{1,25},{9,17},{17,9},{25,1},{2,26},{10... | collective-permute-start | bytes 198152 | tf_op jit(solution)/shard_map/ppermute | solution.py:524
  180.9 242.0 %all-gather.11.cloned.1.call-start = ((), (), s32[]{:S(2)}) async-start(), calls=%async_computation.9 | async-start | bytes 5242880 | tf_op jit(solution)/shard_map/all_gather | solution.py:144
  188.6 60.6 %collective-permute-start.25 = (bf16[2048,256]{1,0:T(8,128)(2,1)S(1)}, bf16[2048,256]{1,0:T(8,128)(2,1)S(1)}, u32[]{:S(2)}, u32[]{:S(2)}) collective-permute-start(bf16[2048,256]{1,0:T(8,128)(2,1)S(1)} %copy-done.13), channel_id=1, source_target_pairs={{0,17},{1,16},{2,19},{3,18},{4,21},{5,20},{6,23},{7,22},{8,25},{9,... | collective-permute-start | bytes 3145736 | tf_op jit(solution)/shard_map/ppermute | solution.py:53
  190.9 58.2 %collective-permute-start.24 = (bf16[2048,256]{1,0:T(8,128)(2,1)S(1)}, bf16[2048,256]{1,0:T(8,128)(2,1)}, u32[]{:S(2)}, u32[]{:S(2)}) collective-permute-start(bf16[2048,256]{1,0:T(8,128)(2,1)S(1)} %copy-done.13), channel_id=1, source_target_pairs={{0,16},{1,17},{2,18},{3,19},{4,20},{5,21},{6,22},{7,23},{8,24},{9,... | collective-permute-start | bytes 3145736 | tf_op jit(solution)/shard_map/ppermute | solution.py:53
  191.5 57.7 %collective-permute-start.23 = (bf16[2048,256]{1,0:T(8,128)(2,1)S(1)}, bf16[2048,256]{1,0:T(8,128)(2,1)}, u32[]{:S(2)}, u32[]{:S(2)}) collective-permute-start(bf16[2048,256]{1,0:T(8,128)(2,1)S(1)} %copy-done.13), channel_id=1, source_target_pairs={{0,1},{1,0},{2,3},{3,2},{4,5},{5,4},{6,7},{7,6},{8,9},{9,8},{10,11... | collective-permute-start | bytes 3145736 | tf_op jit(solution)/shard_map/ppermute | solution.py:53
  193.4 54.6 %collective-permute-start.26 = (bf16[256,1024]{1,0:T(8,128)(2,1)S(1)}, bf16[256,1024]{1,0:T(8,128)(2,1)S(1)}, u32[]{:S(2)}, u32[]{:S(2)}) collective-permute-start(bf16[256,1024]{1,0:T(8,128)(2,1)S(1)} %get-tuple-element.313), channel_id=1, source_target_pairs={{0,1},{1,0},{2,3},{3,2},{4,5},{5,4},{6,7},{7,6},{8,9},{9,8},{10,11... | collective-permute-start | bytes 1572872 | tf_op jit(solution)/shard_map/ppermute | solution.py:23
  194.9 54.2 %collective-permute-start.22 = (bf16[4,1,512,128]{3,2,1,0:T(8,128)(2,1)S(1)}, bf16[4,1,512,128]{3,2,1,0:T(8,128)(2,1)S(1)}, u32[]{:S(2)}, u32[]{:S(2)}) collective-permute-start(bf16[4,1,512,128]{3,2,1,0:T(8,128)(2,1)S(1)} %copy-done.45), channel_id=1, source_target_pairs={{0,2},{1,3},{2,0},{3,1},{4,6},{5,7},{6,4},{7,5},{8,10},{9,11},{10,... | collective-permute-start | bytes 1572872 | tf_op jit(solution)/shard_map/ppermute | solution.py:36
  276.7 27.1 %collective-permute-start.40 = (bf16[256,2048]{1,0:T(8,128)(2,1)S(1)}, bf16[256,2048]{1,0:T(8,128)(2,1)}, u32[]{:S(2)}, u32[]{:S(2)}) collective-permute-start(bf16[256,2048]{1,0:T(8,128)(2,1)S(1)} %multiply_convert_fusion.1.refs_0_), channel_id=1, source_target_pairs={{0,17},{1,16},{2,19},{3,18},{4,21},{5,20},{6,23},{7,22},{8,25},{9,... | collective-permute-start | bytes 3145736 | tf_op jit(solution)/shard_map/ppermute | solution.py:53
  277.6 47.5 %collective-permute-start.39 = (bf16[256,2048]{1,0:T(8,128)(2,1)S(1)}, bf16[256,2048]{1,0:T(8,128)(2,1)}, u32[]{:S(2)}, u32[]{:S(2)}) collective-permute-start(bf16[256,2048]{1,0:T(8,128)(2,1)S(1)} %multiply_convert_fusion.1.refs_0_), channel_id=1, source_target_pairs={{0,16},{1,17},{2,18},{3,19},{4,20},{5,21},{6,22},{7,23},{8,24},{9,... | collective-permute-start | bytes 3145736 | tf_op jit(solution)/shard_map/ppermute | solution.py:53
  278.8 46.3 %collective-permute-start.38 = (bf16[256,2048]{1,0:T(8,128)(2,1)S(1)}, bf16[256,2048]{1,0:T(8,128)(2,1)}, u32[]{:S(2)}, u32[]{:S(2)}) collective-permute-start(bf16[256,2048]{1,0:T(8,128)(2,1)S(1)} %multiply_convert_fusion.1.refs_0_), channel_id=1, source_target_pairs={{0,1},{1,0},{2,3},{3,2},{4,5},{5,4},{6,7},{7,6},{8,9},{9,8},{10,11... | collective-permute-start | bytes 3145736 | tf_op jit(solution)/shard_map/ppermute | solution.py:53
  280.3 46.7 %collective-permute-start.44 = (bf16[256,2048]{1,0:T(8,128)(2,1)S(1)}, bf16[256,2048]{1,0:T(8,128)(2,1)}, u32[]{:S(2)}, u32[]{:S(2)}) collective-permute-start(bf16[256,2048]{1,0:T(8,128)(2,1)S(1)} %multiply_convert_fusion.1.refs_0_), channel_id=1, source_target_pairs={{0,8},{8,0},{16,24},{24,16},{1,9},{9,1},{17,25},{25,17},{2,10},{10... | collective-permute-start | bytes 3145736 | tf_op jit(solution)/shard_map/ppermute | solution.py:31
  303.8 24.3 %collective-permute-start.47 = (bf16[256,2048]{1,0:T(8,128)(2,1)}, bf16[256,2048]{1,0:T(8,128)(2,1)}, u32[]{:S(2)}, u32[]{:S(2)}) collective-permute-start(bf16[256,2048]{1,0:T(8,128)(2,1)} %collective-permute-done.40.refs_3_), channel_id=1, source_target_pairs={{0,8},{8,0},{16,24},{24,16},{1,9},{9,1},{17,25},{25,17},{2,10},{10... | collective-permute-start | bytes 3145736 | tf_op jit(solution)/shard_map/ppermute | solution.py:31
  325.7 231.8 %reduce-scatter.7.cloned.1.call-start = ((), (), s32[]{:S(2)}) async-start(), calls=%async_computation.10 | async-start | bytes 5242880 | tf_op jit(solution)/shard_map/reduce_scatter | solution.py:153
  325.7 38.2 %collective-permute-start.43 = (bf16[256,2048]{1,0:T(8,128)(2,1)S(1)}, bf16[256,2048]{1,0:T(8,128)(2,1)}, u32[]{:S(2)}, u32[]{:S(2)}) collective-permute-start(bf16[256,2048]{1,0:T(8,128)(2,1)S(1)} %bitcast.229), channel_id=1, source_target_pairs={{0,17},{1,16},{2,19},{3,18},{4,21},{5,20},{6,23},{7,22},{8,25},{9,... | collective-permute-start | bytes 3145736 | tf_op jit(solution)/shard_map/ppermute | solution.py:53
  327.0 47.4 %collective-permute-start.42 = (bf16[256,2048]{1,0:T(8,128)(2,1)S(1)}, bf16[256,2048]{1,0:T(8,128)(2,1)}, u32[]{:S(2)}, u32[]{:S(2)}) collective-permute-start(bf16[256,2048]{1,0:T(8,128)(2,1)S(1)} %bitcast.230), channel_id=1, source_target_pairs={{0,16},{1,17},{2,18},{3,19},{4,20},{5,21},{6,22},{7,23},{8,24},{9,... | collective-permute-start | bytes 3145736 | tf_op jit(solution)/shard_map/ppermute | solution.py:53
  328.2 46.2 %collective-permute-start.41 = (bf16[256,2048]{1,0:T(8,128)(2,1)S(1)}, bf16[256,2048]{1,0:T(8,128)(2,1)}, u32[]{:S(2)}, u32[]{:S(2)}) collective-permute-start(bf16[256,2048]{1,0:T(8,128)(2,1)S(1)} %bitcast.231), channel_id=1, source_target_pairs={{0,1},{1,0},{2,3},{3,2},{4,5},{5,4},{6,7},{7,6},{8,9},{9,8},{10,11... | collective-permute-start | bytes 3145736 | tf_op jit(solution)/shard_map/ppermute | solution.py:53
  385.2 83.8 %collective-permute-start.54 = (bf16[256,2048]{1,0:T(8,128)(2,1)S(1)}, bf16[256,2048]{1,0:T(8,128)(2,1)}, u32[]{:S(2)}, u32[]{:S(2)}) collective-permute-start(bf16[256,2048]{1,0:T(8,128)(2,1)S(1)} %shard_map.198.refs_0_), channel_id=1, source_target_pairs={{0,17},{1,16},{2,19},{3,18},{4,21},{5,20},{6,23},{7,22},{8,25},{9,... | collective-permute-start | bytes 3145736 | tf_op jit(solution)/shard_map/ppermute | solution.py:53
  386.4 82.5 %collective-permute-start.53 = (bf16[256,2048]{1,0:T(8,128)(2,1)S(1)}, bf16[256,2048]{1,0:T(8,128)(2,1)}, u32[]{:S(2)}, u32[]{:S(2)}) collective-permute-start(bf16[256,2048]{1,0:T(8,128)(2,1)S(1)} %shard_map.198.refs_0_), channel_id=1, source_target_pairs={{0,16},{1,17},{2,18},{3,19},{4,20},{5,21},{6,22},{7,23},{8,24},{9,... | collective-permute-start | bytes 3145736 | tf_op jit(solution)/shard_map/ppermute | solution.py:53
  387.6 81.4 %collective-permute-start.52 = (bf16[256,2048]{1,0:T(8,128)(2,1)S(1)}, bf16[256,2048]{1,0:T(8,128)(2,1)}, u32[]{:S(2)}, u32[]{:S(2)}) collective-permute-start(bf16[256,2048]{1,0:T(8,128)(2,1)S(1)} %shard_map.198.refs_0_), channel_id=1, source_target_pairs={{0,1},{1,0},{2,3},{3,2},{4,5},{5,4},{6,7},{7,6},{8,9},{9,8},{10,11... | collective-permute-start | bytes 3145736 | tf_op jit(solution)/shard_map/ppermute | solution.py:53
  399.6 257.7 %reduce-scatter.11.cloned.1.call-start = ((), (), s32[]{:S(2)}) async-start(), calls=%async_computation.12 | async-start | bytes 5242880 | tf_op jit(solution)/shard_map/reduce_scatter | solution.py:153
  507.5 168.4 %reduce-scatter.9.cloned.1.call-start = ((), (), s32[]{:S(2)}) async-start(), calls=%async_computation.11 | async-start | bytes 5242880 | tf_op jit(solution)/shard_map/reduce_scatter | solution.py:153
  508.2 293.4 %reduce-scatter.13.cloned.1.call-start = ((), (), s32[]{:S(2)}) async-start(), calls=%async_computation.13 | async-start | bytes 9437184 | tf_op jit(solution)/shard_map/reduce_scatter | solution.py:625
  508.3 26.4 %collective-permute-start.59 = (bf16[256,2048]{1,0:T(8,128)(2,1)}, bf16[256,2048]{1,0:T(8,128)(2,1)}, u32[]{:S(2)}, u32[]{:S(2)}) collective-permute-start(bf16[256,2048]{1,0:T(8,128)(2,1)} %get-tuple-element.184), channel_id=1, source_target_pairs={{0,1},{1,0},{2,3},{3,2},{4,5},{5,4},{6,7},{7,6},{8,9},{9,8},{10,11... | collective-permute-start | bytes 3145736 | tf_op jit(solution)/shard_map/ppermute | solution.py:53
  509.9 47.6 %collective-permute-start.60 = (bf16[256,2048]{1,0:T(8,128)(2,1)}, bf16[256,2048]{1,0:T(8,128)(2,1)}, u32[]{:S(2)}, u32[]{:S(2)}) collective-permute-start(bf16[256,2048]{1,0:T(8,128)(2,1)} %get-tuple-element.185), channel_id=1, source_target_pairs={{0,16},{1,17},{2,18},{3,19},{4,20},{5,21},{6,22},{7,23},{8,24},{9,... | collective-permute-start | bytes 3145736 | tf_op jit(solution)/shard_map/ppermute | solution.py:53
  511.4 46.1 %collective-permute-start.61 = (bf16[256,2048]{1,0:T(8,128)(2,1)}, bf16[256,2048]{1,0:T(8,128)(2,1)}, u32[]{:S(2)}, u32[]{:S(2)}) collective-permute-start(bf16[256,2048]{1,0:T(8,128)(2,1)} %get-tuple-element.186), channel_id=1, source_target_pairs={{0,17},{1,16},{2,19},{3,18},{4,21},{5,20},{6,23},{7,22},{8,25},{9,... | collective-permute-start | bytes 3145736 | tf_op jit(solution)/shard_map/ppermute | solution.py:53
  557.5 275.1 %reduce-scatter.15.cloned.1.call-start = ((), (), s32[]{:S(2)}) async-start(), calls=%async_computation.14 | async-start | bytes 3932160 | tf_op jit(solution)/shard_map/reduce_scatter | solution.py:153
  585.4 29.4 %collective-permute-start.69 = (bf16[4,1,512,128]{3,2,1,0:T(8,128)(2,1)S(1)}, bf16[4,1,512,128]{3,2,1,0:T(8,128)(2,1)S(1)}, u32[]{:S(2)}, u32[]{:S(2)}) collective-permute-start(bf16[4,1,512,128]{3,2,1,0:T(8,128)(2,1)S(1)} %get-tuple-element.203), channel_id=1, source_target_pairs={{0,2},{1,3},{2,0},{3,1},{4,6},{5,7},{6,4},{7,5},{8,10},{9,11},{10,... | collective-permute-start | bytes 1572872 | tf_op jit(solution)/shard_map/ppermute | solution.py:36
  586.7 28.0 %collective-permute-start.70 = (bf16[256,1024]{1,0:T(8,128)(2,1)S(1)}, bf16[256,1024]{1,0:T(8,128)(2,1)S(1)}, u32[]{:S(2)}, u32[]{:S(2)}) collective-permute-start(bf16[256,1024]{1,0:T(8,128)(2,1)S(1)} %get-tuple-element.336), channel_id=1, source_target_pairs={{0,1},{1,0},{2,3},{3,2},{4,5},{5,4},{6,7},{7,6},{8,9},{9,8},{10,11... | collective-permute-start | bytes 1572872 | tf_op jit(solution)/shard_map/ppermute | solution.py:23
  590.2 17.1 %collective-permute-start.75 = (bf16[256,256]{1,0:T(8,128)(2,1)S(1)}, bf16[256,256]{1,0:T(8,128)(2,1)S(1)}, u32[]{:S(2)}, u32[]{:S(2)}) collective-permute-start(bf16[256,256]{1,0:T(8,128)(2,1)S(1)} %get-tuple-element.330), channel_id=1, source_target_pairs={{0,9},{1,8},{2,11},{3,10},{4,13},{5,12},{6,15},{7,14},{8,1},{9,0},... | collective-permute-start | bytes 393224 | tf_op jit(solution)/shard_map/ppermute | solution.py:53
  614.7 30.3 %collective-permute-start.79 = (bf16[256,1024]{1,0:T(8,128)(2,1)S(1)}, bf16[256,1024]{1,0:T(8,128)(2,1)S(1)}, u32[]{:S(2)}, u32[]{:S(2)}) collective-permute-start(bf16[256,1024]{1,0:T(8,128)(2,1)S(1)} %get-tuple-element.250.refs_0_), channel_id=1, source_target_pairs={{0,16},{8,24},{16,0},{24,8},{1,17},{9,25},{17,1},{25,9},{2,18},{10... | collective-permute-start | bytes 1572872 | tf_op jit(solution)/shard_map/ppermute | solution.py:27
  615.4 29.7 %collective-permute-start.80 = (bf16[256,1024]{1,0:T(8,128)(2,1)S(1)}, bf16[256,1024]{1,0:T(8,128)(2,1)}, u32[]{:S(2)}, u32[]{:S(2)}) collective-permute-start(bf16[256,1024]{1,0:T(8,128)(2,1)S(1)} %collective-permute-done.70.refs_1_), channel_id=1, source_target_pairs={{0,16},{8,24},{16,0},{24,8},{1,17},{9,25},{17,1},{25,9},{2,18},{10... | collective-permute-start | bytes 1572872 | tf_op jit(solution)/shard_map/ppermute | solution.py:27
  624.2 20.8 %collective-permute-start.78 = (bf16[4,129,128]{2,1,0:T(8,128)(2,1)S(1)}, bf16[4,129,128]{2,1,0:T(8,128)(2,1)S(1)}, u32[]{:S(2)}, u32[]{:S(2)}) collective-permute-start(bf16[4,129,128]{2,1,0:T(8,128)(2,1)S(1)} %pad_maximum_fusion.2), channel_id=1, source_target_pairs={{4,0},{5,1},{6,2},{7,3},{12,8},{13,9},{14,10},{15,11},{20,16},{21,... | collective-permute-start | bytes 396296 | tf_op jit(solution)/shard_map/ppermute | solution.py:650
  655.1 23.8 %collective-permute-start.84 = (bf16[256,2048]{1,0:T(8,128)(2,1)S(1)}, bf16[256,2048]{1,0:T(8,128)(2,1)}, u32[]{:S(2)}, u32[]{:S(2)}) collective-permute-start(bf16[256,2048]{1,0:T(8,128)(2,1)S(1)} %copy-done.11), channel_id=1, source_target_pairs={{0,8},{8,0},{16,24},{24,16},{1,9},{9,1},{17,25},{25,17},{2,10},{10... | collective-permute-start | bytes 3145736 | tf_op jit(solution)/shard_map/ppermute | solution.py:31
  655.1 25.7 %collective-permute-start.85 = (bf16[256,2048]{1,0:T(8,128)(2,1)}, bf16[256,2048]{1,0:T(8,128)(2,1)}, u32[]{:S(2)}, u32[]{:S(2)}) collective-permute-start(bf16[256,2048]{1,0:T(8,128)(2,1)} %collective-permute-done.52.refs_1_), channel_id=1, source_target_pairs={{0,8},{8,0},{16,24},{24,16},{1,9},{9,1},{17,25},{25,17},{2,10},{10... | collective-permute-start | bytes 3145736 | tf_op jit(solution)/shard_map/ppermute | solution.py:31
  655.7 25.4 %collective-permute-start.86 = (bf16[256,2048]{1,0:T(8,128)(2,1)}, bf16[256,2048]{1,0:T(8,128)(2,1)}, u32[]{:S(2)}, u32[]{:S(2)}) collective-permute-start(bf16[256,2048]{1,0:T(8,128)(2,1)} %collective-permute-done.53.refs_2_), channel_id=1, source_target_pairs={{0,8},{8,0},{16,24},{24,16},{1,9},{9,1},{17,25},{25,17},{2,10},{10... | collective-permute-start | bytes 3145736 | tf_op jit(solution)/shard_map/ppermute | solution.py:31
  655.8 25.3 %collective-permute-start.87 = (bf16[256,2048]{1,0:T(8,128)(2,1)}, bf16[256,2048]{1,0:T(8,128)(2,1)}, u32[]{:S(2)}, u32[]{:S(2)}) collective-permute-start(bf16[256,2048]{1,0:T(8,128)(2,1)} %collective-permute-done.54.refs_3_), channel_id=1, source_target_pairs={{0,8},{8,0},{16,24},{24,16},{1,9},{9,1},{17,25},{25,17},{2,10},{10... | collective-permute-start | bytes 3145736 | tf_op jit(solution)/shard_map/ppermute | solution.py:31
  657.3 46.1 %collective-permute-start.81 = (bf16[4,3,512,128]{3,2,1,0:T(8,128)(2,1)}, bf16[4,3,512,128]{3,2,1,0:T(8,128)(2,1)}, u32[]{:S(2)}, u32[]{:S(2)}) collective-permute-start(bf16[4,3,512,128]{3,2,1,0:T(8,128)(2,1)} %bitcast.211), channel_id=1, source_target_pairs={{0,2},{1,3},{2,0},{3,1},{4,6},{5,7},{6,4},{7,5},{8,10},{9,11},{10,... | collective-permute-start | bytes 4718600 | tf_op jit(solution)/shard_map/ppermute | solution.py:36
  679.0 25.6 %collective-permute-start.82 = (bf16[256,2048]{1,0:T(8,128)(2,1)}, bf16[256,2048]{1,0:T(8,128)(2,1)}, u32[]{:S(2)}, u32[]{:S(2)}) collective-permute-start(bf16[256,2048]{1,0:T(8,128)(2,1)} %get-tuple-element.322), channel_id=1, source_target_pairs={{0,1},{1,0},{2,3},{3,2},{4,5},{5,4},{6,7},{7,6},{8,9},{9,8},{10,11... | collective-permute-start | bytes 3145736 | tf_op jit(solution)/shard_map/ppermute | solution.py:23
  680.9 25.2 %collective-permute-start.83 = (bf16[256,2048]{1,0:T(8,128)(2,1)}, bf16[256,2048]{1,0:T(8,128)(2,1)}, u32[]{:S(2)}, u32[]{:S(2)}) collective-permute-start(bf16[256,2048]{1,0:T(8,128)(2,1)} %get-tuple-element.257.refs_0_), channel_id=1, source_target_pairs={{0,16},{8,24},{16,0},{24,8},{1,17},{9,25},{17,1},{25,9},{2,18},{10... | collective-permute-start | bytes 3145736 | tf_op jit(solution)/shard_map/ppermute | solution.py:27
  723.8 139.9 %reduce-scatter.17.cloned.1.call-start = ((), (), s32[]{:S(2)}) async-start(), calls=%async_computation.15 | async-start | bytes 1310720 | tf_op jit(solution)/shard_map/reduce_scatter | solution.py:153
  723.8 37.0 %collective-permute-start.88 = (bf16[256,2048]{1,0:T(8,128)(2,1)}, bf16[256,2048]{1,0:T(8,128)(2,1)S(1)}, u32[]{:S(2)}, u32[]{:S(2)}) collective-permute-start(bf16[256,2048]{1,0:T(8,128)(2,1)} %collective-permute-done.82.refs_1_), channel_id=1, source_target_pairs={{0,16},{8,24},{16,0},{24,8},{1,17},{9,25},{17,1},{25,9},{2,18},{10... | collective-permute-start | bytes 3145736 | tf_op jit(solution)/shard_map/ppermute | solution.py:27
  779.6 27.3 %collective-permute-start.95 = (bf16[256,2048]{1,0:T(8,128)(2,1)}, bf16[256,2048]{1,0:T(8,128)(2,1)}, u32[]{:S(2)}, u32[]{:S(2)}) collective-permute-start(bf16[256,2048]{1,0:T(8,128)(2,1)} %get-tuple-element.292), channel_id=1, source_target_pairs={{0,17},{1,16},{2,19},{3,18},{4,21},{5,20},{6,23},{7,22},{8,25},{9,... | collective-permute-start | bytes 3145736 | tf_op jit(solution)/shard_map/ppermute | solution.py:53
  781.0 47.6 %collective-permute-start.93 = (bf16[256,2048]{1,0:T(8,128)(2,1)}, bf16[256,2048]{1,0:T(8,128)(2,1)}, u32[]{:S(2)}, u32[]{:S(2)}) collective-permute-start(bf16[256,2048]{1,0:T(8,128)(2,1)} %get-tuple-element.293), channel_id=1, source_target_pairs={{0,16},{1,17},{2,18},{3,19},{4,20},{5,21},{6,22},{7,23},{8,24},{9,... | collective-permute-start | bytes 3145736 | tf_op jit(solution)/shard_map/ppermute | solution.py:53
  782.4 46.2 %collective-permute-start.91 = (bf16[256,2048]{1,0:T(8,128)(2,1)}, bf16[256,2048]{1,0:T(8,128)(2,1)}, u32[]{:S(2)}, u32[]{:S(2)}) collective-permute-start(bf16[256,2048]{1,0:T(8,128)(2,1)} %get-tuple-element.294), channel_id=1, source_target_pairs={{0,1},{1,0},{2,3},{3,2},{4,5},{5,4},{6,7},{7,6},{8,9},{9,8},{10,11... | collective-permute-start | bytes 3145736 | tf_op jit(solution)/shard_map/ppermute | solution.py:53
  790.5 42.1 %collective-permute-start.104 = (bf16[2,129,128]{2,1,0:T(8,128)(2,1)}, bf16[2,129,128]{2,1,0:T(8,128)(2,1)S(1)}, u32[]{:S(2)}, u32[]{:S(2)}) collective-permute-start(bf16[2,129,128]{2,1,0:T(8,128)(2,1)} %bitcast.216), channel_id=1, source_target_pairs={{0,8},{8,0},{16,24},{24,16},{1,9},{9,1},{17,25},{25,17},{2,10},{10... | collective-permute-start | bytes 198152 | tf_op jit(solution)/shard_map/ppermute | solution.py:721
  790.5 42.1 %collective-permute-start.105 = (bf16[2,129,128]{2,1,0:T(8,128)(2,1)S(1)}, bf16[2,129,128]{2,1,0:T(8,128)(2,1)S(1)}, u32[]{:S(2)}, u32[]{:S(2)}) collective-permute-start(bf16[2,129,128]{2,1,0:T(8,128)(2,1)S(1)} %bitcast.269), channel_id=1, source_target_pairs={{0,16},{8,24},{16,0},{24,8},{1,17},{9,25},{17,1},{25,9},{2,18},{10... | collective-permute-start | bytes 198152 | tf_op jit(solution)/shard_map/ppermute | solution.py:721
  806.8 25.8 %collective-permute-start.106 = (bf16[2,129,128]{2,1,0:T(8,128)(2,1)S(1)}, bf16[2,129,128]{2,1,0:T(8,128)(2,1)S(1)}, u32[]{:S(2)}, u32[]{:S(2)}) collective-permute-start(bf16[2,129,128]{2,1,0:T(8,128)(2,1)S(1)} %bitcast.268), channel_id=1, source_target_pairs={{0,24},{8,16},{16,8},{24,0},{1,25},{9,17},{17,9},{25,1},{2,26},{10... | collective-permute-start | bytes 198152 | tf_op jit(solution)/shard_map/ppermute | solution.py:721
  836.4 27.3 %collective-permute-start.110 = (bf16[256,768]{1,0:T(8,128)(2,1)S(1)}, bf16[256,768]{1,0:T(8,128)(2,1)S(1)}, u32[]{:S(2)}, u32[]{:S(2)}) collective-permute-start(bf16[256,768]{1,0:T(8,128)(2,1)S(1)} %get-tuple-element.358), channel_id=1, source_target_pairs={{0,1},{1,0},{2,3},{3,2},{4,5},{5,4},{6,7},{7,6},{8,9},{9,8},{10,11... | collective-permute-start | bytes 1179656 | tf_op jit(solution)/shard_map/ppermute | solution.py:23
  842.3 30.9 %collective-permute-start.111 = (bf16[256,768]{1,0:T(8,128)(2,1)S(1)}, bf16[256,768]{1,0:T(8,128)(2,1)S(1)}, u32[]{:S(2)}, u32[]{:S(2)}) collective-permute-start(bf16[256,768]{1,0:T(8,128)(2,1)S(1)} %get-tuple-element.359.refs_0_), channel_id=1, source_target_pairs={{0,16},{8,24},{16,0},{24,8},{1,17},{9,25},{17,1},{25,9},{2,18},{10... | collective-permute-start | bytes 1179656 | tf_op jit(solution)/shard_map/ppermute | solution.py:27
  848.1 18.3 %collective-permute-start.127 = (f32[4112]{0:T(1024)S(1)}, f32[4112]{0:T(1024)S(1)}, u32[]{:S(2)}, u32[]{:S(2)}) collective-permute-start(f32[4112]{0:T(1024)S(1)} %add.559), channel_id=1, source_target_pairs={{0,2},{1,3},{2,0},{3,1},{4,6},{5,7},{6,4},{7,5},{8,10},{9,11},{10,... | collective-permute-start | bytes 49352 | tf_op jit(solution)/shard_map/ppermute | solution.py:36
  850.8 16.8 %collective-permute-start.108 = (bf16[4,1,129,128]{3,2,0,1:T(8,128)(2,1)S(1)}, bf16[4,1,129,128]{3,2,0,1:T(8,128)(2,1)S(1)}, u32[]{:S(2)}, u32[]{:S(2)}) collective-permute-start(bf16[4,1,129,128]{3,2,0,1:T(8,128)(2,1)S(1)} %add_convert_fusion.9), channel_id=1, source_target_pairs={{0,2},{1,3},{2,0},{3,1},{4,6},{5,7},{6,4},{7,5},{8,10},{9,11},{10,... | collective-permute-start | bytes 396296 | tf_op jit(solution)/shard_map/ppermute | solution.py:36
  (154 other events, 1858.0 us)
Sparse Core Ops, SparseCore 0:
  25.0 82.2 all-gather.4
  155.4 92.5 all-gather.6
  250.1 81.2 all-gather.8
  333.4 89.4 all-gather.10
  425.1 75.2 reduce-scatter.6
  507.6 75.0 reduce-scatter.10
  585.5 90.3 reduce-scatter.8
  679.7 87.9 reduce-scatter.12
  770.0 60.2 reduce-scatter.14
  832.4 31.2 reduce-scatter.16
